TPU v7x, 32 devices: a whole 2x2x4 slice. The times are simulated.
32 devices in a mesh: dp: 16 (over z, y, x), mp: 2 (over core).
Axes of the slice: x: 2, y: 2, z: 4, core: 2. Of those that a mesh axis runs over, the one named last changes fastest.
Arguments:
- dec_input: bfloat16 [32, 128, 768], P('dp'), may hold values from -6 to 6
- enc_output: bfloat16 [32, 512, 768], P('dp'), may hold values from -6 to 6
- dec_lengths: int32 [16, 2], P('dp'), may hold values from 1 to 128, 192 in all within a row
- enc_lengths: int32 [16, 2], P('dp'), may hold values from 1 to 512, 768 in all within a row
- self_query: bfloat16 [768, 768], P(None, 'mp'), may hold values from -0.0546875 to 0.0546875
- self_key: bfloat16 [768, 768], P(None, 'mp'), may hold values from -0.21875 to 0.21875
- self_value: bfloat16 [768, 768], P(None, 'mp'), may hold values from -0.21875 to 0.21875
- self_output: bfloat16 [768, 768], P('mp'), may hold values from -0.625 to 0.625
- self_gain: float32 [768], replicated, may hold values from 0.1 to 1.9
- rel_bias: float32 [32, 12], P(None, 'mp'), may hold values from -4 to 4
- cross_query: bfloat16 [768, 768], P(None, 'mp'), may hold values from -0.0546875 to 0.0546875
- cross_key: bfloat16 [768, 768], P(None, 'mp'), may hold values from -0.21875 to 0.21875
- cross_value: bfloat16 [768, 768], P(None, 'mp'), may hold values from -0.21875 to 0.21875
- cross_output: bfloat16 [768, 768], P('mp'), may hold values from -0.625 to 0.625
- cross_gain: float32 [768], replicated, may hold values from 0.1 to 1.9
- ffn_in: bfloat16 [768, 3072], P(None, 'mp'), may hold values from -0.21875 to 0.21875
- ffn_out: bfloat16 [3072, 768], P('mp'), may hold values from -0.15625 to 0.15625
- ffn_gain: float32 [768], replicated, may hold values from 0.1 to 1.9
- cotangent: bfloat16 [32, 128, 768], P('dp'), may hold values from -6 to 6
Outputs:
- layer_output: bfloat16 [32, 128, 768], P('dp')
- dec_grad: bfloat16 [32, 128, 768], P('dp')
- enc_grad: bfloat16 [32, 512, 768], P('dp')
- self_query_grad: float32 [768, 768], P('dp', 'mp')
- self_key_grad: float32 [768, 768], P('dp', 'mp')
- self_value_grad: float32 [768, 768], P('dp', 'mp')
- self_output_grad: float32 [768, 768], P('mp', 'dp')
- self_gain_grad: float32 [768], replicated
- rel_bias_grad: float32 [32, 12], P(None, 'mp')
- cross_query_grad: float32 [768, 768], P('dp', 'mp')
- cross_key_grad: float32 [768, 768], P('dp', 'mp')
- cross_value_grad: float32 [768, 768], P('dp', 'mp')
- cross_output_grad: float32 [768, 768], P('mp', 'dp')
- cross_gain_grad: float32 [768], replicated
- ffn_in_grad: float32 [768, 3072], P('dp', 'mp')
- ffn_out_grad: float32 [3072, 768], P('mp', 'dp')
- ffn_gain_grad: float32 [768], replicated
Inputs may be any that keep to these rules, and one draw needn't show every extreme that they name: `dec_lengths`: each device's 2 decoder lengths sum to 192. `enc_lengths`: each device's 2 encoder lengths sum to 768.
All inputs are finite; a program needn't handle non-finite values.
Results may differ from a plain program's by a relative error of at most 0.024.
The roundings to bfloat16 on the way count: a program that leaves them out, or rounds other values in their place, can miss the bound.
Values sent between devices are 32-bit elements; how exact they have to be, the bound alone decides.
No kernel may reach another device: no remote copies, remote signals or barrier semaphores. Data moves between devices by JAX's collectives and lax.ppermute only.
A program may use at most 128 MiB of HBM per device.

v0:
```python
import functools

import jax
import jax.numpy as jnp
import numpy as np
from jax import lax
from jax.experimental import pallas as pl
from jax.experimental.pallas import tpu as pltpu
from jax.sharding import PartitionSpec as P

epsilon = 1e-06
masked_value = -1e30
head_width = 64
pair_width = 2 * head_width
bf16 = jnp.bfloat16
f32 = jnp.float32
curve = 0.7978845608028654
cubic = 0.044715


def nn(left, right, precision=None):
    return lax.dot_general(
        left, right, (((1,), (0,)), ((), ())), precision=precision, preferred_element_type=f32
    )


def nt(left, right, precision=None):
    return lax.dot_general(
        left, right, (((1,), (1,)), ((), ())), precision=precision, preferred_element_type=f32
    )


def tn(left, right, precision=None):
    return lax.dot_general(
        left, right, (((0,), (0,)), ((), ())), precision=precision, preferred_element_type=f32
    )


def gain_row(gain):
    return gain[...].reshape(1, gain.shape[0])


def iota(shape, dim):
    return lax.broadcasted_iota(jnp.int32, shape, dim)


def inverse_rms(values):
    return lax.rsqrt(jnp.sum(values * values, -1, keepdims=True) / values.shape[-1] + epsilon)


def norm_back(values, gain, upstream):
    inverse = inverse_rms(values)
    scaled = upstream * gain
    mean = jnp.sum(scaled * values, -1, keepdims=True) / values.shape[-1]
    gain_grad = jnp.sum(upstream * values * inverse, 0, keepdims=True)
    return inverse * scaled - values * (inverse * inverse * inverse * mean), gain_grad


def bucket_bounds(buckets):
    half = buckets // 2
    return [int(b) for b in np.ceil(16.0 * 8.0 ** (np.arange(1, half) / half))]


def bucket_rows(buckets, width):
    distance = iota((buckets, width), 1)
    coarse = jnp.full((buckets, width), buckets // 2, jnp.int32)
    for bound in bucket_bounds(buckets):
        coarse += (distance >= bound).astype(jnp.int32)
    chosen = jnp.where(distance < buckets // 2, distance, coarse)
    return (chosen == iota((buckets, width), 0)).astype(f32)


def half_masks():
    lane = iota((1, pair_width), 1)
    low = (lane < head_width).astype(f32)
    return low.astype(bf16), (1.0 - low).astype(bf16)


def pick_rows(first, tokens, slots):
    row, col = iota((tokens, 2 * slots), 0), iota((tokens, 2 * slots), 1)
    return (col == jnp.where(row < first, row, row + (slots - first))).astype(f32).astype(bf16)


def self_bias(bias_ref, width):
    return nn(
        bias_ref[...], bucket_rows(bias_ref.shape[1], width), precision=lax.Precision.HIGHEST
    )


def self_allowed(first, tokens):
    key, query = iota((tokens, tokens), 0), iota((tokens, tokens), 1)
    return (key <= query) & ((key < first) == (query < first))


def spread_bias(base, head, tokens):
    width = base.shape[1]
    rows = jnp.broadcast_to(base[head : head + 1], (tokens, width))
    return pltpu.roll(rows, 0, 1, stride=1, stride_axis=0)[:, :tokens]


def own_half(values):
    half = values.shape[0] // 2
    return jnp.where(lax.axis_index("mp") == 0, values[:half], values[half:])


def flush(out):
    if isinstance(out, Leaving):
        out.leave()


def self_forward(
    dec_len, dec, gain, w_q, w_k, w_v, cot, bias, w_o, x_out, low_out, qkv_out, att_out, lse_out, part_out, x_half
):
    slots, width = dec.shape[1], dec.shape[2]
    tokens = x_out.shape[0]
    heads = bias.shape[0]
    first = dec_len[:, 0:1]
    picked = pick_rows(first, tokens, slots)
    x = nn(picked, dec[...].reshape(2 * slots, width))
    x_out[...] = x.astype(bf16)
    flush(x_out)
    half = tokens // 2
    x_half[:half, :] = own_half(x)
    x_half[half:, :] = jnp.broadcast_to(first.astype(f32), (8, width))
    flush(x_half)
    normed = (x * inverse_rms(x) * gain_row(gain)).astype(bf16)
    inner = w_q.shape[1]
    for k, w in enumerate((w_q, w_k, w_v)):
        qkv_out[:, k * inner : (k + 1) * inner] = nn(normed, w[...]).astype(bf16)
    flush(qkv_out)
    low_out[...] = nn(picked, cot[...].reshape(2 * slots, width)).astype(bf16)
    flush(low_out)
    base = self_bias(bias, 2 * slots)
    allowed = self_allowed(first, tokens)
    masks = half_masks()
    top = iota((pair_width, tokens), 0) < head_width
    lse_out[...] = jnp.zeros_like(lse_out)
    for pair in range(heads // 2):
        lanes = slice(pair * pair_width, (pair + 1) * pair_width)
        q = qkv_out[:, lanes]
        k = qkv_out[:, inner + pair * pair_width : inner + (pair + 1) * pair_width]
        v = qkv_out[:, 2 * inner + pair * pair_width : 2 * inner + (pair + 1) * pair_width]
        v_t = v.astype(f32).T.astype(bf16)
        mixed = []
        for side in range(2):
            head = 2 * pair + side
            scores = nt(k, q * masks[side]) + spread_bias(base, head, tokens)
            scores = jnp.where(allowed, scores, masked_value)
            top_score = jnp.max(scores, 0, keepdims=True)
            weights = jnp.exp(scores - top_score)
            total = jnp.sum(weights, 0, keepdims=True)
            lse_out[head : head + 1, :] = top_score + jnp.log(total)
            mixed.append(nn(v_t, (weights * (1.0 / total)).astype(bf16)))
        att_out[:, lanes] = jnp.where(top, mixed[0], mixed[1]).T.astype(bf16)
    flush(att_out)
    flush(lse_out)
    part_out[...] = nn(att_out[...], w_o[...])


def encoder_forward(enc, w_k, w_v, k_out, vt_out, k_far, v_far, kt_far):
    steps = enc.shape[1]
    for w, out, out_t in ((w_v, v_far, vt_out), (w_k, k_out, kt_far)):
        for e in range(enc.shape[0]):
            rows = slice(e * steps, (e + 1) * steps)
            made = nn(enc[e], w[...])
            out[rows, :] = made.astype(bf16)
            out_t[:, rows] = made.T.astype(bf16)
        if out is v_far:
            flush(v_far)
    k_far[...] = k_out[...]


def cross_rows(first, tokens, slots, e):
    row = iota((slots, 1), 0) + e * (tokens - slots)
    return row < first if e == 0 else row >= first


def cross_forward(
    dec_len, enc_len, x, part, moved, gain, w_q, w_o, k_in, vt_in, after_out, q_out, att_out, lse_out, part_out
):
    tokens = x.shape[0]
    slots = 2 * tokens // 3
    steps = k_in.shape[0] // 2
    first = dec_len[:, 0:1]
    after = x[...].astype(f32) + (part[...] + moved[...])
    after_out[...] = after
    normed = (after * inverse_rms(after) * gain_row(gain)).astype(bf16)
    q_out[...] = nn(normed, w_q[...]).astype(bf16)
    flush(q_out)
    masks = half_masks()
    top = iota((pair_width, slots), 0) < head_width
    own = iota((tokens, 1), 0) < first
    lse_out[...] = jnp.zeros_like(lse_out)
    shift = tokens - slots
    for pair in range(q_out.shape[1] // pair_width):
        lanes = slice(pair * pair_width, (pair + 1) * pair_width)
        parts = []
        for e in range(2):
            q = q_out[e * shift : e * shift + slots, lanes]
            both = jnp.concatenate([q * masks[0], q * masks[1]], 0)
            scores = nt(k_in[e * steps : (e + 1) * steps, lanes], both)
            valid = iota((steps, 1), 0) < enc_len[:, e : e + 1]
            scores = jnp.where(valid, scores, masked_value)
            top_score = jnp.max(scores, 0, keepdims=True)
            weights = jnp.exp(scores - top_score)
            total = jnp.sum(weights, 0, keepdims=True)
            lse_out[2 * pair + e : 2 * pair + e + 1, :] = top_score + jnp.log(total)
            mixed = nn(
                vt_in[lanes, e * steps : (e + 1) * steps], (weights * (1.0 / total)).astype(bf16)
            )
            parts.append(jnp.where(top, mixed[:, :slots], mixed[:, slots:]).T)
        fill = jnp.zeros((shift, pair_width), f32)
        att_out[:, lanes] = jnp.where(
            own, jnp.concatenate([parts[0], fill], 0), jnp.concatenate([fill, parts[1]], 0)
        ).astype(bf16)
    flush(lse_out)
    part_out[...] = nn(att_out[...], w_o[...])


def ffn_both(
    after, part, moved, gain, low, w_in, w_out, *outs
):
    if len(outs) > 6:
        x_half, x_moved, *outs, x_rest = outs
        stack(x_rest, x_half, x_moved)
    after_out, normed_out, halves_out, act_out, hid_out, back_out = outs
    total = after[...] + (part[...] + moved[...])
    after_out[...] = total
    normed = (total * inverse_rms(total) * gain_row(gain)).astype(bf16)
    normed_out[...] = normed
    flush(normed_out)
    low_in = low[...]
    half = low_in.shape[0] // 2
    halves_out[:half, :] = own_half(low_in.astype(f32))
    halves_out[half:, :] = own_half(normed.astype(f32))
    hidden = w_in.shape[1]
    chunk = 512 if hidden % 512 == 0 else hidden
    for start in range(0, hidden, chunk):
        cols = slice(start, start + chunk)
        u = nn(normed, w_in[:, cols])
        t = jnp.tanh(curve * (u + cubic * (u * u * u)))
        act = (0.5 * u * (1.0 + t)).astype(bf16)
        slope = 0.5 * (1.0 + t) + 0.5 * u * (1.0 - t * t) * (curve * (1.0 + 3.0 * cubic * (u * u)))
        hid = (nt(low_in, w_out[cols, :]) * slope).astype(bf16)
        act_out[:, cols] = act
        hid_out[:, cols] = hid
        backward = nt(hid, w_in[:, cols])
        if start == 0:
            back_out[...] = backward
        else:
            back_out[...] += backward


def cross_backward(
    dec_len, enc_len, after, part, moved, gain, low, w_o, w_q, q_in, k_in, v_in, kt_in, lse,
    grad_out, low_out, dq_out, dk_out, dv_out, gain_out, part_out
):
    tokens = after.shape[0]
    slots = 2 * tokens // 3
    steps = k_in.shape[0] // 2
    first = dec_len[:, 0:1]
    shift = tokens - slots
    norm_in, gain_grad = norm_back(after[...], gain_row(gain), part[...] + moved[...])
    gain_out[...] = gain_grad
    flush(gain_out)
    grad = low[...].astype(f32) + norm_in
    grad_out[...] = grad
    flush(grad_out)
    low_grad = grad.astype(bf16)
    low_out[...] = low_grad
    flush(low_out)
    g_all = nt(low_grad, w_o[...])
    masks = half_masks()
    top = iota((pair_width, slots), 0) < head_width
    for pair in range(q_in.shape[1] // pair_width):
        lanes = slice(pair * pair_width, (pair + 1) * pair_width)
        parts = []
        for e in range(2):
            keys = slice(e * steps, (e + 1) * steps)
            window = slice(e * shift, e * shift + slots)
            q = q_in[window, lanes]
            g = jnp.where(cross_rows(first, tokens, slots, e), g_all[window, lanes], 0.0)
            g = g.astype(bf16)
            q_both = jnp.concatenate([q * masks[0], q * masks[1]], 0)
            g_both = jnp.concatenate([g * masks[0], g * masks[1]], 0)
            valid = iota((steps, 1), 0) < enc_len[:, e : e + 1]
            scores = jnp.where(valid, nt(k_in[keys, lanes], q_both), masked_value)
            p = jnp.exp(scores - lse[2 * pair + e : 2 * pair + e + 1, :])
            dp = nt(v_in[keys, lanes], g_both)
            ds = (p * (dp - jnp.sum(p * dp, 0, keepdims=True))).astype(bf16)
            dk_out[keys, lanes] = nn(ds, q_both).astype(bf16)
            dv_out[keys, lanes] = nn(p.astype(bf16), g_both).astype(bf16)
            dq = nn(kt_in[lanes, keys], ds)
            parts.append(jnp.where(top, dq[:, :slots], dq[:, slots:]).T)
        fill = jnp.zeros((shift, pair_width), f32)
        dq_out[:, lanes] = (
            jnp.concatenate([parts[0], fill], 0) + jnp.concatenate([fill, parts[1]], 0)
        ).astype(bf16)
    part_out[...] = nt(dq_out[...], w_q[...])


def self_grad(after, part, moved, gain, grad_in, grad_out, low_out, half_out, gain_out):
    norm_in, gain_grad = norm_back(after[...], gain_row(gain), part[...] + moved[...])
    gain_out[...] = gain_grad
    grad = grad_in[...] + norm_in
    grad_out[...] = grad
    low = grad.astype(bf16)
    low_out[...] = low
    half_out[...] = own_half(low.astype(f32))


def back_all(
    dec_len, low, bias, w_o, w_q, w_k, w_v, qkv, lse, dk, dv, w_ck, w_cv, act, w_ffn, dqkv_out, bias_out, part_out
):
    tokens = low.shape[0]
    self_backward(
        dec_len, low, bias, w_o, w_q, w_k, w_v, qkv, lse, dqkv_out, bias_out, part_out.at[pl.ds(0, tokens), :]
    )
    part_out[tokens : 2 * tokens, :] = nn(act[...], w_ffn[...])
    steps = dk.shape[0] // 2
    for e in range(2):
        rows = slice(e * steps, (e + 1) * steps)
        part_out[2 * tokens + e * steps : 2 * tokens + (e + 1) * steps, :] = nt(dk[rows, :], w_ck[...]) + nt(
            dv[rows, :], w_cv[...]
        )


def self_backward(dec_len, low, bias, w_o, w_q, w_k, w_v, qkv, lse, dqkv_out, bias_out, part_out):
    tokens = low.shape[0]
    heads = bias.shape[0]
    first = dec_len[:, 0:1]
    inner = w_q.shape[1]
    g_all = nt(low[...], w_o[...]).astype(bf16)
    reach = 4 * tokens // 3
    base = self_bias(bias, reach)
    allowed = self_allowed(first, tokens)
    masks = half_masks()
    top = iota((pair_width, tokens), 0) < head_width
    diagonals = []
    for pair in range(heads // 2):
        lanes = slice(pair * pair_width, (pair + 1) * pair_width)
        k_lanes = slice(inner + pair * pair_width, inner + (pair + 1) * pair_width)
        v_lanes = slice(2 * inner + pair * pair_width, 2 * inner + (pair + 1) * pair_width)
        q, k, v, g = qkv[:, lanes], qkv[:, k_lanes], qkv[:, v_lanes], g_all[:, lanes]
        k_t = k.astype(f32).T.astype(bf16)
        dk, dv, dq = 0.0, 0.0, []
        for side in range(2):
            head = 2 * pair + side
            q_half, g_half = q * masks[side], g * masks[side]
            scores = nt(k, q_half) + spread_bias(base, head, tokens)
            scores = jnp.where(allowed, scores, masked_value)
            p = jnp.exp(scores - lse[head : head + 1, :])
            dp = nt(v, g_half)
            ds = p * (dp - jnp.sum(p * dp, 0, keepdims=True))
            ds_low = ds.astype(bf16)
            dk += nn(ds_low, q_half)
            dv += nn(p.astype(bf16), g_half)
            dq.append(nn(k_t, ds_low))
            wide = jnp.concatenate([ds, jnp.zeros((tokens, reach - tokens), f32)], 1)
            total = wide[:8]
            for start in range(8, tokens, 8):
                total += pltpu.roll(wide[start : start + 8], reach - start, 1)
            diagonals.append(total)
        dqkv_out[:, lanes] = jnp.where(top, dq[0], dq[1]).T.astype(bf16)
        dqkv_out[:, k_lanes] = dk.astype(bf16)
        dqkv_out[:, v_lanes] = dv.astype(bf16)
    flush(dqkv_out)
    part_out[...] = (
        nt(dqkv_out[:, :inner], w_q[...])
        + nt(dqkv_out[:, inner : 2 * inner], w_k[...])
        + nt(dqkv_out[:, 2 * inner :], w_v[...])
    )
    total = jnp.concatenate(diagonals, 0)
    row = iota(total.shape, 0) & 7
    lined = jnp.zeros_like(total)
    for s in range(8):
        lined += jnp.where(row == s, pltpu.roll(total, (reach - s) % reach, 1), 0.0)
    head_of = ((iota((8, 8 * heads), 1) >> 3) == iota((8, 8 * heads), 0)).astype(f32)
    by_head = nn(head_of, lined, precision=lax.Precision.HIGHEST)
    bias_out[...] = nt(by_head, bucket_rows(bias.shape[1], reach), precision=lax.Precision.HIGHEST)


def unpacked(values, first, slots):
    tokens = values.shape[0]
    slot, row = iota((2 * slots, tokens), 0), iota((2 * slots, tokens), 1)
    limit = jnp.where(slot < slots, first, slots + tokens - first)
    wanted = jnp.where(slot < slots, slot, slot - slots + first)
    spread = ((row == wanted) & (slot < limit)).astype(f32).astype(bf16)
    return nn(spread, values.astype(bf16)).astype(bf16)


def finish_self_norm(
    heads, x, part, moved, gain, grad_in, gain_ffn, gain_cross, bias_grad, dec_out, small_out
):
    tokens, width = x.shape
    norm_in, gain_grad = norm_back(x[...].astype(f32), gain_row(gain), part[:tokens, :] + moved[:tokens, :])
    half, buckets = small_out.shape[1], bias_grad.shape[1]
    small_out[...] = jnp.zeros_like(small_out)
    for k, value in enumerate((gain_grad, gain_cross[...], gain_ffn[...])):
        small_out[2 * k : 2 * k + 1, :] = value[:, :half]
        small_out[2 * k + 1 : 2 * k + 2, :] = value[:, half:]
    small_out[6:7, : heads * buckets] = jnp.concatenate([bias_grad[h : h + 1, :] for h in range(heads)], 1)
    dec_out[...] = (grad_in[...] + norm_in).astype(bf16)


def finish_outputs(dec_len, dec, part, moved, after, dec_out, layer_out, enc_out, token):
    token[...] = jnp.zeros_like(token)
    tokens = dec.shape[0]
    first, slots = dec_len[:, 0:1], dec_out.shape[1]
    dec_out[...] = unpacked(dec[...], first, slots).reshape(dec_out.shape)
    total = after[...] + (part[tokens : 2 * tokens, :] + moved[tokens : 2 * tokens, :])
    layer_out[...] = unpacked(total, first, slots).reshape(layer_out.shape)
    enc_out[...] = (part[2 * tokens :, :] + moved[2 * tokens :, :]).astype(bf16).reshape(enc_out.shape)


def pause(out):
    out[...] = jnp.zeros_like(out)


def collect(low_half, low_a, halves, group_a, low_out, group_out):
    stack(low_out, low_half, low_a)
    stack(group_out, halves, group_a)


def gather_self(x_moved, x_rest, low_a, low_rest, out):
    stack(out, x_moved, x_rest, low_a, low_rest)


def relay(value, out):
    out[...] = value[...]


def gather_ffn(group_a, group_rest, out):
    stack(out, group_a, group_rest)


def place_of():
    return lax.axis_index("dp"), lax.axis_index("mp")


def own_bit(stage):
    place, core = place_of()
    shift = (core, 1 - core, 2 + core, 3 - core)[stage]
    return lax.shift_right_logical(place, shift) & 1


def entry(stage, step, bit):
    if stage % 2:
        return 2 * step + bit
    core = lax.axis_index("mp")
    return jnp.where(core == 0, 2 * step + bit, (step // 2) * 4 + 2 * bit + step % 2)


def pick_chunks(chunks, rows, width):
    gap = iota((rows, width), 1) - iota((rows, width), 0)
    return jnp.concatenate([(gap == chunk * rows).astype(f32) for chunk in chunks], 0).astype(bf16)


def half_pick(other, width):
    bit = own_bit(0)
    bit = 1 - bit if other else bit
    return pick_chunks([entry(0, step, bit) for step in range(8)], width // 16, width)


def fold_lanes(values):
    half = values.shape[0] // 2
    return jnp.concatenate([values[:half], values[half:]], 1)


def unfold_lanes(values):
    half = values.shape[1] // 2
    return jnp.concatenate([values[:, :half], values[:, half:]], 0)


def split_entries(stage, source, send_out, keep_out, rows):
    bit = own_bit(stage)
    for step in range(keep_out.shape[0] // rows):
        here = slice(step * rows, (step + 1) * rows)
        send_out[here, :] = source(entry(stage, step, 1 - bit))
        keep_out[here, :] = source(entry(stage, step, bit))


def pack_early(after, gain, att, early_out, own):
    width = after.shape[1]
    inner = att.shape[1]
    v = after[...]
    normed = (v * inverse_rms(v) * gain_row(gain)).astype(bf16)
    own[...] = nt(half_pick(0, width), normed).astype(bf16)
    early_out[:, :inner] = fold_lanes(nt(half_pick(1, width), normed))
    early_out[:, inner:] = att[...].astype(f32)


def stack(out, *parts):
    at = 0
    for part in parts:
        out[at : at + part.shape[0], :] = part[...]
        at += part.shape[0]


def cross_weights(enc, dk, dv, dq, low, late_out):
    steps, width = enc.shape[1:]
    inner = dk.shape[1]
    half = width // 2
    left = nt(half_pick(1, width), enc[...].reshape(2 * steps, width)).astype(bf16)
    late_out[:half, :inner] = nn(left, dk[...])
    late_out[:half, inner:] = nn(left, dv[...])
    late_out[half:, :inner] = dq[...].astype(f32)
    late_out[half:, inner:] = fold_lanes(nt(half_pick(1, width), low[...]))


def cross_keep(enc, dk, dv, keep_out):
    steps, width = enc.shape[1:]
    inner = dk.shape[1]
    left = nt(half_pick(0, width), enc[...].reshape(2 * steps, width)).astype(bf16)
    keep_out[:, :inner] = nn(left, dk[...])
    keep_out[:, inner:] = nn(left, dv[...])


def side_by_side(out, at, small):
    n = small.shape[1]
    out[at:, :n] = small[:8, :]
    out[at:, n : 2 * n] = small[8:, :]
    out[at:, 2 * n :] = jnp.zeros_like(out[at:, 2 * n :])


def above(rows, n):
    return jnp.concatenate([rows[:, :n], rows[:, n : 2 * n]], 0)


def cross_fold(keep, moved, early, own, dq, low, att, small, small_moved, send_out, keep_out, small_out, total):
    width = low.shape[1]
    half, inner = own.shape[0], dq.shape[1]
    rows = width // 16
    total[:, :inner] = nn(own[...], dq[...]) + nn(
        unfold_lanes(early[:, :inner]).astype(bf16), moved[half:, :inner].astype(bf16)
    )
    total[:, 3 * inner :] = nn(nt(half_pick(0, width), low[...]).astype(bf16), att[...]) + nn(
        unfold_lanes(moved[half:, inner:]).astype(bf16), early[:, inner:].astype(bf16)
    )
    total[:, inner : 3 * inner] = keep[...] + moved[:half, :]
    split_entries(1, lambda i: total[pl.ds(pl.multiple_of(i * rows, 8), rows), :], send_out, keep_out, rows)
    stack(small_out, small, small_moved)
    side_by_side(send_out, keep_out.shape[0], small_out)


def self_group(
    x, dqkv, low, att, here, there, gain, bias, w_q, w_k, w_v, w_o,
    send_out, keep_out, made, grads, total
):
    tokens, width = x.shape
    inner = att.shape[1]
    heads = bias.shape[0]
    half = tokens // 2
    place, core = place_of()
    rows = width // 16
    base = self_bias(bias, 4 * tokens // 3)
    masks = half_masks()
    top = iota((pair_width, tokens), 0) < head_width
    biases = [spread_bias(base, head, tokens) for head in range(heads)]
    tall = half + 8
    x_at, low_at = (0, tall, 2 * tall), (3 * tall, 3 * tall + half, 3 * tall + 2 * half)
    orders = ((0, 1), (1, 0), (2, 2))

    def joined(starts, mine, other):
        a, b = here[starts[mine] : starts[mine] + half, :], there[starts[other] : starts[other] + half, :]
        return [jnp.where(core == 0, a, b), jnp.where(core == 0, b, a)]

    v = jnp.concatenate([part for order in orders for part in joined(x_at, *order)], 0)
    normed = (v * inverse_rms(v) * gain_row(gain)).astype(bf16)
    low_all = jnp.concatenate([part for order in orders for part in joined(low_at, *order)], 0).astype(bf16)
    for k, w in enumerate((w_q, w_k, w_v)):
        made[:, k * inner : (k + 1) * inner] = nn(normed, w[...]).astype(bf16)
    made[:, 3 * inner :] = nt(low_all, w_o[...]).astype(bf16)
    grads[:tokens, : 3 * inner] = dqkv[...]
    grads[:tokens, 3 * inner :] = att[...]
    def one_chip(k, carry):
        first = here[pl.ds(pl.multiple_of(k * tall + half, 8), 8), :][0:1, 0:1].astype(jnp.int32)
        allowed = self_allowed(first, tokens)
        source = pl.ds(pl.multiple_of(k * tokens, 16), tokens)
        target = pl.ds(pl.multiple_of((k + 1) * tokens, 16), tokens)
        every = range(heads)
        lanes = [slice(pair * pair_width, (pair + 1) * pair_width) for pair in range(heads // 2)]
        q, key, value, g = (
            [made[source, n * inner + lane.start : n * inner + lane.stop] for lane in lanes] for n in range(4)
        )
        k_t = [part.astype(f32).T.astype(bf16) for part in key]
        v_t = [part.astype(f32).T.astype(bf16) for part in value]
        q_half = [q[h // 2] * masks[h % 2] for h in every]
        g_half = [g[h // 2] * masks[h % 2] for h in every]
        scores = [jnp.where(allowed, nt(key[h // 2], q_half[h]) + biases[h], masked_value) for h in every]
        weights = [jnp.exp(score - jnp.max(score, 0, keepdims=True)) for score in scores]
        p = [weight * (1.0 / jnp.sum(weight, 0, keepdims=True)) for weight in weights]
        dp = [nt(value[h // 2], g_half[h]) for h in every]
        ds = [(p[h] * (dp[h] - jnp.sum(p[h] * dp[h], 0, keepdims=True))).astype(bf16) for h in every]
        p = [part.astype(bf16) for part in p]
        dk = [nn(ds[h], q_half[h]) for h in every]
        dv = [nn(p[h], g_half[h]) for h in every]
        dq = [nn(k_t[h // 2], ds[h]) for h in every]
        mixed = [nn(v_t[h // 2], p[h]) for h in every]
        for pair, lane in enumerate(lanes):
            a, b = 2 * pair, 2 * pair + 1
            for n, part in enumerate(
                (jnp.where(top, dq[a], dq[b]).T, dk[a] + dk[b], dv[a] + dv[b], jnp.where(top, mixed[a], mixed[b]).T)
            ):
                grads[target, n * inner + lane.start : n * inner + lane.stop] = part.astype(bf16)
        return carry

    lax.fori_loop(0, 3, one_chip, 0)
    picked = pick_chunks([4 * z + (place & 3) for z in range(4)], rows, width)
    v = x[...].astype(f32)
    own = (v * inverse_rms(v) * gain_row(gain)).astype(bf16)
    left = jnp.concatenate([nt(picked, own), nt(picked, normed)], 1).astype(bf16)
    total[:, : 3 * inner] = nn(left, grads[:, : 3 * inner])
    left = jnp.concatenate([nt(picked, low[...]), nt(picked, low_all)], 1).astype(bf16)
    total[:, 3 * inner :] = nn(left, grads[:, 3 * inner :])
    split_entries(2, lambda i: total[pl.ds(pl.multiple_of(i * rows, 8), rows), :], send_out, keep_out, rows)


def chunk_of(ref, index, rows):
    return ref[pl.ds(pl.multiple_of(index * rows, 8), rows), :]


def entry_here(step):
    core, bit = lax.axis_index("mp"), own_bit(2)
    return jnp.where(core == 0, 2 * step + bit, 2 * bit + step)


def fold_z(rows, keep, small, first, out, small_out):
    for step in range(2):
        index = entry(2, step, 1 - own_bit(2))
        out[step * rows : (step + 1) * rows, :] = chunk_of(keep, index, rows) + chunk_of(first, index, rows)
    n = small.shape[1]
    total = four_sum(small[:8, :], small[8:, :], above(first[keep.shape[0] :, : 2 * n], n))
    small_out[...] = total
    out[2 * rows :, :n] = total
    out[2 * rows :, n:] = jnp.zeros_like(out[2 * rows :, n:])


def three_sum(rows, step, keep, first, second):
    index = entry_here(step)
    return chunk_of(keep, index, rows) + chunk_of(first, index, rows) + chunk_of(second, step, rows)


def fold_last(rows, keep, small, first, second, out, small_out):
    out[:rows, :] = three_sum(rows, 1 - own_bit(3), keep, first, second)
    small_out[:8, :] = small[...]
    small_out[8:, :] = second[2 * rows :, : small.shape[1]]
    side_by_side(out, rows, small_out)


def four_sum(mine, first, second):
    core = lax.axis_index("mp")
    near = mine + jnp.where(core == 0, first, second[:8])
    return near + (jnp.where(core == 0, second[:8], first) + second[8:])


def finish_cross(
    heads, rows, keep, first, second, sums, third, q_out, k_out, v_out, o_out, gain_s, gain_c, gain_f, bias_out, token
):
    token[...] = jnp.zeros_like(token)
    inner = q_out.shape[1]
    total = three_sum(rows, own_bit(3), keep, first, second) + third[:rows, :]
    for k, out in enumerate((q_out, k_out, v_out, o_out)):
        out[...] = total[:, k * inner : (k + 1) * inner]
    width, buckets, n = gain_s.shape[0], bias_out.shape[1], sums.shape[1]
    small = four_sum(sums[:8, :], sums[8:, :], above(third[rows:, : 2 * n], n))
    for k, out in enumerate((gain_s, gain_c, gain_f)):
        out[...] = jnp.concatenate([small[2 * k : 2 * k + 1, :], small[2 * k + 1 : 2 * k + 2, :]], 1).reshape(width)
    bias_out[...] = jnp.concatenate([small[6:7, h * buckets : (h + 1) * buckets] for h in range(heads)], 0)


def self_fold(rows, keep, first, out):
    step = 1 - own_bit(3)
    out[...] = chunk_of(keep, step, rows) + chunk_of(first, step, rows)


def finish_self(rows, keep, first, second, q_out, k_out, v_out, o_out, token):
    token[...] = jnp.zeros_like(token)
    inner = q_out.shape[1]
    step = own_bit(3)
    total = chunk_of(keep, step, rows) + chunk_of(first, step, rows) + second[...]
    for k, out in enumerate((q_out, k_out, v_out, o_out)):
        out[...] = total[:, k * inner : (k + 1) * inner]


def ffn_fold(rows, keep, first, out):
    step = 1 - own_bit(1)
    out[...] = chunk_of(keep, step, rows) + chunk_of(first, step, rows)


def finish_ffn(rows, keep, first, second, in_out, out_out):
    step = own_bit(1)
    total = chunk_of(keep, step, rows) + chunk_of(first, step, rows) + second[...]
    hidden = in_out.shape[1]
    in_out[...] = total[:, :hidden]
    out_out[...] = total[:, hidden:]


def ffn_group(normed, low, act, hid, here, there, w_in, w_out, send_out, keep_out, normed_all, low_all, total):
    tokens, width = normed.shape
    hidden = w_in.shape[1]
    half = tokens // 2
    rows = width // 16
    normed_all[:tokens, :] = normed[...]
    low_all[:tokens, :] = low[...]
    at = tokens
    for source in (here, there):
        for k in range(3):
            low_all[at : at + half, :] = source[2 * k * half : (2 * k + 1) * half, :].astype(bf16)
            normed_all[at : at + half, :] = source[(2 * k + 1) * half : (2 * k + 2) * half, :].astype(bf16)
            at += half
    place, core = place_of()
    first = lax.shift_right_logical(place, 2) * 4
    picked = pick_chunks([first + k for k in range(4)], rows, width)
    left_in = nt(picked, normed_all[...]).astype(bf16)
    left_out = nt(picked, low_all[...]).astype(bf16)
    chunk = 512 if hidden % 512 == 0 else hidden

    def one_chunk(k, carry):
        cols = pl.ds(pl.multiple_of(k * chunk, 128), chunk)
        u = nn(normed_all[tokens:, :], w_in[:, cols])
        t = jnp.tanh(curve * (u + cubic * (u * u * u)))
        other_act = (0.5 * u * (1.0 + t)).astype(bf16)
        slope = 0.5 * (1.0 + t) + 0.5 * u * (1.0 - t * t) * (curve * (1.0 + 3.0 * cubic * (u * u)))
        other_hid = (nt(low_all[tokens:, :], w_out[cols, :]) * slope).astype(bf16)
        total[:, cols] = nn(left_in[:, :tokens], hid[:, cols]) + nn(left_in[:, tokens:], other_hid)
        total[:, pl.ds(pl.multiple_of(hidden + k * chunk, 128), chunk)] = nn(
            left_out[:, :tokens], act[:, cols]
        ) + nn(left_out[:, tokens:], other_act)
        return carry

    lax.fori_loop(0, hidden // chunk, one_chunk, 0)
    split_entries(0, lambda i: total[pl.ds(pl.multiple_of(i * rows, 8), rows), :], send_out, keep_out, rows)


class Fetched:
    def __init__(self, ref, copy):
        self.ref, self.copy, self.shape, self.dtype = ref, copy, ref.shape, ref.dtype

    def arrive(self):
        if self.copy is not None:
            self.copy.wait()
            self.copy = None

    def __getitem__(self, place):
        self.arrive()
        return self.ref[place]


class Leaving:
    def __init__(self, ref, copy):
        self.ref, self.copy, self.shape, self.dtype = ref, copy, ref.shape, ref.dtype
        self.left = False

    def leave(self):
        if not self.left:
            self.copy.start()
            self.left = True

    def __getitem__(self, place):
        return self.ref[place]

    def __setitem__(self, place, value):
        self.ref[place] = value


SPACES = {"v": pltpu.VMEM, "h": pltpu.HBM, "a": pl.ANY}


def call(kernel, outs, args, scratch=(), after=(), limit=20, cost=1):
    kinds = [kind for _, kind, *_ in args]
    fetched = [k for k, kind in enumerate(kinds) if kind != "v"]
    written = [k for k, (_, _, kind) in enumerate(outs) if kind != "v"]

    def body(*refs):
        ins, rest = list(refs[: len(args)]), refs[len(args) + len(after) :]
        results, rest = list(rest[: len(outs)]), rest[len(outs) :]
        in_bufs, rest = rest[: len(fetched)], rest[len(fetched) :]
        out_bufs, rest = rest[: len(written)], rest[len(written) :]
        extra, rest = rest[: len(scratch)], rest[len(scratch) :]
        sems = rest[0] if rest else None
        waits = []
        for n, (k, buf) in enumerate(zip(fetched, in_bufs)):
            source = ins[k]
            if len(args[k]) > 2:
                source = source.at[pl.ds(args[k][2], buf.shape[0])]
            copy = pltpu.make_async_copy(source, buf, sems.at[n])
            copy.start()
            ins[k] = Fetched(buf, copy)
            waits.append(ins[k])
        leaving = []
        for n, (k, buf) in enumerate(zip(written, out_bufs)):
            results[k] = Leaving(buf, pltpu.make_async_copy(buf, results[k], sems.at[len(fetched) + n]))
            leaving.append(results[k])
        kernel(*ins, *results, *extra)
        for out in leaving:
            out.leave()
        for wait in waits:
            wait.arrive()
        for out in leaving:
            out.copy.wait()

    places = {kind: pl.BlockSpec(memory_space=space) for kind, space in SPACES.items()}
    shapes = [
        pltpu.VMEM((args[k][3:] or args[k][0].shape[:1]) + args[k][0].shape[1:], args[k][0].dtype) for k in fetched
    ]
    shapes += [pltpu.VMEM(outs[k][0], outs[k][1]) for k in written]
    shapes += [pltpu.VMEM(shape, kind) for shape, kind in scratch]
    if fetched or written:
        shapes.append(pltpu.SemaphoreType.DMA((len(fetched) + len(written),)))
    name = getattr(kernel, "__name__", None) or kernel.func.__name__
    return pl.pallas_call(
        body,
        out_shape=[
            pltpu.HBM(shape, kind) if place == "h" else jax.ShapeDtypeStruct(shape, kind) for shape, kind, place in outs
        ],
        in_specs=[places[kind] for kind in kinds] + [places["a"]] * len(after),
        out_specs=[places[kind] for _, _, kind in outs],
        scratch_shapes=shapes,
        compiler_params=pltpu.CompilerParams(vmem_limit_bytes=limit * 1024 * 1024),
        cost_estimate=pl.CostEstimate(flops=cost * 35 * 10**9, transcendentals=0, bytes_accessed=1000),
        name=name,
    )(
        *[
            pltpu.with_memory_space_constraint(value, pltpu.HBM) if kind == "h" else value
            for value, kind, *_ in args
        ],
        *after,
    )


def pair_swap(values):
    return lax.ppermute(values, "mp", [(0, 1), (1, 0)])


def swap_bit(values, bit, count):
    return lax.ppermute(values, "dp", [(k, k ^ (1 << bit)) for k in range(count)])


def stage_swap(values, stage, count):
    bits = ((0, 1), (1, 0), (2, 3), (3, 2))[stage]
    pairs = [(2 * k + core, 2 * (k ^ (1 << bits[core])) + core) for k in range(count) for core in range(2)]
    return lax.ppermute(values, ("dp", "mp"), pairs)


def half_of(values, dim, which):
    return lax.dynamic_index_in_dim(values, which, dim, keepdims=False)


def scatter_sum(blocks, order, count):
    place = lax.axis_index("dp")
    levels = len(order)
    left = list(reversed(range(levels)))
    blocks = blocks.reshape((2,) * levels + blocks.shape[1:])
    for bit in order:
        dim = left.index(bit)
        mine = (place >> bit) & 1
        moved = swap_bit(half_of(blocks, dim, 1 - mine), bit, count)
        blocks = half_of(blocks, dim, mine) + moved
        left.remove(bit)
    return blocks


def full_sum(values, count):
    for bit in range(count.bit_length() - 1):
        values = values + swap_bit(values, bit, count)
    return values


def on_device(
    dec_input, enc_output, dec_lengths, enc_lengths, self_query, self_key, self_value, self_output, self_gain,
    rel_bias, cross_query, cross_key, cross_value, cross_output, cross_gain, ffn_in, ffn_out, ffn_gain, cotangent
):
    slots, width = dec_input.shape[1:]
    steps = enc_output.shape[1]
    inner = self_query.shape[1]
    hidden = ffn_in.shape[1]
    tokens = 3 * slots // 2
    count = lax.axis_size("dp")
    quick = count == 16
    row, half_row = (tokens, width), (tokens // 2, width)
    part_of = (tokens, inner)
    wide = 4 * inner
    share = width // count

    bias_rows = rel_bias.T
    tall = tokens // 2 + 8
    x, low_ffn, qkv, att_self, lse_self, part_self, x_half = call(
        self_forward,
        [(row, bf16, "h"), (row, bf16, "h"), ((tokens, 3 * inner), bf16, "h"), (part_of, bf16, "v"),
         ((8, tokens), f32, "v"), (row, f32, "v"), ((tall, width), f32, "h")],
        [(dec_lengths, "h"), (dec_input, "h"), (self_gain, "h"), (self_query, "h"), (self_key, "h"), (self_value, "h"),
         (cotangent, "h"), (bias_rows, "h"), (self_output, "h")],
    )
    moved_self = pair_swap(part_self)
    if quick:
        x_moved = stage_swap(x_half, 0, count)
    keys, values_t, keys_far, values, keys_t = call(
        encoder_forward,
        [((2 * steps, inner), bf16, "v"), ((inner, 2 * steps), bf16, "v")] + [((2 * steps, inner), bf16, "h")] * 2
        + [((inner, 2 * steps), bf16, "h")],
        [(enc_output, "v"), (cross_key, "v"), (cross_value, "v")],
        after=(part_self,),
    )
    after_self, cross_q, att_cross, lse_cross, part_cross = call(
        cross_forward,
        [(row, f32, "v"), (part_of, bf16, "h"), (part_of, bf16, "v"), ((8, 2 * slots), f32, "v"), (row, f32, "v")],
        [(dec_lengths, "v"), (enc_lengths, "v"), (x, "v"), (part_self, "v"), (moved_self, "v"), (cross_gain, "v"),
         (cross_query, "v"), (cross_output, "v"), (keys, "v"), (values_t, "v")],
    )
    moved_cross = pair_swap(part_cross)
    after = (part_cross,)
    if quick:
        early, own_cross = call(
            pack_early,
            [(row, f32, "v"), ((width // 2, tokens), bf16, "v")],
            [(after_self, "v"), (cross_gain, "v"), (att_cross, "v")],
            after=after,
        )
        early_moved = stage_swap(early, 0, count)
        after = (early,)
    after_cross, normed_ffn, halves, act, hid, back, *x_two = call(
        ffn_both,
        [(row, f32, "v"), (row, bf16, "h"), (row, f32, "v"), ((tokens, hidden), bf16, "v"), ((tokens, hidden), bf16, "v"),
         (row, f32, "v")] + [((2 * tall, width), f32, "v")] * quick,
        [(after_self, "v"), (part_cross, "v"), (moved_cross, "v"), (ffn_gain, "v"), (low_ffn, "v"), (ffn_in, "v"),
         (ffn_out, "v")] + ([(x_half, "v"), (x_moved, "v")] if quick else []),
        after=after,
    )
    moved_back = pair_swap(back)
    if quick:
        group_a = stage_swap(halves, 2, count)
        x_rest = stage_swap(x_two[0], 1, count)
    grad_cross, low_cross, dq, dk, dv, gain_ffn_grad, part_dq = call(
        cross_backward,
        [(row, f32, "h"), (row, bf16, "v"), (part_of, bf16, "v")] + [((2 * steps, inner), bf16, "v")] * 2
        + [((1, width), f32, "v"), (row, f32, "v")],
        [(dec_lengths, "v"), (enc_lengths, "v"), (after_cross, "v"), (back, "v"), (moved_back, "v"), (ffn_gain, "v"),
         (low_ffn, "v"), (cross_output, "v"), (cross_query, "v"), (cross_q, "v"), (keys_far, "v"), (values, "v"),
         (keys_t, "v"), (lse_cross, "v")],
        after=(rest(back),),
    )
    moved_dq = pair_swap(part_dq)
    after = (rest(part_dq), early_moved) if quick else (rest(part_dq),)
    grad_self, low_self, self_half, gain_cross_grad = call(
        self_grad,
        [(row, f32, "v"), (row, bf16, "v"), ((tokens // 2, width), f32, "v"), ((1, width), f32, "v")],
        [(after_self, "v"), (part_dq, "v"), (moved_dq, "v"), (cross_gain, "v"), (grad_cross, "v")],
        after=after,
    )
    after = (low_self,)
    half = width // 2
    if quick:
        self_a = stage_swap(self_half, 0, count)
    dqkv, bias_grad, parts = call(
        back_all,
        [((tokens, 3 * inner), bf16, "v"), ((8, rel_bias.shape[0]), f32, "v"), ((2 * tokens + 2 * steps, width), f32, "v")],
        [(dec_lengths, "v"), (low_self, "v"), (bias_rows, "v"), (self_output, "v"), (self_query, "v"), (self_key, "v"),
         (self_value, "v"), (qkv, "v"), (lse_self, "v"), (dk, "v"), (dv, "v"), (cross_key, "v"), (cross_value, "v"),
         (act, "v"), (ffn_out, "v")],
        after=after,
    )
    parts_moved = pair_swap(parts)
    after = (rest(parts),)
    if quick:
        self_two, halves_two = call(
            collect,
            [(row, f32, "v"), ((2 * tokens, width), f32, "v")],
            [(self_half, "v"), (self_a, "v"), (halves, "v"), (group_a, "v")],
            after=(parts, x_rest),
        )
        self_rest = stage_swap(self_two, 1, count)
        group_rest = stage_swap(halves_two, 3, count)
        (late_cross,) = call(
            cross_weights,
            [((half + tokens, 2 * inner), f32, "v")],
            [(enc_output, "v"), (dk, "v"), (dv, "v"), (dq, "v"), (low_cross, "v")],
            after=(self_two,),
        )
        late_cross_moved = stage_swap(late_cross, 0, count)
        (self_here,) = call(
            gather_self,
            [((3 * tall + 3 * tokens // 2, width), f32, "v")],
            [(x_moved, "v"), (x_rest, "v"), (self_a, "v"), (self_rest, "v")],
            after=(late_cross,),
        )
        self_there = pair_swap(self_here)
        after = (rest(self_here),)
    dec_packed, small = call(
        named(finish_self_norm, rel_bias.shape[1]),
        [(row, bf16, "v"), ((8, half), f32, "v")],
        [(x, "v"), (parts, "v"), (parts_moved, "v"), (self_gain, "v"), (grad_self, "v"),
         (gain_ffn_grad, "v"), (gain_cross_grad, "v"), (bias_grad, "v")],
        after=after,
    )
    if quick:
        small_moved = stage_swap(small, 0, count)
    after = (small,)
    if quick:
        send_self, keep_self = call(
            self_group,
            [((2 * share, wide), f32, "v")] * 2,
            [(x, "v"), (dqkv, "v"), (low_self, "v"), (att_self, "v"), (self_here, "v"), (self_there, "v"),
             (self_gain, "v"), (bias_rows, "v"), (self_query, "v"), (self_key, "v"), (self_value, "v"), (self_output, "v")],
            scratch=[((3 * tokens, wide), bf16), ((4 * tokens, wide), bf16), ((4 * share, wide), f32)],
            after=after,
        )
        self_first = stage_swap(send_self, 2, count)
        after = (send_self,)
    mark = ((8, 128), f32, "v")
    dec_grad, layer_out, enc_grad, done = call(
        finish_outputs,
        [(dec_input.shape, bf16, "v"), (dec_input.shape, bf16, "v"), (enc_output.shape, bf16, "v"), mark],
        [(dec_lengths, "v"), (dec_packed, "v"), (parts, "v"), (parts_moved, "v"), (after_cross, "v")],
        after=after,
    )
    if not quick:
        return slow_sums(
            locals(), x, after_self, self_gain, cross_gain, rel_bias, enc_output, count
        )
    (keep_cross,) = call(
        cross_keep, [((half, 2 * inner), f32, "v")], [(enc_output, "v"), (dk, "v"), (dv, "v")], after=(done,)
    )
    send_cross, keep_cross, small_two = call(
        cross_fold,
        [((half // 2 + 8, wide), f32, "v"), ((half // 2, wide), f32, "v"), ((16, half), f32, "v")],
        [(keep_cross, "v"), (late_cross_moved, "v"), (early_moved, "v"), (own_cross, "v"), (dq, "v"),
         (low_cross, "v"), (att_cross, "v"), (small, "v"), (small_moved, "v")],
        scratch=[((half, wide), f32)],
        after=(keep_cross,),
    )
    cross_first = stage_swap(send_cross, 1, count)
    (ffn_here,) = call(
        gather_ffn, [((3 * tokens, width), f32, "v")], [(group_a, "v"), (group_rest, "v")], after=(send_cross,)
    )
    ffn_there = pair_swap(ffn_here)
    (send_self2,) = call(
        named(self_fold, share), [((share, wide), f32, "v")], [(keep_self, "v"), (self_first, "v")], after=(ffn_here,)
    )
    self_second = stage_swap(send_self2, 3, count)
    made_ffn, keep_ffn = call(
        ffn_group,
        [((2 * share, 2 * hidden), f32, "v")] * 2,
        [(normed_ffn, "v"), (low_ffn, "v"), (act, "v"), (hid, "v"), (ffn_here, "v"), (ffn_there, "v"), (ffn_in, "v"),
         (ffn_out, "v")],
        scratch=[((4 * tokens, width), bf16), ((4 * tokens, width), bf16), ((4 * share, 2 * hidden), f32)],
        after=(send_self2,),
    )
    send_cross2, small_four = call(
        named(fold_z, share),
        [((half // 4 + 8, wide), f32, "v"), ((8, half), f32, "v")],
        [(keep_cross, "v"), (small_two, "v"), (cross_first, "v")],
        after=(made_ffn,),
    )
    cross_second = stage_swap(send_cross2, 2, count)
    (send_ffn,) = call(relay, [((2 * share, 2 * hidden), f32, "v")], [(made_ffn, "v")], after=(send_cross2,))
    ffn_first = stage_swap(send_ffn, 0, count)
    send_cross3, small_last = call(
        named(fold_last, share),
        [((share + 8, wide), f32, "v"), ((16, half), f32, "v")],
        [(keep_cross, "v"), (small_four, "v"), (cross_first, "v"), (cross_second, "v")],
        after=(send_ffn,),
    )
    cross_third = stage_swap(send_cross3, 3, count)
    (send_ffn2,) = call(
        named(ffn_fold, share), [((share, 2 * hidden), f32, "v")], [(keep_ffn, "v"), (ffn_first, "v")], after=(send_cross3,)
    )
    ffn_second = stage_swap(send_ffn2, 1, count)
    *self_grads, self_out_grad, done = call(
        named(finish_self, share),
        [((share, inner), f32, "v")] * 4 + [mark],
        [(keep_self, "v"), (self_first, "v"), (self_second, "v")],
        after=(rest(send_ffn2),),
    )
    *cross_grads, cross_out_grad, gain_self_sum, gain_cross_sum, gain_ffn_sum, bias_sum, done = call(
        named(finish_cross, rel_bias.shape[1], share),
        [((share, inner), f32, "v")] * 4 + [((width,), f32, "v")] * 3 + [(rel_bias.shape[::-1], f32, "v"), mark],
        [(keep_cross, "v"), (cross_first, "v"), (cross_second, "v"), (small_last, "v"), (cross_third, "v")],
        after=(done,),
    )
    grad_ffn_in, grad_ffn_out = call(
        named(finish_ffn, share),
        [((share, hidden), f32, "h")] * 2,
        [(keep_ffn, "v"), (ffn_first, "v"), (ffn_second, "v")],
        after=(done,),
    )
    return (
        layer_out,
        dec_grad,
        enc_grad,
        *self_grads,
        self_out_grad.T,
        gain_self_sum,
        bias_sum.T,
        *cross_grads,
        cross_out_grad.T,
        gain_cross_sum,
        grad_ffn_in,
        grad_ffn_out.T,
        gain_ffn_sum,
    )


def rest(made):
    (out,) = call(pause, [((8, 128), f32, "v")], [], after=(made,))
    return out


def named(kernel, *given):
    def run(*refs):
        return kernel(*given, *refs)

    run.__name__ = kernel.__name__
    return run


def slow_sums(made, x, after_self, self_gain, cross_gain, rel_bias, enc_output, count):
    width = x.shape[1]
    heads, buckets = rel_bias.shape[1], rel_bias.shape[0]
    inner = made["dq"].shape[1]
    bits = list(range(count.bit_length() - 1))
    order_a, order_b = bits, bits[1::-1] + bits[2:]

    def scattered(order, *grads):
        parts = [grad.reshape(count, -1, grad.shape[1]) for grad in grads]
        widths = [part.shape[2] for part in parts]
        total = scatter_sum(jnp.concatenate(parts, axis=2), order, count)
        return jnp.split(total, np.cumsum(widths)[:-1].tolist(), axis=1)

    def outer(left, right):
        return jnp.einsum("rm,rn->mn", left, right, preferred_element_type=f32)

    def normed(values, gain):
        return (values * inverse_rms(values) * gain).astype(bf16)

    normed_self = normed(x.astype(f32), self_gain)
    normed_cross = normed(after_self, cross_gain)
    enc_flat = enc_output.reshape(-1, width)
    dqkv = made["dqkv"]
    (grad_ffn_in,) = scattered(order_a, outer(made["normed_ffn"], made["hid"]))
    (grad_ffn_out,) = scattered(order_b, outer(made["low_ffn"], made["act"]))
    cross_query, cross_key = scattered(order_a, outer(normed_cross, made["dq"]), outer(enc_flat, made["dk"]))
    cross_value, cross_output = scattered(
        order_b, outer(enc_flat, made["dv"]), outer(made["low_cross"], made["att_cross"])
    )
    self_query, self_key = scattered(
        order_a, outer(normed_self, dqkv[:, :inner]), outer(normed_self, dqkv[:, inner : 2 * inner])
    )
    self_value, self_output = scattered(
        order_b, outer(normed_self, dqkv[:, 2 * inner :]), outer(made["low_self"], made["att_self"])
    )
    small = full_sum(made["small"], count)
    return (
        made["layer_out"],
        made["dec_grad"],
        made["enc_grad"],
        self_query,
        self_key,
        self_value,
        self_output.T,
        small[0:2].reshape(-1),
        small[6, : heads * buckets].reshape(heads, buckets).T,
        cross_query,
        cross_key,
        cross_value,
        cross_output.T,
        small[2:4].reshape(-1),
        grad_ffn_in,
        grad_ffn_out.T,
        small[4:6].reshape(-1),
    )


def solution(mesh):
    in_specs = (
        P("dp", None, None),
        P("dp", None, None),
        P("dp", None),
        P("dp", None),
        P(None, "mp"),
        P(None, "mp"),
        P(None, "mp"),
        P("mp", None),
        P(),
        P(None, "mp"),
        P(None, "mp"),
        P(None, "mp"),
        P(None, "mp"),
        P("mp", None),
        P(),
        P(None, "mp"),
        P("mp", None),
        P(),
        P("dp", None, None),
    )
    out_specs = (
        P("dp", None, None),
        P("dp", None, None),
        P("dp", None, None),
        P("dp", "mp"),
        P("dp", "mp"),
        P("dp", "mp"),
        P("mp", "dp"),
        P(),
        P(None, "mp"),
        P("dp", "mp"),
        P("dp", "mp"),
        P("dp", "mp"),
        P("mp", "dp"),
        P(),
        P("dp", "mp"),
        P("mp", "dp"),
        P(),
    )
    return jax.shard_map(
        on_device, mesh=mesh, in_specs=in_specs, out_specs=out_specs, check_vma=False
    )
```

profile of v0, /device:TPU:1, one launch (start us, length us, event | category | flops | bytes accessed | tf_op | source)
XLA Modules:
  0.0 121.1 jit_solution(10149425644661752129)
XLA Ops:
  0.7 4.5 %self_forward.1 = (bf16[192,768]{1,0:T(8,128)(2,1)}, bf16[192,768]{1,0:T(8,128)(2,1)}, bf16[192,1152]{1,0:T(8,128)(2,1)}, bf16[192,384]{1,0:T(8,128)(2,1)S(1)}, ...) custom-call(s32[1,2]{1,0:T(1,128)} %refs_0_.14, bf16[2,128,768]{2,1,0:T(8,128)(2,1)} %refs_1_.5, ...), custom_call_target="tpu_custom_call" | custom-call | flops 35000000512 | bytes 1000 | tf_op jit(solution)/shard_map/self_forward/pallas_call | solution.py:812
  5.2 2.1 %collective-permute-start.2 = (f32[104,768]{1,0:T(8,128)}, f32[104,768]{1,0:T(8,128)S(1)}, u32[]{:S(2)}, u32[]{:S(2)}) collective-permute-start(f32[104,768]{1,0:T(8,128)} %get-tuple-element.99.refs_7_), channel_id=1, source_target_pairs={{0,2},{1,5},{2,0},{3,7},{4,6},{5,1},{6,4},{7,3},{8,10},{9,13},{10,... | collective-permute-start | bytes 958472 | tf_op jit(solution)/shard_map/ppermute | solution.py:843
  7.4 1.0 collective-permute-start
  8.4 3.1 %encoder_forward.1 = (bf16[1024,384]{1,0:T(8,128)(2,1)S(1)}, bf16[384,1024]{1,0:T(8,128)(2,1)S(1)}, bf16[1024,384]{1,0:T(8,128)(2,1)}, bf16[1024,384]{1,0:T(8,128)(2,1)}, bf16[384,1024]{1,0:T(8,128)(2,1)}) custom-call(bf16[2,512,768]{2,1,0:T(8,128)(2,1)S(1)} %copy-done.4, bf16[768,384]{1,0:T(8,128)(2,1)S(1)} %copy-done.9, bf16[768,384]{1,0:T(8,128)(2,1)S(1)} %copy-done.11, ...), custom_call_target="tpu_custom_call" | custom-call | flops 35000000512 | bytes 1000 | tf_op jit(solution)/shard_map/encoder_forward/pallas_call | solution.py:812
  11.6 3.9 %cross_forward.1 = (f32[192,768]{1,0:T(8,128)S(1)}, bf16[192,384]{1,0:T(8,128)(2,1)}, bf16[192,384]{1,0:T(8,128)(2,1)S(1)}, f32[8,256]{1,0:T(8,128)S(1)}, f32[192,768]{1,0:T(8,128)S(1)}) custom-call(s32[1,2]{1,0:T(1,128)S(1)} %copy-done.34, s32[1,2]{1,0:T(1,128)S(1)} %copy-done.33, bf16[192,768]{1,0:T(8,128)(2,1)S(1)} %copy-done.50, ...), custom_call_target="tpu_custom_call" | custom-call | flops 35000000512 | bytes 1000 | tf_op jit(solution)/shard_map/cross_forward/pallas_call | solution.py:812
  15.7 0.7 pack_early.1
  16.3 1.3 %collective-permute-start.5 = (f32[192,768]{1,0:T(8,128)S(1)}, f32[192,768]{1,0:T(8,128)S(1)}, u32[]{:S(2)}, u32[]{:S(2)}) collective-permute-start(f32[192,768]{1,0:T(8,128)S(1)} %get-tuple-element.101.refs_9_), channel_id=1, source_target_pairs={{0,2},{1,5},{2,0},{3,7},{4,6},{5,1},{6,4},{7,3},{8,10},{9,13},{10,... | collective-permute-start | bytes 1769480 | tf_op jit(solution)/shard_map/ppermute | solution.py:843
  18.1 2.4 %ffn_both.1 = (f32[192,768]{1,0:T(8,128)S(1)}, bf16[192,768]{1,0:T(8,128)(2,1)}, f32[192,768]{1,0:T(8,128)S(1)}, bf16[192,1536]{1,0:T(8,128)(2,1)S(1)}, bf16[192...) custom-call(f32[192,768]{1,0:T(8,128)S(1)} %get-tuple-element.96.refs_0_, ...), custom_call_target="tpu_custom_call" | custom-call | flops 35000000512 | bytes 1000 | tf_op jit(solution)/shard_map/ffn_both/pallas_call | solution.py:812
  20.6 0.7 collective-permute-start.3
  21.3 2.3 %collective-permute-start.9 = (f32[192,768]{1,0:T(8,128)S(1)}, f32[192,768]{1,0:T(8,128)S(1)}, u32[]{:S(2)}, u32[]{:S(2)}) collective-permute-start(f32[192,768]{1,0:T(8,128)S(1)} %get-tuple-element.124.refs_2_), channel_id=1, source_target_pairs={{0,8},{1,17},{2,10},{3,19},{4,12},{5,21},{6,14},{7,23},{8,0},{9,25... | collective-permute-start | bytes 1769480 | tf_op jit(solution)/shard_map/ppermute | solution.py:843
  23.6 0.4 collective-permute-start.7
  24.0 4.7 %cross_backward.1 = (f32[192,768]{1,0:T(8,128)}, bf16[192,768]{1,0:T(8,128)(2,1)S(1)}, bf16[192,384]{1,0:T(8,128)(2,1)S(1)}, bf16[1024,384]{1,0:T(8,128)(2,1)S(1...) custom-call(s32[1,2]{1,0:T(1,128)S(1)} %copy-done.34, s32[1,2]{1,0:T(1,128)S(1)} %copy-done.33, ...), custom_call_target="tpu_custom_call" | custom-call | flops 35000000512 | bytes 1000 | tf_op jit(solution)/shard_map/cross_backward/pallas_call | solution.py:812
  28.8 0.6 collective-permute-start.4
  29.4 1.6 %collective-permute-done.4.refs_2_ = f32[192,768]{1,0:T(8,128)S(1)} collective-permute-done((f32[192,768]{1,0:T(8,128)S(1)}, f32[192,768]{1,0:T(8,128)S(1)}, u32[]{:S(2)}, u32[]{:S(2)}) %collective-permute-start.4) | collective-permute-done | bytes 589856 | tf_op jit(solution)/shard_map/ppermute | solution.py:833
  31.1 0.4 self_grad.1
  31.5 1.0 collective-permute-start.8
  33.2 5.3 %back_all.1 = (bf16[192,1152]{1,0:T(8,128)(2,1)S(1)}, f32[8,32]{1,0:T(8,128)S(1)}, f32[1408,768]{1,0:T(8,128)S(1)}) custom-call(s32[1,2]{1,0:T(1,128)S(1)} %copy-done.34, bf16[192,768]{1,0:T(8,128)(2,1)S(1)} %get-tuple-element.111.refs_1_.refs_15_.refs_2_, f32[6,32]{1,0:T(8,128)S(1)} %bitcast.6, bf16[384,768]{1,0:T(8,128)(2,1)S(1)} %copy-done.19, ...), custom_call_target="tpu_custom_call" | custom-call | flops 35000000512 | bytes 1000 | tf_op jit(solution)/shard_map/back_all/pallas_call | solution.py:812
  38.5 0.4 collective-permute-start.6
  39.0 1.2 %collect.1 = (f32[192,768]{1,0:T(8,128)S(1)}, f32[384,768]{1,0:T(8,128)}) custom-call(f32[96,768]{1,0:T(8,128)S(1)} %get-tuple-element.123.refs_0_, f32[96,768]{1,0:T(8,128)S(1)} %collective-permute-done.8.refs_1_.refs_2_, f32[192,768]{1,0:T(8,128)S(1)} %get-tuple-element.124.refs_2_, f32[192,768]{1,0:T(8,128)S(1)} %collective-permute-done.9.refs_3_.refs_0_, ...), custom_call_target="tpu_custom_call" | custom-call | flops 35000000512 | bytes 1000 | tf_op jit(solution)/shard_map/collect/pallas_call | solution.py:812
  40.2 0.7 collective-permute-start.10
  40.9 1.3 %collective-permute-start.13 = (f32[384,768]{1,0:T(8,128)}, f32[384,768]{1,0:T(8,128)}, u32[]{:S(2)}, u32[]{:S(2)}) collective-permute-start(f32[384,768]{1,0:T(8,128)} %get-tuple-element.137), channel_id=1, source_target_pairs={{0,16},{1,9},{2,18},{3,11},{4,20},{5,13},{6,22},{7,15},{8,24},{9,1... | collective-permute-start | bytes 3538952 | tf_op jit(solution)/shard_map/ppermute | solution.py:843
  42.3 3.1 %cross_weights.1.refs_4_ = f32[576,768]{1,0:T(8,128)} custom-call(bf16[2,512,768]{2,1,0:T(8,128)(2,1)S(1)} %copy-done.5, bf16[1024,384]{1,0:T(8,128)(2,1)S(1)} %get-tuple-element.114.refs_9_.refs_1_, bf16[1024,384]{1,0:T(8,128)(2,1)S(1)} %get-tuple-element.115.refs_10_.refs_2_, bf16[192,384]{1,0:T(8,128)(2,1)S(1)} %get-tuple-element.126.refs_3_.refs_4_, ...), custom_call_target="tpu_custom_call" | custom-call | flops 35000000512 | bytes 1000 | tf_op jit(solution)/shard_map/cross_weights/pallas_call | solution.py:812
  45.4 1.2 %collective-permute-start.14 = (f32[576,768]{1,0:T(8,128)}, f32[576,768]{1,0:T(8,128)}, u32[]{:S(2)}, u32[]{:S(2)}) collective-permute-start(f32[576,768]{1,0:T(8,128)} %cross_weights.1.refs_4_), channel_id=1, source_target_pairs={{0,2},{1,5},{2,0},{3,7},{4,6},{5,1},{6,4},{7,3},{8,10},{9,13},{10,... | collective-permute-start | bytes 5308424 | tf_op jit(solution)/shard_map/ppermute | solution.py:843
  46.6 2.8 %collective-permute-done.10.refs_3_ = f32[192,768]{1,0:T(8,128)S(1)} collective-permute-done((f32[192,768]{1,0:T(8,128)S(1)}, f32[192,768]{1,0:T(8,128)S(1)}, u32[]{:S(2)}, u32[]{:S(2)}) %collective-permute-start.10) | collective-permute-done | bytes 589856 | tf_op jit(solution)/shard_map/ppermute | solution.py:843
  49.5 2.4 %collective-permute-start.11 = (f32[600,768]{1,0:T(8,128)S(1)}, f32[600,768]{1,0:T(8,128)S(1)}, u32[]{:S(2)}, u32[]{:S(2)}) collective-permute-start(f32[600,768]{1,0:T(8,128)S(1)} %gather_self.1.refs_0_.refs_4_), channel_id=1, source_target_pairs={{0,1},{1,0},{2,3},{3,2},{4,5},{5,4},{6,7},{7,6},{8,9},{9,8},{10,11... | collective-permute-start | bytes 5529608 | tf_op jit(solution)/shard_map/ppermute | solution.py:833
  52.0 0.4 finish_self_norm.1
  52.4 0.7 collective-permute-start.15
  53.1 2.2 %collective-permute-done.11.refs_5_ = f32[600,768]{1,0:T(8,128)S(1)} collective-permute-done((f32[600,768]{1,0:T(8,128)S(1)}, f32[600,768]{1,0:T(8,128)S(1)}, u32[]{:S(2)}, u32[]{:S(2)}) %collective-permute-start.11) | collective-permute-done | bytes 1843232 | tf_op jit(solution)/shard_map/ppermute | solution.py:833
  55.4 8.8 %self_group.1 = (f32[96,1536]{1,0:T(8,128)S(1)}, f32[96,1536]{1,0:T(8,128)S(1)}) custom-call(bf16[192,768]{1,0:T(8,128)(2,1)S(1)} %copy-done.51, bf16[192,1152]{1,0:T(8,128)(2,1)S(1)} %get-tuple-element.129.refs_1_, bf16[192,768]{1,0:T(8,128)(2,1)S(1)} %copy-done.53, bf16[192,384]{1,0:T(8,128)(2,1)S(1)} %get-tuple-element.130.refs_3_, ...), custom_call_target="tpu_custom_call" | custom-call | flops 35000000512 | bytes 1000 | tf_op jit(solution)/shard_map/self_group/pallas_call | solution.py:812
  64.1 3.9 %collective-permute-start.12 = (f32[96,1536]{1,0:T(8,128)S(1)}, f32[96,1536]{1,0:T(8,128)S(1)}, u32[]{:S(2)}, u32[]{:S(2)}) collective-permute-start(f32[96,1536]{1,0:T(8,128)S(1)} %get-tuple-element.132.refs_5_), channel_id=1, source_target_pairs={{0,8},{1,17},{2,10},{3,19},{4,12},{5,21},{6,14},{7,23},{8,0},{9,25... | collective-permute-start | bytes 1769480 | tf_op jit(solution)/shard_map/ppermute | solution.py:843
  68.0 2.0 %finish_outputs.1 = (bf16[2,128,768]{2,1,0:T(8,128)(2,1)}, bf16[2,128,768]{2,1,0:T(8,128)(2,1)}, bf16[2,512,768]{2,1,0:T(8,128)(2,1)}, f32[8,128]{1,0:T(8,128)S(1)}) custom-call(s32[1,2]{1,0:T(1,128)S(1)} %copy-done.35, bf16[192,768]{1,0:T(8,128)(2,1)S(1)} %get-tuple-element.128.refs_1_, f32[1408,768]{1,0:T(8,128)S(1)} %get-tuple-element.117.refs_4_.refs_1_.refs_2_, ...), custom_call_target="tpu_custom_call" | custom-call | flops 35000000512 | bytes 1000 | tf_op jit(solution)/shard_map/finish_outputs/pallas_call | solution.py:812
  70.1 1.6 %cross_keep.1.refs_0_.refs_9_ = f32[384,768]{1,0:T(8,128)S(1)} custom-call(bf16[2,512,768]{2,1,0:T(8,128)(2,1)S(1)} %copy-done.6, bf16[1024,384]{1,0:T(8,128)(2,1)S(1)} %copy-done.37, bf16[1024,384]{1,0:T(8,128)(2,1)S(1)} %get-tuple-element.115.refs_10_.refs_2_, f32[8,128]{1,0:T(8,128)S(1)} %get-tuple-element.138.refs_3_), custom_call_target="tpu_custom_call" | custom-call | flops 35000000512 | bytes 1000 | tf_op jit(solution)/shard_map/cross_keep/pallas_call | solution.py:812
  71.8 2.9 %cross_fold.1 = (f32[200,1536]{1,0:T(8,128)S(1)}, f32[192,1536]{1,0:T(8,128)S(1)}, f32[16,384]{1,0:T(8,128)S(1)}) custom-call(f32[384,768]{1,0:T(8,128)S(1)} %cross_keep.1.refs_0_.refs_9_, f32[576,768]{1,0:T(8,128)} %collective-permute-done.14.refs_1_, f32[192,768]{1,0:T(8,128)S(1)} %copy-done.22, bf16[384,192]{1,0:T(8,128)(2,1)S(1)} %get-tuple-element.139.refs_3_, ...), custom_call_target="tpu_custom_call" | custom-call | flops 35000000512 | bytes 1000 | tf_op jit(solution)/shard_map/cross_fold/pallas_call | solution.py:812
  74.8 1.4 %gather_ffn.1.refs_2_.refs_4_ = f32[576,768]{1,0:T(8,128)S(1)} custom-call(f32[192,768]{1,0:T(8,128)S(1)} %copy-done.24, f32[384,768]{1,0:T(8,128)} %collective-permute-done.13.refs_1_, f32[200,1536]{1,0:T(8,128)S(1)} %get-tuple-element.140.refs_2_), custom_call_target="tpu_custom_call" | custom-call | flops 35000000512 | bytes 1000 | tf_op jit(solution)/shard_map/gather_ffn/pallas_call | solution.py:812
  76.2 0.3 collective-permute-start.17
  76.5 7.0 %collective-permute-done.12.refs_1_ = f32[96,1536]{1,0:T(8,128)S(1)} collective-permute-done((f32[96,1536]{1,0:T(8,128)S(1)}, f32[96,1536]{1,0:T(8,128)S(1)}, u32[]{:S(2)}, u32[]{:S(2)}) %collective-permute-start.12) | collective-permute-done | bytes 589856 | tf_op jit(solution)/shard_map/ppermute | solution.py:843
  83.5 0.8 self_fold.1.refs_8_
  84.3 1.0 copy-done.1
  85.3 0.7 copy-done.3
  86.2 6.3 %ffn_group.1 = (f32[96,3072]{1,0:T(8,128)S(1)}, f32[96,3072]{1,0:T(8,128)S(1)}) custom-call(bf16[192,768]{1,0:T(8,128)(2,1)S(1)} %copy-done.49, bf16[192,768]{1,0:T(8,128)(2,1)S(1)} %copy-done.48, bf16[192,1536]{1,0:T(8,128)(2,1)S(1)} %copy-done.42, bf16[192,1536]{1,0:T(8,128)(2,1)S(1)} %get-tuple-element.142.refs_3_, ...), custom_call_target="tpu_custom_call" | custom-call | flops 35000000512 | bytes 1000 | tf_op jit(solution)/shard_map/ffn_group/pallas_call | solution.py:812
  92.7 0.8 collective-permute-start.20
  93.6 0.4 collective-permute-start.19
  94.0 15.8 %collective-permute-done.20.refs_3_.refs_2_ = f32[104,1536]{1,0:T(8,128)S(1)} collective-permute-done((f32[104,1536]{1,0:T(8,128)S(1)}, f32[104,1536]{1,0:T(8,128)S(1)}, u32[]{:S(2)}, u32[]{:S(2)}) %collective-permute-start.20) | collective-permute-done | bytes 639008 | tf_op jit(solution)/shard_map/ppermute | solution.py:843
  110.2 0.6 collective-permute-start.22
  110.8 1.7 %finish_self.1 = (f32[48,384]{1,0:T(8,128)}, f32[48,384]{1,0:T(8,128)}, f32[48,384]{1,0:T(8,128)}, f32[48,384]{1,0:T(8,128)}, f32[8,128]{1,0:T(8,128)S(1)}) custom-call(f32[96,1536]{1,0:T(8,128)S(1)} %get-tuple-element.136.refs_0_, f32[96,1536]{1,0:T(8,128)S(1)} %collective-permute-done.12.refs_1_, f32[48,1536]{1,0:T(8,128)} %collective-permute-done.16.refs_2_, ...), custom_call_target="tpu_custom_call" | custom-call | flops 35000000512 | bytes 1000 | tf_op jit(solution)/shard_map/finish_self/pallas_call | solution.py:812
  112.5 6.7 %collective-permute-done.21.refs_4_ = f32[56,1536]{1,0:T(8,128)S(1)} collective-permute-done((f32[56,1536]{1,0:T(8,128)S(1)}, f32[56,1536]{1,0:T(8,128)S(1)}, u32[]{:S(2)}, u32[]{:S(2)}) %collective-permute-start.21) | collective-permute-done | bytes 344096 | tf_op jit(solution)/shard_map/ppermute | solution.py:843
  119.2 0.7 finish_cross.1
  120.0 0.9 finish_ffn.1
  (150 shorter events, 2.7 us)
Async XLA Ops:
  0.7 7.7 %copy-start.4 = (bf16[2,512,768]{2,1,0:T(8,128)(2,1)S(1)}, bf16[2,512,768]{2,1,0:T(8,128)(2,1)}, u32[]{:S(2)}) copy-start(bf16[2,512,768]{2,1,0:T(8,128)(2,1)} %refs_0_.15) | copy-start | bytes 4718596
  0.7 7.7 %copy-start.9 = (bf16[768,384]{1,0:T(8,128)(2,1)S(1)}, bf16[768,384]{1,0:T(8,128)(2,1)}, u32[]{:S(2)}) copy-start(bf16[768,384]{1,0:T(8,128)(2,1)} %refs_11_.2) | copy-start | bytes 1769476
  0.7 7.7 %copy-start.11 = (bf16[768,384]{1,0:T(8,128)(2,1)S(1)}, bf16[768,384]{1,0:T(8,128)(2,1)}, u32[]{:S(2)}) copy-start(bf16[768,384]{1,0:T(8,128)(2,1)} %refs_12_.1) | copy-start | bytes 1769476
  5.2 12.4 %collective-permute-start.2 = (f32[104,768]{1,0:T(8,128)}, f32[104,768]{1,0:T(8,128)S(1)}, u32[]{:S(2)}, u32[]{:S(2)}) collective-permute-start(f32[104,768]{1,0:T(8,128)} %get-tuple-element.99.refs_7_), channel_id=1, source_target_pairs={{0,2},{1,5},{2,0},{3,7},{4,6},{5,1},{6,4},{7,3},{8,10},{9,13},{10,... | collective-permute-start | bytes 958472 | tf_op jit(solution)/shard_map/ppermute | solution.py:843
  7.4 4.2 %copy-start.7 = (bf16[768,384]{1,0:T(8,128)(2,1)S(1)}, bf16[768,384]{1,0:T(8,128)(2,1)}, u32[]{:S(2)}) copy-start(bf16[768,384]{1,0:T(8,128)(2,1)} %refs_8_.4) | copy-start | bytes 1769476
  7.4 4.2 %copy-start.8 = (bf16[384,768]{1,0:T(8,128)(2,1)S(1)}, bf16[384,768]{1,0:T(8,128)(2,1)}, u32[]{:S(2)}) copy-start(bf16[384,768]{1,0:T(8,128)(2,1)} %refs_7_.4) | copy-start | bytes 1769476
  7.4 4.2 %copy-start.29 = (f32[768]{0:T(1024)S(1)}, f32[768]{0:T(1024)}, u32[]{:S(2)}) copy-start(f32[768]{0:T(1024)} %refs_3_.7) | copy-start | bytes 9220
  7.4 4.2 %copy-start.33 = (s32[1,2]{1,0:T(1,128)S(1)}, s32[1,2]{1,0:T(1,128)}, u32[]{:S(2)}) copy-start(s32[1,2]{1,0:T(1,128)} %refs_1_.9) | copy-start | bytes 28
  7.4 4.2 %copy-start.34 = (s32[1,2]{1,0:T(1,128)S(1)}, s32[1,2]{1,0:T(1,128)}, u32[]{:S(2)}) copy-start(s32[1,2]{1,0:T(1,128)} %refs_0_.14) | copy-start | bytes 28
  7.4 4.2 %copy-start.50 = (bf16[192,768]{1,0:T(8,128)(2,1)S(1)}, bf16[192,768]{1,0:T(8,128)(2,1)}, u32[]{:S(2)}) copy-start(bf16[192,768]{1,0:T(8,128)(2,1)} %get-tuple-element.92.refs_2_.refs_0_) | copy-start | bytes 884740
  7.4 4.1 %collective-permute-start = (f32[192,768]{1,0:T(8,128)S(1)}, f32[192,768]{1,0:T(8,128)S(1)}, u32[]{:S(2)}, u32[]{:S(2)}) collective-permute-start(f32[192,768]{1,0:T(8,128)S(1)} %get-tuple-element.93.refs_3_), channel_id=1, source_target_pairs={{0,1},{1,0},{2,3},{3,2},{4,5},{5,4},{6,7},{7,6},{8,9},{9,8},{10,11... | collective-permute-start | bytes 1769480 | tf_op jit(solution)/shard_map/ppermute | solution.py:833
  15.5 2.1 %collective-permute-start.1 = (f32[192,768]{1,0:T(8,128)S(1)}, f32[192,768]{1,0:T(8,128)S(1)}, u32[]{:S(2)}, u32[]{:S(2)}) collective-permute-start(f32[192,768]{1,0:T(8,128)S(1)} %get-tuple-element.97.refs_3_.refs_1_), channel_id=1, source_target_pairs={{0,1},{1,0},{2,3},{3,2},{4,5},{5,4},{6,7},{7,6},{8,9},{9,8},{10,11... | collective-permute-start | bytes 1769480 | tf_op jit(solution)/shard_map/ppermute | solution.py:833
  16.3 13.0 %collective-permute-start.5 = (f32[192,768]{1,0:T(8,128)S(1)}, f32[192,768]{1,0:T(8,128)S(1)}, u32[]{:S(2)}, u32[]{:S(2)}) collective-permute-start(f32[192,768]{1,0:T(8,128)S(1)} %get-tuple-element.101.refs_9_), channel_id=1, source_target_pairs={{0,2},{1,5},{2,0},{3,7},{4,6},{5,1},{6,4},{7,3},{8,10},{9,13},{10,... | collective-permute-start | bytes 1769480 | tf_op jit(solution)/shard_map/ppermute | solution.py:843
  20.6 3.4 %copy-start.43 = (f32[192,768]{1,0:T(8,128)}, f32[192,768]{1,0:T(8,128)S(1)}, u32[]{:S(2)}) copy-start(f32[192,768]{1,0:T(8,128)S(1)} %get-tuple-element.102.refs_2_.refs_4_) | copy-start | bytes 1769476
  20.6 11.9 %copy-start.41 = (bf16[192,1536]{1,0:T(8,128)(2,1)}, bf16[192,1536]{1,0:T(8,128)(2,1)S(1)}, u32[]{:S(2)}) copy-start(bf16[192,1536]{1,0:T(8,128)(2,1)S(1)} %get-tuple-element.116.refs_13_.refs_2_) | copy-start | bytes 1769476
  20.6 3.4 %copy-start.38 = (bf16[1024,384]{1,0:T(8,128)(2,1)S(1)}, bf16[1024,384]{1,0:T(8,128)(2,1)}, u32[]{:S(2)}) copy-start(bf16[1024,384]{1,0:T(8,128)(2,1)} %get-tuple-element.105.refs_10_) | copy-start | bytes 2359300
  20.6 3.4 %copy-start.39 = (bf16[1024,384]{1,0:T(8,128)(2,1)S(1)}, bf16[1024,384]{1,0:T(8,128)(2,1)}, u32[]{:S(2)}) copy-start(bf16[1024,384]{1,0:T(8,128)(2,1)} %get-tuple-element.106.refs_11_) | copy-start | bytes 2359300
  20.6 3.4 %copy-start.40 = (bf16[384,1024]{1,0:T(8,128)(2,1)S(1)}, bf16[384,1024]{1,0:T(8,128)(2,1)}, u32[]{:S(2)}) copy-start(bf16[384,1024]{1,0:T(8,128)(2,1)} %get-tuple-element.107.refs_12_) | copy-start | bytes 2359300
  20.6 3.3 %collective-permute-start.3 = (f32[192,768]{1,0:T(8,128)S(1)}, f32[192,768]{1,0:T(8,128)S(1)}, u32[]{:S(2)}, u32[]{:S(2)}) collective-permute-start(f32[192,768]{1,0:T(8,128)S(1)} %get-tuple-element.103.refs_0_.refs_3_), channel_id=1, source_target_pairs={{0,1},{1,0},{2,3},{3,2},{4,5},{5,4},{6,7},{7,6},{8,9},{9,8},{10,11... | collective-permute-start | bytes 1769480 | tf_op jit(solution)/shard_map/ppermute | solution.py:833
  21.3 17.7 %collective-permute-start.9 = (f32[192,768]{1,0:T(8,128)S(1)}, f32[192,768]{1,0:T(8,128)S(1)}, u32[]{:S(2)}, u32[]{:S(2)}) collective-permute-start(f32[192,768]{1,0:T(8,128)S(1)} %get-tuple-element.124.refs_2_), channel_id=1, source_target_pairs={{0,8},{1,17},{2,10},{3,19},{4,12},{5,21},{6,14},{7,23},{8,0},{9,25... | collective-permute-start | bytes 1769480 | tf_op jit(solution)/shard_map/ppermute | solution.py:843
  23.6 15.4 %collective-permute-start.7 = (f32[208,768]{1,0:T(8,128)S(1)}, f32[208,768]{1,0:T(8,128)S(1)}, u32[]{:S(2)}, u32[]{:S(2)}) collective-permute-start(f32[208,768]{1,0:T(8,128)S(1)} %get-tuple-element.122), channel_id=1, source_target_pairs={{0,4},{1,3},{2,6},{3,1},{4,0},{5,7},{6,2},{7,5},{8,12},{9,11},{10,... | collective-permute-start | bytes 1916936 | tf_op jit(solution)/shard_map/ppermute | solution.py:843
  28.8 13.4 %copy-start.36 = (bf16[1024,384]{1,0:T(8,128)(2,1)}, bf16[1024,384]{1,0:T(8,128)(2,1)S(1)}, u32[]{:S(2)}) copy-start(bf16[1024,384]{1,0:T(8,128)(2,1)S(1)} %get-tuple-element.114.refs_9_.refs_1_) | copy-start | bytes 2359300
  28.8 13.4 %copy-start.54 = (bf16[192,768]{1,0:T(8,128)(2,1)}, bf16[192,768]{1,0:T(8,128)(2,1)S(1)}, u32[]{:S(2)}) copy-start(bf16[192,768]{1,0:T(8,128)(2,1)S(1)} %get-tuple-element.127.refs_4_.refs_5_) | copy-start | bytes 884740
  28.8 13.4 %copy-start.56 = (bf16[192,384]{1,0:T(8,128)(2,1)}, bf16[192,384]{1,0:T(8,128)(2,1)S(1)}, u32[]{:S(2)}) copy-start(bf16[192,384]{1,0:T(8,128)(2,1)S(1)} %get-tuple-element.126.refs_3_.refs_4_) | copy-start | bytes 442372
  28.8 2.2 %collective-permute-start.4 = (f32[192,768]{1,0:T(8,128)S(1)}, f32[192,768]{1,0:T(8,128)S(1)}, u32[]{:S(2)}, u32[]{:S(2)}) collective-permute-start(f32[192,768]{1,0:T(8,128)S(1)} %get-tuple-element.109.refs_0_.refs_1_), channel_id=1, source_target_pairs={{0,1},{1,0},{2,3},{3,2},{4,5},{5,4},{6,7},{7,6},{8,9},{9,8},{10,11... | collective-permute-start | bytes 1769480 | tf_op jit(solution)/shard_map/ppermute | solution.py:833
  31.5 7.0 %copy-start.52 = (bf16[192,768]{1,0:T(8,128)(2,1)}, bf16[192,768]{1,0:T(8,128)(2,1)S(1)}, u32[]{:S(2)}) copy-start(bf16[192,768]{1,0:T(8,128)(2,1)S(1)} %get-tuple-element.111.refs_1_.refs_15_.refs_2_) | copy-start | bytes 884740
  31.5 7.5 %collective-permute-start.8 = (f32[96,768]{1,0:T(8,128)S(1)}, f32[96,768]{1,0:T(8,128)S(1)}, u32[]{:S(2)}, u32[]{:S(2)}) collective-permute-start(f32[96,768]{1,0:T(8,128)S(1)} %get-tuple-element.123.refs_0_), channel_id=1, source_target_pairs={{0,2},{1,5},{2,0},{3,7},{4,6},{5,1},{6,4},{7,3},{8,10},{9,13},{10,... | collective-permute-start | bytes 884744 | tf_op jit(solution)/shard_map/ppermute | solution.py:843
  38.5 3.7 %copy-start.5 = (bf16[2,512,768]{2,1,0:T(8,128)(2,1)S(1)}, bf16[2,512,768]{2,1,0:T(8,128)(2,1)}, u32[]{:S(2)}) copy-start(bf16[2,512,768]{2,1,0:T(8,128)(2,1)} %refs_0_.15) | copy-start | bytes 4718596
  38.5 13.4 %collective-permute-start.6 = (f32[1408,768]{1,0:T(8,128)S(1)}, f32[1408,768]{1,0:T(8,128)S(1)}, u32[]{:S(2)}, u32[]{:S(2)}) collective-permute-start(f32[1408,768]{1,0:T(8,128)S(1)} %get-tuple-element.117.refs_4_.refs_1_.refs_2_), channel_id=1, source_target_pairs={{0,1},{1,0},{2,3},{3,2},{4,5},{5,4},{6,7},{7,6},{8,9},{9,8},{10,11... | collective-permute-start | bytes 12976136 | tf_op jit(solution)/shard_map/ppermute | solution.py:833
  40.2 9.1 %collective-permute-start.10 = (f32[192,768]{1,0:T(8,128)S(1)}, f32[192,768]{1,0:T(8,128)S(1)}, u32[]{:S(2)}, u32[]{:S(2)}) collective-permute-start(f32[192,768]{1,0:T(8,128)S(1)} %get-tuple-element.125.refs_5_), channel_id=1, source_target_pairs={{0,4},{1,3},{2,6},{3,1},{4,0},{5,7},{6,2},{7,5},{8,12},{9,11},{10,... | collective-permute-start | bytes 1769480 | tf_op jit(solution)/shard_map/ppermute | solution.py:843
  40.9 33.8 %collective-permute-start.13 = (f32[384,768]{1,0:T(8,128)}, f32[384,768]{1,0:T(8,128)}, u32[]{:S(2)}, u32[]{:S(2)}) collective-permute-start(f32[384,768]{1,0:T(8,128)} %get-tuple-element.137), channel_id=1, source_target_pairs={{0,16},{1,9},{2,18},{3,11},{4,20},{5,13},{6,22},{7,15},{8,24},{9,1... | collective-permute-start | bytes 3538952 | tf_op jit(solution)/shard_map/ppermute | solution.py:843
  42.2 7.1 %copy-start.26 = (f32[104,768]{1,0:T(8,128)S(1)}, f32[104,768]{1,0:T(8,128)}, u32[]{:S(2)}) copy-start(f32[104,768]{1,0:T(8,128)} %copy-done.25) | copy-start | bytes 958468
  45.4 26.4 %collective-permute-start.14 = (f32[576,768]{1,0:T(8,128)}, f32[576,768]{1,0:T(8,128)}, u32[]{:S(2)}, u32[]{:S(2)}) collective-permute-start(f32[576,768]{1,0:T(8,128)} %cross_weights.1.refs_4_), channel_id=1, source_target_pairs={{0,2},{1,5},{2,0},{3,7},{4,6},{5,1},{6,4},{7,3},{8,10},{9,13},{10,... | collective-permute-start | bytes 5308424 | tf_op jit(solution)/shard_map/ppermute | solution.py:843
  49.5 5.8 %collective-permute-start.11 = (f32[600,768]{1,0:T(8,128)S(1)}, f32[600,768]{1,0:T(8,128)S(1)}, u32[]{:S(2)}, u32[]{:S(2)}) collective-permute-start(f32[600,768]{1,0:T(8,128)S(1)} %gather_self.1.refs_0_.refs_4_), channel_id=1, source_target_pairs={{0,1},{1,0},{2,3},{3,2},{4,5},{5,4},{6,7},{7,6},{8,9},{9,8},{10,11... | collective-permute-start | bytes 5529608 | tf_op jit(solution)/shard_map/ppermute | solution.py:833
  51.9 3.4 %copy-start.14 = (bf16[768,384]{1,0:T(8,128)(2,1)S(1)}, bf16[768,384]{1,0:T(8,128)(2,1)}, u32[]{:S(2)}) copy-start(bf16[768,384]{1,0:T(8,128)(2,1)} %refs_8_.5) | copy-start | bytes 1769476
  51.9 3.4 %copy-start.16 = (bf16[768,384]{1,0:T(8,128)(2,1)S(1)}, bf16[768,384]{1,0:T(8,128)(2,1)}, u32[]{:S(2)}) copy-start(bf16[768,384]{1,0:T(8,128)(2,1)} %refs_9_.1) | copy-start | bytes 1769476
  51.9 3.4 %copy-start.18 = (bf16[768,384]{1,0:T(8,128)(2,1)S(1)}, bf16[768,384]{1,0:T(8,128)(2,1)}, u32[]{:S(2)}) copy-start(bf16[768,384]{1,0:T(8,128)(2,1)} %refs_10_.1) | copy-start | bytes 1769476
  52.4 19.4 %collective-permute-start.15 = (f32[8,384]{1,0:T(8,128)S(1)}, f32[8,384]{1,0:T(8,128)S(1)}, u32[]{:S(2)}, u32[]{:S(2)}) collective-permute-start(f32[8,384]{1,0:T(8,128)S(1)} %get-tuple-element.131.refs_12_.refs_7_), channel_id=1, source_target_pairs={{0,2},{1,5},{2,0},{3,7},{4,6},{5,1},{6,4},{7,3},{8,10},{9,13},{10,... | collective-permute-start | bytes 36872 | tf_op jit(solution)/shard_map/ppermute | solution.py:843
  55.3 12.7 %copy-start.35 = (s32[1,2]{1,0:T(1,128)S(1)}, s32[1,2]{1,0:T(1,128)}, u32[]{:S(2)}) copy-start(s32[1,2]{1,0:T(1,128)} %refs_0_.14) | copy-start | bytes 28
  55.3 12.7 %copy-start.44 = (f32[192,768]{1,0:T(8,128)S(1)}, f32[192,768]{1,0:T(8,128)}, u32[]{:S(2)}) copy-start(f32[192,768]{1,0:T(8,128)} %copy-done.43) | copy-start | bytes 1769476
  64.1 19.4 %collective-permute-start.12 = (f32[96,1536]{1,0:T(8,128)S(1)}, f32[96,1536]{1,0:T(8,128)S(1)}, u32[]{:S(2)}, u32[]{:S(2)}) collective-permute-start(f32[96,1536]{1,0:T(8,128)S(1)} %get-tuple-element.132.refs_5_), channel_id=1, source_target_pairs={{0,8},{1,17},{2,10},{3,19},{4,12},{5,21},{6,14},{7,23},{8,0},{9,25... | collective-permute-start | bytes 1769480 | tf_op jit(solution)/shard_map/ppermute | solution.py:843
  74.7 17.9 %collective-permute-start.18 = (f32[200,1536]{1,0:T(8,128)S(1)}, f32[200,1536]{1,0:T(8,128)S(1)}, u32[]{:S(2)}, u32[]{:S(2)}) collective-permute-start(f32[200,1536]{1,0:T(8,128)S(1)} %get-tuple-element.140.refs_2_), channel_id=1, source_target_pairs={{0,4},{1,3},{2,6},{3,1},{4,0},{5,7},{6,2},{7,5},{8,12},{9,11},{10,... | collective-permute-start | bytes 3686408 | tf_op jit(solution)/shard_map/ppermute | solution.py:843
  76.2 8.1 %collective-permute-start.17 = (f32[576,768]{1,0:T(8,128)S(1)}, f32[576,768]{1,0:T(8,128)S(1)}, u32[]{:S(2)}, u32[]{:S(2)}) collective-permute-start(f32[576,768]{1,0:T(8,128)S(1)} %gather_ffn.1.refs_2_.refs_4_), channel_id=1, source_target_pairs={{0,1},{1,0},{2,3},{3,2},{4,5},{5,4},{6,7},{7,6},{8,9},{9,8},{10,11... | collective-permute-start | bytes 5308424 | tf_op jit(solution)/shard_map/ppermute | solution.py:833
  84.3 26.5 %collective-permute-start.16 = (f32[48,1536]{1,0:T(8,128)}, f32[48,1536]{1,0:T(8,128)}, u32[]{:S(2)}, u32[]{:S(2)}) collective-permute-start(f32[48,1536]{1,0:T(8,128)} %self_fold.1.refs_8_), channel_id=1, source_target_pairs={{0,16},{1,9},{2,18},{3,11},{4,20},{5,13},{6,22},{7,15},{8,24},{9,1... | collective-permute-start | bytes 884744 | tf_op jit(solution)/shard_map/ppermute | solution.py:843
  92.7 17.1 %collective-permute-start.20 = (f32[104,1536]{1,0:T(8,128)S(1)}, f32[104,1536]{1,0:T(8,128)S(1)}, u32[]{:S(2)}, u32[]{:S(2)}) collective-permute-start(f32[104,1536]{1,0:T(8,128)S(1)} %get-tuple-element.147.refs_1_), channel_id=1, source_target_pairs={{0,8},{1,17},{2,10},{3,19},{4,12},{5,21},{6,14},{7,23},{8,0},{9,25... | collective-permute-start | bytes 1916936 | tf_op jit(solution)/shard_map/ppermute | solution.py:843
  93.6 16.5 %collective-permute-start.19 = (f32[96,3072]{1,0:T(8,128)S(1)}, f32[96,3072]{1,0:T(8,128)S(1)}, u32[]{:S(2)}, u32[]{:S(2)}) collective-permute-start(f32[96,3072]{1,0:T(8,128)S(1)} %relay.1.refs_4_), channel_id=1, source_target_pairs={{0,2},{1,5},{2,0},{3,7},{4,6},{5,1},{6,4},{7,3},{8,10},{9,13},{10,... | collective-permute-start | bytes 3538952 | tf_op jit(solution)/shard_map/ppermute | solution.py:843
  109.8 9.4 %collective-permute-start.21 = (f32[56,1536]{1,0:T(8,128)S(1)}, f32[56,1536]{1,0:T(8,128)S(1)}, u32[]{:S(2)}, u32[]{:S(2)}) collective-permute-start(f32[56,1536]{1,0:T(8,128)S(1)} %get-tuple-element.149.refs_2_), channel_id=1, source_target_pairs={{0,16},{1,9},{2,18},{3,11},{4,20},{5,13},{6,22},{7,15},{8,24},{9,1... | collective-permute-start | bytes 1032200 | tf_op jit(solution)/shard_map/ppermute | solution.py:843
  110.2 9.8 %collective-permute-start.22 = (f32[48,3072]{1,0:T(8,128)S(1)}, f32[48,3072]{1,0:T(8,128)S(1)}, u32[]{:S(2)}, u32[]{:S(2)}) collective-permute-start(f32[48,3072]{1,0:T(8,128)S(1)} %ffn_fold.1.refs_0_), channel_id=1, source_target_pairs={{0,4},{1,3},{2,6},{3,1},{4,0},{5,7},{6,2},{7,5},{8,12},{9,11},{10,... | collective-permute-start | bytes 1769480 | tf_op jit(solution)/shard_map/ppermute | solution.py:843
  (36 other events, 79.4 us)
where the time goes:
time: 122 us; the launch traced here: 121 us
  Pallas kernels  57.4 us (47%)
  waiting for transfers between devices  36.1 us (30%)
  starting transfers between devices  22.6 us (19%)
  local copies, waits for them, and re-layouts  3.46 us (3%)
  between operations  1.58 us (1%)
    pallas_call x30, Pallas kernels, call(): pl.pallas_call(body, out_shape=[pltpu.HBM(shape, kind) if place == 'h' el...  57.4 us
    ppermute x16, waiting for transfers between devices, stage_swap(): return lax.ppermute(values, ('dp', 'mp'), pairs)  32.3 us
    ppermute x16, starting transfers between devices, stage_swap(): return lax.ppermute(values, ('dp', 'mp'), pairs)  17.1 us
    ppermute x7, starting transfers between devices, pair_swap(): return lax.ppermute(values, 'mp', [(0, 1), (1, 0)])  5.45 us
    ppermute x7, waiting for transfers between devices, pair_swap(): return lax.ppermute(values, 'mp', [(0, 1), (1, 0)])  3.86 us
    unnamed x122, local copies, waits for them, and re-layouts  3.46 us
  transfers between devices with their start and end apart: 23, of which 6 were waited for; matrix products, arithmetic and copies ran while one was open for 0% of the time, Pallas kernels for 43%

commit v1 on v0

--- a/solution.py
+++ b/solution.py
@@ -655,9 +655,8 @@
 
 
 def finish_cross(
-    heads, rows, keep, first, second, sums, third, q_out, k_out, v_out, o_out, gain_s, gain_c, gain_f, bias_out, token
+    heads, rows, keep, first, second, sums, third, q_out, k_out, v_out, o_out, gain_s, gain_c, gain_f, bias_out
 ):
-    token[...] = jnp.zeros_like(token)
     inner = q_out.shape[1]
     total = three_sum(rows, own_bit(3), keep, first, second) + third[:rows, :]
     for k, out in enumerate((q_out, k_out, v_out, o_out)):
@@ -688,7 +687,8 @@
     out[...] = chunk_of(keep, step, rows) + chunk_of(first, step, rows)
 
 
-def finish_ffn(rows, keep, first, second, in_out, out_out):
+def finish_ffn(rows, keep, first, second, in_out, out_out, token):
+    token[...] = jnp.zeros_like(token)
     step = own_bit(1)
     total = chunk_of(keep, step, rows) + chunk_of(first, step, rows) + second[...]
     hidden = in_out.shape[1]
@@ -1008,18 +1008,22 @@
         self_first = stage_swap(send_self, 2, count)
         after = (send_self,)
     mark = ((8, 128), f32, "v")
-    dec_grad, layer_out, enc_grad, done = call(
-        finish_outputs,
-        [(dec_input.shape, bf16, "v"), (dec_input.shape, bf16, "v"), (enc_output.shape, bf16, "v"), mark],
-        [(dec_lengths, "v"), (dec_packed, "v"), (parts, "v"), (parts_moved, "v"), (after_cross, "v")],
-        after=after,
-    )
+
+    def outputs(after):
+        return call(
+            finish_outputs,
+            [(dec_input.shape, bf16, "v"), (dec_input.shape, bf16, "v"), (enc_output.shape, bf16, "v"), mark],
+            [(dec_lengths, "v"), (dec_packed, "v"), (parts, "v"), (parts_moved, "v"), (after_cross, "v")],
+            after=after,
+        )
+
     if not quick:
+        dec_grad, layer_out, enc_grad, done = outputs(after)
         return slow_sums(
             locals(), x, after_self, self_gain, cross_gain, rel_bias, enc_output, count
         )
     (keep_cross,) = call(
-        cross_keep, [((half, 2 * inner), f32, "v")], [(enc_output, "v"), (dk, "v"), (dv, "v")], after=(done,)
+        cross_keep, [((half, 2 * inner), f32, "v")], [(enc_output, "v"), (dk, "v"), (dv, "v")], after=(send_self,)
     )
     send_cross, keep_cross, small_two = call(
         cross_fold,
@@ -1034,54 +1038,55 @@
         gather_ffn, [((3 * tokens, width), f32, "v")], [(group_a, "v"), (group_rest, "v")], after=(send_cross,)
     )
     ffn_there = pair_swap(ffn_here)
-    (send_self2,) = call(
-        named(self_fold, share), [((share, wide), f32, "v")], [(keep_self, "v"), (self_first, "v")], after=(ffn_here,)
-    )
-    self_second = stage_swap(send_self2, 3, count)
+    dec_grad, layer_out, enc_grad, done = outputs((ffn_here,))
     made_ffn, keep_ffn = call(
         ffn_group,
         [((2 * share, 2 * hidden), f32, "v")] * 2,
         [(normed_ffn, "v"), (low_ffn, "v"), (act, "v"), (hid, "v"), (ffn_here, "v"), (ffn_there, "v"), (ffn_in, "v"),
          (ffn_out, "v")],
         scratch=[((4 * tokens, width), bf16), ((4 * tokens, width), bf16), ((4 * share, 2 * hidden), f32)],
-        after=(send_self2,),
-    )
+        after=(done,),
+    )
+    (send_self2,) = call(
+        named(self_fold, share), [((share, wide), f32, "v")], [(keep_self, "v"), (self_first, "v")], after=(made_ffn,)
+    )
+    self_second = stage_swap(send_self2, 3, count)
     send_cross2, small_four = call(
         named(fold_z, share),
         [((half // 4 + 8, wide), f32, "v"), ((8, half), f32, "v")],
         [(keep_cross, "v"), (small_two, "v"), (cross_first, "v")],
-        after=(made_ffn,),
+        after=(send_self2,),
     )
     cross_second = stage_swap(send_cross2, 2, count)
     (send_ffn,) = call(relay, [((2 * share, 2 * hidden), f32, "v")], [(made_ffn, "v")], after=(send_cross2,))
     ffn_first = stage_swap(send_ffn, 0, count)
+    *self_grads, self_out_grad, done = call(
+        named(finish_self, share),
+        [((share, inner), f32, "v")] * 4 + [mark],
+        [(keep_self, "v"), (self_first, "v"), (self_second, "v")],
+        after=(send_ffn,),
+    )
+    (send_ffn2,) = call(
+        named(ffn_fold, share), [((share, 2 * hidden), f32, "v")], [(keep_ffn, "v"), (ffn_first, "v")], after=(done,)
+    )
+    ffn_second = stage_swap(send_ffn2, 1, count)
     send_cross3, small_last = call(
         named(fold_last, share),
         [((share + 8, wide), f32, "v"), ((16, half), f32, "v")],
         [(keep_cross, "v"), (small_four, "v"), (cross_first, "v"), (cross_second, "v")],
-        after=(send_ffn,),
+        after=(send_ffn2,),
     )
     cross_third = stage_swap(send_cross3, 3, count)
-    (send_ffn2,) = call(
-        named(ffn_fold, share), [((share, 2 * hidden), f32, "v")], [(keep_ffn, "v"), (ffn_first, "v")], after=(send_cross3,)
-    )
-    ffn_second = stage_swap(send_ffn2, 1, count)
-    *self_grads, self_out_grad, done = call(
-        named(finish_self, share),
-        [((share, inner), f32, "v")] * 4 + [mark],
-        [(keep_self, "v"), (self_first, "v"), (self_second, "v")],
-        after=(rest(send_ffn2),),
-    )
-    *cross_grads, cross_out_grad, gain_self_sum, gain_cross_sum, gain_ffn_sum, bias_sum, done = call(
+    grad_ffn_in, grad_ffn_out, done = call(
+        named(finish_ffn, share),
+        [((share, hidden), f32, "h")] * 2 + [mark],
+        [(keep_ffn, "v"), (ffn_first, "v"), (ffn_second, "v")],
+        after=(rest(send_cross3),),
+    )
+    *cross_grads, cross_out_grad, gain_self_sum, gain_cross_sum, gain_ffn_sum, bias_sum = call(
         named(finish_cross, rel_bias.shape[1], share),
-        [((share, inner), f32, "v")] * 4 + [((width,), f32, "v")] * 3 + [(rel_bias.shape[::-1], f32, "v"), mark],
+        [((share, inner), f32, "h")] * 4 + [((width,), f32, "h")] * 3 + [(rel_bias.shape[::-1], f32, "h")],
         [(keep_cross, "v"), (cross_first, "v"), (cross_second, "v"), (small_last, "v"), (cross_third, "v")],
-        after=(done,),
-    )
-    grad_ffn_in, grad_ffn_out = call(
-        named(finish_ffn, share),
-        [((share, hidden), f32, "h")] * 2,
-        [(keep_ffn, "v"), (ffn_first, "v"), (ffn_second, "v")],
         after=(done,),
     )
     return (

time: 122 us -> 120 us (0.984)
  local copies, waits for them, and re-layouts: 3.46 us -> 1.65 us
  starting transfers between devices: 22.6 us -> 24.3 us
  Pallas kernels: 57.4 us -> 55.7 us
    unnamed x122 -> x114, local copies, waits for them, and re-layouts: 3.46 us -> 1.65 us
    pallas_call x30, Pallas kernels: 57.4 us -> 55.7 us  [call(): pl.pallas_call(body, out_shape=[pltpu.HBM(shape, kind) if place == 'h' el...]
    ppermute x7, waiting for transfers between devices: 3.86 us -> 5.18 us  [pair_swap(): return lax.ppermute(values, 'mp', [(0, 1), (1, 0)])]
  transfers between devices with their start and end apart: 23 -> 23, of which waited for: 6 -> 10; matrix products, arithmetic and copies ran while one was open for 0% -> 0% of each run, Pallas kernels for 43% -> 42%
where the time goes in v1:
time: 120 us
  Pallas kernels  55.7 us (46%)
  waiting for transfers between devices  36.7 us (31%)
  starting transfers between devices  24.3 us (20%)
  local copies, waits for them, and re-layouts  1.65 us (1%)
  between operations  1.56 us (1%)
    pallas_call x30, Pallas kernels, call(): pl.pallas_call(body, out_shape=[pltpu.HBM(shape, kind) if place == 'h' el...  55.7 us
    ppermute x16, waiting for transfers between devices, stage_swap(): return lax.ppermute(values, ('dp', 'mp'), pairs)  31.5 us
    ppermute x16, starting transfers between devices, stage_swap(): return lax.ppermute(values, ('dp', 'mp'), pairs)  18.1 us
    ppermute x7, starting transfers between devices, pair_swap(): return lax.ppermute(values, 'mp', [(0, 1), (1, 0)])  6.2 us
    ppermute x7, waiting for transfers between devices, pair_swap(): return lax.ppermute(values, 'mp', [(0, 1), (1, 0)])  5.18 us
  transfers between devices with their start and end apart: 23, of which 10 were waited for; matrix products, arithmetic and copies ran while one was open for 0% of the time, Pallas kernels for 42%

profile of v1, /device:TPU:1, one launch (start us, length us, event | category | flops | bytes accessed | tf_op | source)
XLA Modules:
  0.0 119.9 jit_solution(5980519139389146465)
XLA Ops:
  0.7 4.5 %self_forward.1 = (bf16[192,768]{1,0:T(8,128)(2,1)}, bf16[192,768]{1,0:T(8,128)(2,1)}, bf16[192,1152]{1,0:T(8,128)(2,1)}, bf16[192,384]{1,0:T(8,128)(2,1)S(1)}, ...) custom-call(s32[1,2]{1,0:T(1,128)} %refs_0_.15, bf16[2,128,768]{2,1,0:T(8,128)(2,1)} %refs_1_.5, ...), custom_call_target="tpu_custom_call" | custom-call | flops 35000000512 | bytes 1000 | tf_op jit(solution)/shard_map/self_forward/pallas_call | solution.py:812
  5.2 2.1 %collective-permute-start.2 = (f32[104,768]{1,0:T(8,128)}, f32[104,768]{1,0:T(8,128)S(1)}, u32[]{:S(2)}, u32[]{:S(2)}) collective-permute-start(f32[104,768]{1,0:T(8,128)} %get-tuple-element.99.refs_7_), channel_id=1, source_target_pairs={{0,2},{1,5},{2,0},{3,7},{4,6},{5,1},{6,4},{7,3},{8,10},{9,13},{10,... | collective-permute-start | bytes 958472 | tf_op jit(solution)/shard_map/ppermute | solution.py:843
  7.4 1.0 collective-permute-start
  8.4 3.1 %encoder_forward.1 = (bf16[1024,384]{1,0:T(8,128)(2,1)S(1)}, bf16[384,1024]{1,0:T(8,128)(2,1)S(1)}, bf16[1024,384]{1,0:T(8,128)(2,1)}, bf16[1024,384]{1,0:T(8,128)(2,1)}, bf16[384,1024]{1,0:T(8,128)(2,1)}) custom-call(bf16[2,512,768]{2,1,0:T(8,128)(2,1)S(1)} %copy-done.4, bf16[768,384]{1,0:T(8,128)(2,1)S(1)} %copy-done.8, bf16[768,384]{1,0:T(8,128)(2,1)S(1)} %copy-done.10, ...), custom_call_target="tpu_custom_call" | custom-call | flops 35000000512 | bytes 1000 | tf_op jit(solution)/shard_map/encoder_forward/pallas_call | solution.py:812
  11.6 3.9 %cross_forward.1 = (f32[192,768]{1,0:T(8,128)S(1)}, bf16[192,384]{1,0:T(8,128)(2,1)}, bf16[192,384]{1,0:T(8,128)(2,1)S(1)}, f32[8,256]{1,0:T(8,128)S(1)}, f32[192,768]{1,0:T(8,128)S(1)}) custom-call(s32[1,2]{1,0:T(1,128)S(1)} %copy-done.32, s32[1,2]{1,0:T(1,128)S(1)} %copy-done.31, bf16[192,768]{1,0:T(8,128)(2,1)S(1)} %copy-done.46, ...), custom_call_target="tpu_custom_call" | custom-call | flops 35000000512 | bytes 1000 | tf_op jit(solution)/shard_map/cross_forward/pallas_call | solution.py:812
  15.6 0.7 pack_early.1
  16.3 1.3 %collective-permute-start.5 = (f32[192,768]{1,0:T(8,128)S(1)}, f32[192,768]{1,0:T(8,128)S(1)}, u32[]{:S(2)}, u32[]{:S(2)}) collective-permute-start(f32[192,768]{1,0:T(8,128)S(1)} %get-tuple-element.101.refs_9_), channel_id=1, source_target_pairs={{0,2},{1,5},{2,0},{3,7},{4,6},{5,1},{6,4},{7,3},{8,10},{9,13},{10,... | collective-permute-start | bytes 1769480 | tf_op jit(solution)/shard_map/ppermute | solution.py:843
  18.1 2.5 %ffn_both.1 = (f32[192,768]{1,0:T(8,128)S(1)}, bf16[192,768]{1,0:T(8,128)(2,1)}, f32[192,768]{1,0:T(8,128)S(1)}, bf16[192,1536]{1,0:T(8,128)(2,1)S(1)}, bf16[192...) custom-call(f32[192,768]{1,0:T(8,128)S(1)} %get-tuple-element.96.refs_0_, ...), custom_call_target="tpu_custom_call" | custom-call | flops 35000000512 | bytes 1000 | tf_op jit(solution)/shard_map/ffn_both/pallas_call | solution.py:812
  20.6 0.7 collective-permute-start.3
  21.3 2.3 %collective-permute-start.9 = (f32[192,768]{1,0:T(8,128)S(1)}, f32[192,768]{1,0:T(8,128)S(1)}, u32[]{:S(2)}, u32[]{:S(2)}) collective-permute-start(f32[192,768]{1,0:T(8,128)S(1)} %get-tuple-element.124.refs_2_), channel_id=1, source_target_pairs={{0,8},{1,17},{2,10},{3,19},{4,12},{5,21},{6,14},{7,23},{8,0},{9,25... | collective-permute-start | bytes 1769480 | tf_op jit(solution)/shard_map/ppermute | solution.py:843
  24.0 4.7 %cross_backward.1 = (f32[192,768]{1,0:T(8,128)}, bf16[192,768]{1,0:T(8,128)(2,1)S(1)}, bf16[192,384]{1,0:T(8,128)(2,1)S(1)}, bf16[1024,384]{1,0:T(8,128)(2,1)S(1...) custom-call(s32[1,2]{1,0:T(1,128)S(1)} %copy-done.32, s32[1,2]{1,0:T(1,128)S(1)} %copy-done.31, ...), custom_call_target="tpu_custom_call" | custom-call | flops 35000000512 | bytes 1000 | tf_op jit(solution)/shard_map/cross_backward/pallas_call | solution.py:812
  28.8 0.6 collective-permute-start.4
  29.4 1.6 %collective-permute-done.4.refs_2_ = f32[192,768]{1,0:T(8,128)S(1)} collective-permute-done((f32[192,768]{1,0:T(8,128)S(1)}, f32[192,768]{1,0:T(8,128)S(1)}, u32[]{:S(2)}, u32[]{:S(2)}) %collective-permute-start.4) | collective-permute-done | bytes 589856 | tf_op jit(solution)/shard_map/ppermute | solution.py:833
  31.1 0.4 self_grad.1
  31.5 1.0 collective-permute-start.8
  33.2 5.3 %back_all.1 = (bf16[192,1152]{1,0:T(8,128)(2,1)S(1)}, f32[8,32]{1,0:T(8,128)S(1)}, f32[1408,768]{1,0:T(8,128)S(1)}) custom-call(s32[1,2]{1,0:T(1,128)S(1)} %copy-done.32, bf16[192,768]{1,0:T(8,128)(2,1)S(1)} %get-tuple-element.111.refs_1_.refs_15_.refs_2_, f32[6,32]{1,0:T(8,128)S(1)} %bitcast.6, bf16[384,768]{1,0:T(8,128)(2,1)S(1)} %copy-done.17, ...), custom_call_target="tpu_custom_call" | custom-call | flops 35000000512 | bytes 1000 | tf_op jit(solution)/shard_map/back_all/pallas_call | solution.py:812
  38.5 0.4 collective-permute-start.6
  39.0 1.2 collect.1
  40.2 0.7 collective-permute-start.10
  40.9 1.3 %collective-permute-start.11 = (f32[384,768]{1,0:T(8,128)}, f32[384,768]{1,0:T(8,128)}, u32[]{:S(2)}, u32[]{:S(2)}) collective-permute-start(f32[384,768]{1,0:T(8,128)} %get-tuple-element.129), channel_id=1, source_target_pairs={{0,16},{1,9},{2,18},{3,11},{4,20},{5,13},{6,22},{7,15},{8,24},{9,1... | collective-permute-start | bytes 3538952 | tf_op jit(solution)/shard_map/ppermute | solution.py:843
  42.2 3.1 %cross_weights.1.refs_4_ = f32[576,768]{1,0:T(8,128)} custom-call(bf16[2,512,768]{2,1,0:T(8,128)(2,1)S(1)} %copy-done.5, bf16[1024,384]{1,0:T(8,128)(2,1)S(1)} %get-tuple-element.114.refs_9_.refs_1_, bf16[1024,384]{1,0:T(8,128)(2,1)S(1)} %get-tuple-element.115.refs_10_.refs_2_, bf16[192,384]{1,0:T(8,128)(2,1)S(1)} %get-tuple-element.126.refs_3_.refs_4_, ...), custom_call_target="tpu_custom_call" | custom-call | flops 35000000512 | bytes 1000 | tf_op jit(solution)/shard_map/cross_weights/pallas_call | solution.py:812
  45.4 1.2 %collective-permute-start.13 = (f32[576,768]{1,0:T(8,128)}, f32[576,768]{1,0:T(8,128)}, u32[]{:S(2)}, u32[]{:S(2)}) collective-permute-start(f32[576,768]{1,0:T(8,128)} %cross_weights.1.refs_4_), channel_id=1, source_target_pairs={{0,2},{1,5},{2,0},{3,7},{4,6},{5,1},{6,4},{7,3},{8,10},{9,13},{10,... | collective-permute-start | bytes 5308424 | tf_op jit(solution)/shard_map/ppermute | solution.py:843
  46.6 2.7 %collective-permute-done.10.refs_3_ = f32[192,768]{1,0:T(8,128)S(1)} collective-permute-done((f32[192,768]{1,0:T(8,128)S(1)}, f32[192,768]{1,0:T(8,128)S(1)}, u32[]{:S(2)}, u32[]{:S(2)}) %collective-permute-start.10) | collective-permute-done | bytes 589856 | tf_op jit(solution)/shard_map/ppermute | solution.py:843
  49.4 2.4 %collective-permute-start.12 = (f32[600,768]{1,0:T(8,128)S(1)}, f32[600,768]{1,0:T(8,128)S(1)}, u32[]{:S(2)}, u32[]{:S(2)}) collective-permute-start(f32[600,768]{1,0:T(8,128)S(1)} %gather_self.1.refs_0_.refs_4_), channel_id=1, source_target_pairs={{0,1},{1,0},{2,3},{3,2},{4,5},{5,4},{6,7},{7,6},{8,9},{9,8},{10,11... | collective-permute-start | bytes 5529608 | tf_op jit(solution)/shard_map/ppermute | solution.py:833
  51.9 0.4 finish_self_norm.1
  52.3 0.6 collective-permute-start.14
  53.0 2.3 %collective-permute-done.12.refs_5_ = f32[600,768]{1,0:T(8,128)S(1)} collective-permute-done((f32[600,768]{1,0:T(8,128)S(1)}, f32[600,768]{1,0:T(8,128)S(1)}, u32[]{:S(2)}, u32[]{:S(2)}) %collective-permute-start.12) | collective-permute-done | bytes 1843232 | tf_op jit(solution)/shard_map/ppermute | solution.py:833
  55.3 8.8 %self_group.1 = (f32[96,1536]{1,0:T(8,128)S(1)}, f32[96,1536]{1,0:T(8,128)S(1)}) custom-call(bf16[192,768]{1,0:T(8,128)(2,1)S(1)} %copy-done.47, bf16[192,1152]{1,0:T(8,128)(2,1)S(1)} %get-tuple-element.130.refs_1_, bf16[192,768]{1,0:T(8,128)(2,1)S(1)} %copy-done.49, bf16[192,384]{1,0:T(8,128)(2,1)S(1)} %get-tuple-element.131.refs_3_, ...), custom_call_target="tpu_custom_call" | custom-call | flops 35000000512 | bytes 1000 | tf_op jit(solution)/shard_map/self_group/pallas_call | solution.py:812
  64.1 1.6 %cross_keep.1.refs_0_.refs_9_ = f32[384,768]{1,0:T(8,128)S(1)} custom-call(bf16[2,512,768]{2,1,0:T(8,128)(2,1)S(1)} %copy-done.5, bf16[1024,384]{1,0:T(8,128)(2,1)S(1)} %get-tuple-element.114.refs_9_.refs_1_, bf16[1024,384]{1,0:T(8,128)(2,1)S(1)} %get-tuple-element.115.refs_10_.refs_2_, f32[96,1536]{1,0:T(8,128)S(1)} %get-tuple-element.133.refs_3_), custom_call_target="tpu_custom_call" | custom-call | flops 35000000512 | bytes 1000 | tf_op jit(solution)/shard_map/cross_keep/pallas_call | solution.py:812
  65.7 3.9 %collective-permute-start.15 = (f32[96,1536]{1,0:T(8,128)S(1)}, f32[96,1536]{1,0:T(8,128)S(1)}, u32[]{:S(2)}, u32[]{:S(2)}) collective-permute-start(f32[96,1536]{1,0:T(8,128)S(1)} %get-tuple-element.133.refs_3_), channel_id=1, source_target_pairs={{0,8},{1,17},{2,10},{3,19},{4,12},{5,21},{6,14},{7,23},{8,0},{9,25... | collective-permute-start | bytes 1769480 | tf_op jit(solution)/shard_map/ppermute | solution.py:843
  69.7 2.9 %cross_fold.1 = (f32[200,1536]{1,0:T(8,128)S(1)}, f32[192,1536]{1,0:T(8,128)S(1)}, f32[16,384]{1,0:T(8,128)S(1)}) custom-call(f32[384,768]{1,0:T(8,128)S(1)} %cross_keep.1.refs_0_.refs_9_, f32[576,768]{1,0:T(8,128)} %collective-permute-done.13.refs_1_, f32[192,768]{1,0:T(8,128)S(1)} %copy-done.20, bf16[384,192]{1,0:T(8,128)(2,1)S(1)} %get-tuple-element.134.refs_3_, ...), custom_call_target="tpu_custom_call" | custom-call | flops 35000000512 | bytes 1000 | tf_op jit(solution)/shard_map/cross_fold/pallas_call | solution.py:812
  72.6 0.4 collective-permute-start.18
  72.9 1.4 %gather_ffn.1.refs_5_.refs_4_ = f32[576,768]{1,0:T(8,128)S(1)} custom-call(f32[192,768]{1,0:T(8,128)S(1)} %copy-done.22, f32[384,768]{1,0:T(8,128)} %collective-permute-done.11.refs_1_, f32[200,1536]{1,0:T(8,128)S(1)} %get-tuple-element.135.refs_2_), custom_call_target="tpu_custom_call" | custom-call | flops 35000000512 | bytes 1000 | tf_op jit(solution)/shard_map/gather_ffn/pallas_call | solution.py:812
  74.3 1.1 collective-permute-start.16
  75.4 2.0 %finish_outputs.1 = (bf16[2,128,768]{2,1,0:T(8,128)(2,1)}, bf16[2,128,768]{2,1,0:T(8,128)(2,1)}, bf16[2,512,768]{2,1,0:T(8,128)(2,1)}, f32[8,128]{1,0:T(8,128)S(1)}) custom-call(s32[1,2]{1,0:T(1,128)S(1)} %copy-done.33, bf16[192,768]{1,0:T(8,128)(2,1)S(1)} %get-tuple-element.128.refs_1_, f32[1408,768]{1,0:T(8,128)S(1)} %get-tuple-element.117.refs_4_.refs_1_.refs_2_, ...), custom_call_target="tpu_custom_call" | custom-call | flops 35000000512 | bytes 1000 | tf_op jit(solution)/shard_map/finish_outputs/pallas_call | solution.py:812
  77.5 1.2 %collective-permute-done.16.refs_5_ = f32[576,768]{1,0:T(8,128)S(1)} collective-permute-done((f32[576,768]{1,0:T(8,128)S(1)}, f32[576,768]{1,0:T(8,128)S(1)}, u32[]{:S(2)}, u32[]{:S(2)}) %collective-permute-start.16) | collective-permute-done | bytes 1769504 | tf_op jit(solution)/shard_map/ppermute | solution.py:833
  78.9 6.3 %ffn_group.1 = (f32[96,3072]{1,0:T(8,128)S(1)}, f32[96,3072]{1,0:T(8,128)S(1)}) custom-call(bf16[192,768]{1,0:T(8,128)(2,1)S(1)} %copy-done.45, bf16[192,768]{1,0:T(8,128)(2,1)S(1)} %copy-done.44, bf16[192,1536]{1,0:T(8,128)(2,1)S(1)} %copy-done.40, bf16[192,1536]{1,0:T(8,128)(2,1)S(1)} %get-tuple-element.141.refs_3_, ...), custom_call_target="tpu_custom_call" | custom-call | flops 35000000512 | bytes 1000 | tf_op jit(solution)/shard_map/ffn_group/pallas_call | solution.py:812
  85.3 0.6 collective-permute-start.17
  85.9 2.6 %collective-permute-done.18.refs_2_.refs_1_ = f32[200,1536]{1,0:T(8,128)S(1)} collective-permute-done((f32[200,1536]{1,0:T(8,128)S(1)}, f32[200,1536]{1,0:T(8,128)S(1)}, u32[]{:S(2)}, u32[]{:S(2)}) %collective-permute-start.18) | collective-permute-done | bytes 1228832 | tf_op jit(solution)/shard_map/ppermute | solution.py:843
  88.7 1.7 %collective-permute-start.19 = (f32[104,1536]{1,0:T(8,128)S(1)}, f32[104,1536]{1,0:T(8,128)S(1)}, u32[]{:S(2)}, u32[]{:S(2)}) collective-permute-start(f32[104,1536]{1,0:T(8,128)S(1)} %get-tuple-element.146.refs_1_), channel_id=1, source_target_pairs={{0,8},{1,17},{2,10},{3,19},{4,12},{5,21},{6,14},{7,23},{8,0},{9,25... | collective-permute-start | bytes 1916936 | tf_op jit(solution)/shard_map/ppermute | solution.py:843
  90.6 3.0 %collective-permute-done.17.refs_2_ = f32[48,1536]{1,0:T(8,128)S(1)} collective-permute-done((f32[48,1536]{1,0:T(8,128)S(1)}, f32[48,1536]{1,0:T(8,128)S(1)}, u32[]{:S(2)}, u32[]{:S(2)}) %collective-permute-start.17) | collective-permute-done | bytes 294944 | tf_op jit(solution)/shard_map/ppermute | solution.py:843
  93.7 0.7 finish_self.1
  94.4 11.3 %collective-permute-done.20.refs_1_ = f32[96,3072]{1,0:T(8,128)S(1)} collective-permute-done((f32[96,3072]{1,0:T(8,128)S(1)}, f32[96,3072]{1,0:T(8,128)S(1)}, u32[]{:S(2)}, u32[]{:S(2)}) %collective-permute-start.20) | collective-permute-done | bytes 1179680 | tf_op jit(solution)/shard_map/ppermute | solution.py:843
  106.1 3.3 %collective-permute-done.19.refs_3_.refs_2_ = f32[104,1536]{1,0:T(8,128)S(1)} collective-permute-done((f32[104,1536]{1,0:T(8,128)S(1)}, f32[104,1536]{1,0:T(8,128)S(1)}, u32[]{:S(2)}, u32[]{:S(2)}) %collective-permute-start.19) | collective-permute-done | bytes 639008 | tf_op jit(solution)/shard_map/ppermute | solution.py:843
  109.5 5.4 %collective-permute-done.22.refs_2_ = f32[48,3072]{1,0:T(8,128)S(1)} collective-permute-done((f32[48,3072]{1,0:T(8,128)S(1)}, f32[48,3072]{1,0:T(8,128)S(1)}, u32[]{:S(2)}, u32[]{:S(2)}) %collective-permute-start.22) | collective-permute-done | bytes 589856 | tf_op jit(solution)/shard_map/ppermute | solution.py:843
  114.9 0.9 finish_ffn.1
  115.8 3.1 %collective-permute-done.21.refs_4_ = f32[56,1536]{1,0:T(8,128)S(1)} collective-permute-done((f32[56,1536]{1,0:T(8,128)S(1)}, f32[56,1536]{1,0:T(8,128)S(1)}, u32[]{:S(2)}, u32[]{:S(2)}) %collective-permute-start.21) | collective-permute-done | bytes 344096 | tf_op jit(solution)/shard_map/ppermute | solution.py:843
  119.0 0.8 finish_cross.1
  (142 shorter events, 3.2 us)
Async XLA Ops:
  0.7 7.7 %copy-start.4 = (bf16[2,512,768]{2,1,0:T(8,128)(2,1)S(1)}, bf16[2,512,768]{2,1,0:T(8,128)(2,1)}, u32[]{:S(2)}) copy-start(bf16[2,512,768]{2,1,0:T(8,128)(2,1)} %refs_0_.14) | copy-start | bytes 4718596
  0.7 7.7 %copy-start.8 = (bf16[768,384]{1,0:T(8,128)(2,1)S(1)}, bf16[768,384]{1,0:T(8,128)(2,1)}, u32[]{:S(2)}) copy-start(bf16[768,384]{1,0:T(8,128)(2,1)} %refs_11_.2) | copy-start | bytes 1769476
  0.7 7.7 %copy-start.10 = (bf16[768,384]{1,0:T(8,128)(2,1)S(1)}, bf16[768,384]{1,0:T(8,128)(2,1)}, u32[]{:S(2)}) copy-start(bf16[768,384]{1,0:T(8,128)(2,1)} %refs_12_.1) | copy-start | bytes 1769476
  5.2 12.4 %collective-permute-start.2 = (f32[104,768]{1,0:T(8,128)}, f32[104,768]{1,0:T(8,128)S(1)}, u32[]{:S(2)}, u32[]{:S(2)}) collective-permute-start(f32[104,768]{1,0:T(8,128)} %get-tuple-element.99.refs_7_), channel_id=1, source_target_pairs={{0,2},{1,5},{2,0},{3,7},{4,6},{5,1},{6,4},{7,3},{8,10},{9,13},{10,... | collective-permute-start | bytes 958472 | tf_op jit(solution)/shard_map/ppermute | solution.py:843
  7.4 4.2 %copy-start.6 = (bf16[768,384]{1,0:T(8,128)(2,1)S(1)}, bf16[768,384]{1,0:T(8,128)(2,1)}, u32[]{:S(2)}) copy-start(bf16[768,384]{1,0:T(8,128)(2,1)} %refs_8_.4) | copy-start | bytes 1769476
  7.4 4.2 %copy-start.7 = (bf16[384,768]{1,0:T(8,128)(2,1)S(1)}, bf16[384,768]{1,0:T(8,128)(2,1)}, u32[]{:S(2)}) copy-start(bf16[384,768]{1,0:T(8,128)(2,1)} %refs_7_.4) | copy-start | bytes 1769476
  7.4 4.2 %copy-start.27 = (f32[768]{0:T(1024)S(1)}, f32[768]{0:T(1024)}, u32[]{:S(2)}) copy-start(f32[768]{0:T(1024)} %refs_3_.7) | copy-start | bytes 9220
  7.4 4.2 %copy-start.31 = (s32[1,2]{1,0:T(1,128)S(1)}, s32[1,2]{1,0:T(1,128)}, u32[]{:S(2)}) copy-start(s32[1,2]{1,0:T(1,128)} %refs_1_.9) | copy-start | bytes 28
  7.4 4.2 %copy-start.32 = (s32[1,2]{1,0:T(1,128)S(1)}, s32[1,2]{1,0:T(1,128)}, u32[]{:S(2)}) copy-start(s32[1,2]{1,0:T(1,128)} %refs_0_.15) | copy-start | bytes 28
  7.4 4.2 %copy-start.46 = (bf16[192,768]{1,0:T(8,128)(2,1)S(1)}, bf16[192,768]{1,0:T(8,128)(2,1)}, u32[]{:S(2)}) copy-start(bf16[192,768]{1,0:T(8,128)(2,1)} %get-tuple-element.92.refs_2_.refs_0_) | copy-start | bytes 884740
  7.4 4.2 %collective-permute-start = (f32[192,768]{1,0:T(8,128)S(1)}, f32[192,768]{1,0:T(8,128)S(1)}, u32[]{:S(2)}, u32[]{:S(2)}) collective-permute-start(f32[192,768]{1,0:T(8,128)S(1)} %get-tuple-element.93.refs_3_), channel_id=1, source_target_pairs={{0,1},{1,0},{2,3},{3,2},{4,5},{5,4},{6,7},{7,6},{8,9},{9,8},{10,11... | collective-permute-start | bytes 1769480 | tf_op jit(solution)/shard_map/ppermute | solution.py:833
  15.5 2.1 %collective-permute-start.1 = (f32[192,768]{1,0:T(8,128)S(1)}, f32[192,768]{1,0:T(8,128)S(1)}, u32[]{:S(2)}, u32[]{:S(2)}) collective-permute-start(f32[192,768]{1,0:T(8,128)S(1)} %get-tuple-element.97.refs_3_.refs_1_), channel_id=1, source_target_pairs={{0,1},{1,0},{2,3},{3,2},{4,5},{5,4},{6,7},{7,6},{8,9},{9,8},{10,11... | collective-permute-start | bytes 1769480 | tf_op jit(solution)/shard_map/ppermute | solution.py:833
  16.3 13.0 %collective-permute-start.5 = (f32[192,768]{1,0:T(8,128)S(1)}, f32[192,768]{1,0:T(8,128)S(1)}, u32[]{:S(2)}, u32[]{:S(2)}) collective-permute-start(f32[192,768]{1,0:T(8,128)S(1)} %get-tuple-element.101.refs_9_), channel_id=1, source_target_pairs={{0,2},{1,5},{2,0},{3,7},{4,6},{5,1},{6,4},{7,3},{8,10},{9,13},{10,... | collective-permute-start | bytes 1769480 | tf_op jit(solution)/shard_map/ppermute | solution.py:843
  20.6 3.4 %copy-start.37 = (f32[192,768]{1,0:T(8,128)}, f32[192,768]{1,0:T(8,128)S(1)}, u32[]{:S(2)}) copy-start(f32[192,768]{1,0:T(8,128)S(1)} %get-tuple-element.102.refs_2_.refs_4_) | copy-start | bytes 1769476
  20.6 11.8 %copy-start.39 = (bf16[192,1536]{1,0:T(8,128)(2,1)}, bf16[192,1536]{1,0:T(8,128)(2,1)S(1)}, u32[]{:S(2)}) copy-start(bf16[192,1536]{1,0:T(8,128)(2,1)S(1)} %get-tuple-element.116.refs_13_.refs_2_) | copy-start | bytes 1769476
  20.6 3.4 %copy-start.34 = (bf16[1024,384]{1,0:T(8,128)(2,1)S(1)}, bf16[1024,384]{1,0:T(8,128)(2,1)}, u32[]{:S(2)}) copy-start(bf16[1024,384]{1,0:T(8,128)(2,1)} %get-tuple-element.105.refs_10_) | copy-start | bytes 2359300
  20.6 3.3 %collective-permute-start.3 = (f32[192,768]{1,0:T(8,128)S(1)}, f32[192,768]{1,0:T(8,128)S(1)}, u32[]{:S(2)}, u32[]{:S(2)}) collective-permute-start(f32[192,768]{1,0:T(8,128)S(1)} %get-tuple-element.103.refs_0_.refs_3_), channel_id=1, source_target_pairs={{0,1},{1,0},{2,3},{3,2},{4,5},{5,4},{6,7},{7,6},{8,9},{9,8},{10,11... | collective-permute-start | bytes 1769480 | tf_op jit(solution)/shard_map/ppermute | solution.py:833
  21.3 17.7 %collective-permute-start.9 = (f32[192,768]{1,0:T(8,128)S(1)}, f32[192,768]{1,0:T(8,128)S(1)}, u32[]{:S(2)}, u32[]{:S(2)}) collective-permute-start(f32[192,768]{1,0:T(8,128)S(1)} %get-tuple-element.124.refs_2_), channel_id=1, source_target_pairs={{0,8},{1,17},{2,10},{3,19},{4,12},{5,21},{6,14},{7,23},{8,0},{9,25... | collective-permute-start | bytes 1769480 | tf_op jit(solution)/shard_map/ppermute | solution.py:843
  23.6 15.4 %collective-permute-start.7 = (f32[208,768]{1,0:T(8,128)S(1)}, f32[208,768]{1,0:T(8,128)S(1)}, u32[]{:S(2)}, u32[]{:S(2)}) collective-permute-start(f32[208,768]{1,0:T(8,128)S(1)} %get-tuple-element.122), channel_id=1, source_target_pairs={{0,4},{1,3},{2,6},{3,1},{4,0},{5,7},{6,2},{7,5},{8,12},{9,11},{10,... | collective-permute-start | bytes 1916936 | tf_op jit(solution)/shard_map/ppermute | solution.py:843
  28.8 13.4 %copy-start.50 = (bf16[192,768]{1,0:T(8,128)(2,1)}, bf16[192,768]{1,0:T(8,128)(2,1)S(1)}, u32[]{:S(2)}) copy-start(bf16[192,768]{1,0:T(8,128)(2,1)S(1)} %get-tuple-element.127.refs_4_.refs_5_) | copy-start | bytes 884740
  28.8 13.4 %copy-start.52 = (bf16[192,384]{1,0:T(8,128)(2,1)}, bf16[192,384]{1,0:T(8,128)(2,1)S(1)}, u32[]{:S(2)}) copy-start(bf16[192,384]{1,0:T(8,128)(2,1)S(1)} %get-tuple-element.126.refs_3_.refs_4_) | copy-start | bytes 442372
  28.8 2.2 %collective-permute-start.4 = (f32[192,768]{1,0:T(8,128)S(1)}, f32[192,768]{1,0:T(8,128)S(1)}, u32[]{:S(2)}, u32[]{:S(2)}) collective-permute-start(f32[192,768]{1,0:T(8,128)S(1)} %get-tuple-element.109.refs_0_.refs_1_), channel_id=1, source_target_pairs={{0,1},{1,0},{2,3},{3,2},{4,5},{5,4},{6,7},{7,6},{8,9},{9,8},{10,11... | collective-permute-start | bytes 1769480 | tf_op jit(solution)/shard_map/ppermute | solution.py:833
  31.4 7.0 %copy-start.48 = (bf16[192,768]{1,0:T(8,128)(2,1)}, bf16[192,768]{1,0:T(8,128)(2,1)S(1)}, u32[]{:S(2)}) copy-start(bf16[192,768]{1,0:T(8,128)(2,1)S(1)} %get-tuple-element.111.refs_1_.refs_15_.refs_2_) | copy-start | bytes 884740
  31.5 7.5 %collective-permute-start.8 = (f32[96,768]{1,0:T(8,128)S(1)}, f32[96,768]{1,0:T(8,128)S(1)}, u32[]{:S(2)}, u32[]{:S(2)}) collective-permute-start(f32[96,768]{1,0:T(8,128)S(1)} %get-tuple-element.123.refs_0_), channel_id=1, source_target_pairs={{0,2},{1,5},{2,0},{3,7},{4,6},{5,1},{6,4},{7,3},{8,10},{9,13},{10,... | collective-permute-start | bytes 884744 | tf_op jit(solution)/shard_map/ppermute | solution.py:843
  38.5 3.7 %copy-start.5 = (bf16[2,512,768]{2,1,0:T(8,128)(2,1)S(1)}, bf16[2,512,768]{2,1,0:T(8,128)(2,1)}, u32[]{:S(2)}) copy-start(bf16[2,512,768]{2,1,0:T(8,128)(2,1)} %refs_0_.14) | copy-start | bytes 4718596
  38.5 13.3 %collective-permute-start.6 = (f32[1408,768]{1,0:T(8,128)S(1)}, f32[1408,768]{1,0:T(8,128)S(1)}, u32[]{:S(2)}, u32[]{:S(2)}) collective-permute-start(f32[1408,768]{1,0:T(8,128)S(1)} %get-tuple-element.117.refs_4_.refs_1_.refs_2_), channel_id=1, source_target_pairs={{0,1},{1,0},{2,3},{3,2},{4,5},{5,4},{6,7},{7,6},{8,9},{9,8},{10,11... | collective-permute-start | bytes 12976136 | tf_op jit(solution)/shard_map/ppermute | solution.py:833
  40.2 9.1 %collective-permute-start.10 = (f32[192,768]{1,0:T(8,128)S(1)}, f32[192,768]{1,0:T(8,128)S(1)}, u32[]{:S(2)}, u32[]{:S(2)}) collective-permute-start(f32[192,768]{1,0:T(8,128)S(1)} %get-tuple-element.125.refs_5_), channel_id=1, source_target_pairs={{0,4},{1,3},{2,6},{3,1},{4,0},{5,7},{6,2},{7,5},{8,12},{9,11},{10,... | collective-permute-start | bytes 1769480 | tf_op jit(solution)/shard_map/ppermute | solution.py:843
  40.9 32.0 %collective-permute-start.11 = (f32[384,768]{1,0:T(8,128)}, f32[384,768]{1,0:T(8,128)}, u32[]{:S(2)}, u32[]{:S(2)}) collective-permute-start(f32[384,768]{1,0:T(8,128)} %get-tuple-element.129), channel_id=1, source_target_pairs={{0,16},{1,9},{2,18},{3,11},{4,20},{5,13},{6,22},{7,15},{8,24},{9,1... | collective-permute-start | bytes 3538952 | tf_op jit(solution)/shard_map/ppermute | solution.py:843
  42.2 7.1 %copy-start.24 = (f32[104,768]{1,0:T(8,128)S(1)}, f32[104,768]{1,0:T(8,128)}, u32[]{:S(2)}) copy-start(f32[104,768]{1,0:T(8,128)} %copy-done.23) | copy-start | bytes 958468
  45.4 24.3 %collective-permute-start.13 = (f32[576,768]{1,0:T(8,128)}, f32[576,768]{1,0:T(8,128)}, u32[]{:S(2)}, u32[]{:S(2)}) collective-permute-start(f32[576,768]{1,0:T(8,128)} %cross_weights.1.refs_4_), channel_id=1, source_target_pairs={{0,2},{1,5},{2,0},{3,7},{4,6},{5,1},{6,4},{7,3},{8,10},{9,13},{10,... | collective-permute-start | bytes 5308424 | tf_op jit(solution)/shard_map/ppermute | solution.py:843
  49.4 5.8 %collective-permute-start.12 = (f32[600,768]{1,0:T(8,128)S(1)}, f32[600,768]{1,0:T(8,128)S(1)}, u32[]{:S(2)}, u32[]{:S(2)}) collective-permute-start(f32[600,768]{1,0:T(8,128)S(1)} %gather_self.1.refs_0_.refs_4_), channel_id=1, source_target_pairs={{0,1},{1,0},{2,3},{3,2},{4,5},{5,4},{6,7},{7,6},{8,9},{9,8},{10,11... | collective-permute-start | bytes 5529608 | tf_op jit(solution)/shard_map/ppermute | solution.py:833
  51.9 3.4 %copy-start.14 = (bf16[768,384]{1,0:T(8,128)(2,1)S(1)}, bf16[768,384]{1,0:T(8,128)(2,1)}, u32[]{:S(2)}) copy-start(bf16[768,384]{1,0:T(8,128)(2,1)} %refs_9_.1) | copy-start | bytes 1769476
  51.9 3.4 %copy-start.16 = (bf16[768,384]{1,0:T(8,128)(2,1)S(1)}, bf16[768,384]{1,0:T(8,128)(2,1)}, u32[]{:S(2)}) copy-start(bf16[768,384]{1,0:T(8,128)(2,1)} %refs_10_.1) | copy-start | bytes 1769476
  51.9 3.4 %copy-start.18 = (bf16[384,768]{1,0:T(8,128)(2,1)S(1)}, bf16[384,768]{1,0:T(8,128)(2,1)}, u32[]{:S(2)}) copy-start(bf16[384,768]{1,0:T(8,128)(2,1)} %refs_11_.3) | copy-start | bytes 1769476
  52.3 17.3 %collective-permute-start.14 = (f32[8,384]{1,0:T(8,128)S(1)}, f32[8,384]{1,0:T(8,128)S(1)}, u32[]{:S(2)}, u32[]{:S(2)}) collective-permute-start(f32[8,384]{1,0:T(8,128)S(1)} %get-tuple-element.132.refs_12_.refs_7_), channel_id=1, source_target_pairs={{0,2},{1,5},{2,0},{3,7},{4,6},{5,1},{6,4},{7,3},{8,10},{9,13},{10,... | collective-permute-start | bytes 36872 | tf_op jit(solution)/shard_map/ppermute | solution.py:843
  64.1 5.6 %copy-start.20 = (f32[192,768]{1,0:T(8,128)S(1)}, f32[192,768]{1,0:T(8,128)}, u32[]{:S(2)}) copy-start(f32[192,768]{1,0:T(8,128)} %copy-done.19) | copy-start | bytes 1769476
  64.1 5.6 %copy-start.51 = (bf16[192,768]{1,0:T(8,128)(2,1)S(1)}, bf16[192,768]{1,0:T(8,128)(2,1)}, u32[]{:S(2)}) copy-start(bf16[192,768]{1,0:T(8,128)(2,1)} %copy-done.50) | copy-start | bytes 884740
  64.1 5.6 %copy-start.53 = (bf16[192,384]{1,0:T(8,128)(2,1)S(1)}, bf16[192,384]{1,0:T(8,128)(2,1)}, u32[]{:S(2)}) copy-start(bf16[192,384]{1,0:T(8,128)(2,1)} %copy-done.52) | copy-start | bytes 442372
  64.1 5.6 %copy-start.56 = (bf16[192,384]{1,0:T(8,128)(2,1)S(1)}, bf16[192,384]{1,0:T(8,128)(2,1)}, u32[]{:S(2)}) copy-start(bf16[192,384]{1,0:T(8,128)(2,1)} %copy-done.55) | copy-start | bytes 442372
  65.7 19.5 %collective-permute-start.15 = (f32[96,1536]{1,0:T(8,128)S(1)}, f32[96,1536]{1,0:T(8,128)S(1)}, u32[]{:S(2)}, u32[]{:S(2)}) collective-permute-start(f32[96,1536]{1,0:T(8,128)S(1)} %get-tuple-element.133.refs_3_), channel_id=1, source_target_pairs={{0,8},{1,17},{2,10},{3,19},{4,12},{5,21},{6,14},{7,23},{8,0},{9,25... | collective-permute-start | bytes 1769480 | tf_op jit(solution)/shard_map/ppermute | solution.py:843
  72.6 15.9 %collective-permute-start.18 = (f32[200,1536]{1,0:T(8,128)S(1)}, f32[200,1536]{1,0:T(8,128)S(1)}, u32[]{:S(2)}, u32[]{:S(2)}) collective-permute-start(f32[200,1536]{1,0:T(8,128)S(1)} %get-tuple-element.135.refs_2_), channel_id=1, source_target_pairs={{0,4},{1,3},{2,6},{3,1},{4,0},{5,7},{6,2},{7,5},{8,12},{9,11},{10,... | collective-permute-start | bytes 3686408 | tf_op jit(solution)/shard_map/ppermute | solution.py:843
  74.3 4.4 %collective-permute-start.16 = (f32[576,768]{1,0:T(8,128)S(1)}, f32[576,768]{1,0:T(8,128)S(1)}, u32[]{:S(2)}, u32[]{:S(2)}) collective-permute-start(f32[576,768]{1,0:T(8,128)S(1)} %gather_ffn.1.refs_5_.refs_4_), channel_id=1, source_target_pairs={{0,1},{1,0},{2,3},{3,2},{4,5},{5,4},{6,7},{7,6},{8,9},{9,8},{10,11... | collective-permute-start | bytes 5308424 | tf_op jit(solution)/shard_map/ppermute | solution.py:833
  75.4 3.5 %copy-start.45 = (bf16[192,768]{1,0:T(8,128)(2,1)S(1)}, bf16[192,768]{1,0:T(8,128)(2,1)}, u32[]{:S(2)}) copy-start(bf16[192,768]{1,0:T(8,128)(2,1)} %get-tuple-element.140.refs_0_) | copy-start | bytes 884740
  85.3 8.4 %collective-permute-start.17 = (f32[48,1536]{1,0:T(8,128)S(1)}, f32[48,1536]{1,0:T(8,128)S(1)}, u32[]{:S(2)}, u32[]{:S(2)}) collective-permute-start(f32[48,1536]{1,0:T(8,128)S(1)} %self_fold.1.refs_3_), channel_id=1, source_target_pairs={{0,16},{1,9},{2,18},{3,11},{4,20},{5,13},{6,22},{7,15},{8,24},{9,1... | collective-permute-start | bytes 884744 | tf_op jit(solution)/shard_map/ppermute | solution.py:843
  88.7 20.7 %collective-permute-start.19 = (f32[104,1536]{1,0:T(8,128)S(1)}, f32[104,1536]{1,0:T(8,128)S(1)}, u32[]{:S(2)}, u32[]{:S(2)}) collective-permute-start(f32[104,1536]{1,0:T(8,128)S(1)} %get-tuple-element.146.refs_1_), channel_id=1, source_target_pairs={{0,8},{1,17},{2,10},{3,19},{4,12},{5,21},{6,14},{7,23},{8,0},{9,25... | collective-permute-start | bytes 1916936 | tf_op jit(solution)/shard_map/ppermute | solution.py:843
  90.4 15.3 %collective-permute-start.20 = (f32[96,3072]{1,0:T(8,128)S(1)}, f32[96,3072]{1,0:T(8,128)S(1)}, u32[]{:S(2)}, u32[]{:S(2)}) collective-permute-start(f32[96,3072]{1,0:T(8,128)S(1)} %relay.1.refs_3_), channel_id=1, source_target_pairs={{0,2},{1,5},{2,0},{3,7},{4,6},{5,1},{6,4},{7,3},{8,10},{9,13},{10,... | collective-permute-start | bytes 3538952 | tf_op jit(solution)/shard_map/ppermute | solution.py:843
  105.8 9.1 %collective-permute-start.22 = (f32[48,3072]{1,0:T(8,128)S(1)}, f32[48,3072]{1,0:T(8,128)S(1)}, u32[]{:S(2)}, u32[]{:S(2)}) collective-permute-start(f32[48,3072]{1,0:T(8,128)S(1)} %ffn_fold.1.refs_4_), channel_id=1, source_target_pairs={{0,4},{1,3},{2,6},{3,1},{4,0},{5,7},{6,2},{7,5},{8,12},{9,11},{10,... | collective-permute-start | bytes 1769480 | tf_op jit(solution)/shard_map/ppermute | solution.py:843
  109.4 9.5 %collective-permute-start.21 = (f32[56,1536]{1,0:T(8,128)S(1)}, f32[56,1536]{1,0:T(8,128)S(1)}, u32[]{:S(2)}, u32[]{:S(2)}) collective-permute-start(f32[56,1536]{1,0:T(8,128)S(1)} %get-tuple-element.155.refs_0_), channel_id=1, source_target_pairs={{0,16},{1,9},{2,18},{3,11},{4,20},{5,13},{6,22},{7,15},{8,24},{9,1... | collective-permute-start | bytes 1032200 | tf_op jit(solution)/shard_map/ppermute | solution.py:843
  (32 other events, 79.1 us)

commit v2 on v1

--- a/solution.py
+++ b/solution.py
@@ -527,17 +527,17 @@
     return jnp.concatenate([rows[:, :n], rows[:, n : 2 * n]], 0)
 
 
-def cross_fold(keep, moved, early, own, dq, low, att, small, small_moved, send_out, keep_out, small_out, total):
+def cross_fold(keep, factors, moved, early, own, dq, low, att, small, small_moved, send_out, keep_out, small_out, total):
     width = low.shape[1]
     half, inner = own.shape[0], dq.shape[1]
     rows = width // 16
     total[:, :inner] = nn(own[...], dq[...]) + nn(
-        unfold_lanes(early[:, :inner]).astype(bf16), moved[half:, :inner].astype(bf16)
+        unfold_lanes(early[:, :inner]).astype(bf16), factors[:, :inner].astype(bf16)
     )
     total[:, 3 * inner :] = nn(nt(half_pick(0, width), low[...]).astype(bf16), att[...]) + nn(
-        unfold_lanes(moved[half:, inner:]).astype(bf16), early[:, inner:].astype(bf16)
-    )
-    total[:, inner : 3 * inner] = keep[...] + moved[:half, :]
+        unfold_lanes(factors[:, inner:]).astype(bf16), early[:, inner:].astype(bf16)
+    )
+    total[:, inner : 3 * inner] = keep[...] + moved[...]
     split_entries(1, lambda i: total[pl.ds(pl.multiple_of(i * rows, 8), rows), :], send_out, keep_out, rows)
     stack(small_out, small, small_moved)
     side_by_side(send_out, keep_out.shape[0], small_out)
@@ -1028,7 +1028,7 @@
     send_cross, keep_cross, small_two = call(
         cross_fold,
         [((half // 2 + 8, wide), f32, "v"), ((half // 2, wide), f32, "v"), ((16, half), f32, "v")],
-        [(keep_cross, "v"), (late_cross_moved, "v"), (early_moved, "v"), (own_cross, "v"), (dq, "v"),
+        [(keep_cross, "v"), (late_cross_moved, "a", half, tokens), (late_cross_moved, "a", 0, half), (early_moved, "v"), (own_cross, "v"), (dq, "v"),
          (low_cross, "v"), (att_cross, "v"), (small, "v"), (small_moved, "v")],
         scratch=[((half, wide), f32)],
         after=(keep_cross,),

time: 120 us -> 120 us (level)
  no operation moved by 1% of the time
where the time goes in v2:
time: 120 us
  Pallas kernels  55.3 us (46%)
  waiting for transfers between devices  36.7 us (31%)
  starting transfers between devices  24.3 us (20%)
  local copies, waits for them, and re-layouts  1.65 us (1%)
  between operations  1.56 us (1%)
    pallas_call x30, Pallas kernels, call(): pl.pallas_call(body, out_shape=[pltpu.HBM(shape, kind) if place == 'h' el...  55.3 us
    ppermute x16, waiting for transfers between devices, stage_swap(): return lax.ppermute(values, ('dp', 'mp'), pairs)  31.5 us
    ppermute x16, starting transfers between devices, stage_swap(): return lax.ppermute(values, ('dp', 'mp'), pairs)  18.1 us
    ppermute x7, starting transfers between devices, pair_swap(): return lax.ppermute(values, 'mp', [(0, 1), (1, 0)])  6.2 us
    ppermute x7, waiting for transfers between devices, pair_swap(): return lax.ppermute(values, 'mp', [(0, 1), (1, 0)])  5.18 us
  transfers between devices with their start and end apart: 23, of which 10 were waited for; matrix products, arithmetic and copies ran while one was open for 0% of the time, Pallas kernels for 42%

profile of v2, /device:TPU:1, one launch (start us, length us, event | category | flops | bytes accessed | tf_op | source)
XLA Modules:
  0.0 119.5 jit_solution(7507738360111265986)
XLA Ops:
  0.7 4.5 %self_forward.1 = (bf16[192,768]{1,0:T(8,128)(2,1)}, bf16[192,768]{1,0:T(8,128)(2,1)}, bf16[192,1152]{1,0:T(8,128)(2,1)}, bf16[192,384]{1,0:T(8,128)(2,1)S(1)}, ...) custom-call(s32[1,2]{1,0:T(1,128)} %refs_0_.15, bf16[2,128,768]{2,1,0:T(8,128)(2,1)} %refs_1_.5, ...), custom_call_target="tpu_custom_call" | custom-call | flops 35000000512 | bytes 1000 | tf_op jit(solution)/shard_map/self_forward/pallas_call | solution.py:812
  5.2 2.1 %collective-permute-start.2 = (f32[104,768]{1,0:T(8,128)}, f32[104,768]{1,0:T(8,128)S(1)}, u32[]{:S(2)}, u32[]{:S(2)}) collective-permute-start(f32[104,768]{1,0:T(8,128)} %get-tuple-element.99.refs_7_), channel_id=1, source_target_pairs={{0,2},{1,5},{2,0},{3,7},{4,6},{5,1},{6,4},{7,3},{8,10},{9,13},{10,... | collective-permute-start | bytes 958472 | tf_op jit(solution)/shard_map/ppermute | solution.py:843
  7.4 1.0 collective-permute-start
  8.4 3.1 %encoder_forward.1 = (bf16[1024,384]{1,0:T(8,128)(2,1)S(1)}, bf16[384,1024]{1,0:T(8,128)(2,1)S(1)}, bf16[1024,384]{1,0:T(8,128)(2,1)}, bf16[1024,384]{1,0:T(8,128)(2,1)}, bf16[384,1024]{1,0:T(8,128)(2,1)}) custom-call(bf16[2,512,768]{2,1,0:T(8,128)(2,1)S(1)} %copy-done.4, bf16[768,384]{1,0:T(8,128)(2,1)S(1)} %copy-done.8, bf16[768,384]{1,0:T(8,128)(2,1)S(1)} %copy-done.10, ...), custom_call_target="tpu_custom_call" | custom-call | flops 35000000512 | bytes 1000 | tf_op jit(solution)/shard_map/encoder_forward/pallas_call | solution.py:812
  11.6 3.9 %cross_forward.1 = (f32[192,768]{1,0:T(8,128)S(1)}, bf16[192,384]{1,0:T(8,128)(2,1)}, bf16[192,384]{1,0:T(8,128)(2,1)S(1)}, f32[8,256]{1,0:T(8,128)S(1)}, f32[192,768]{1,0:T(8,128)S(1)}) custom-call(s32[1,2]{1,0:T(1,128)S(1)} %copy-done.32, s32[1,2]{1,0:T(1,128)S(1)} %copy-done.31, bf16[192,768]{1,0:T(8,128)(2,1)S(1)} %copy-done.46, ...), custom_call_target="tpu_custom_call" | custom-call | flops 35000000512 | bytes 1000 | tf_op jit(solution)/shard_map/cross_forward/pallas_call | solution.py:812
  15.6 0.7 pack_early.1
  16.3 1.3 %collective-permute-start.5 = (f32[192,768]{1,0:T(8,128)S(1)}, f32[192,768]{1,0:T(8,128)S(1)}, u32[]{:S(2)}, u32[]{:S(2)}) collective-permute-start(f32[192,768]{1,0:T(8,128)S(1)} %get-tuple-element.101.refs_9_), channel_id=1, source_target_pairs={{0,2},{1,5},{2,0},{3,7},{4,6},{5,1},{6,4},{7,3},{8,10},{9,13},{10,... | collective-permute-start | bytes 1769480 | tf_op jit(solution)/shard_map/ppermute | solution.py:843
  18.1 2.5 %ffn_both.1 = (f32[192,768]{1,0:T(8,128)S(1)}, bf16[192,768]{1,0:T(8,128)(2,1)}, f32[192,768]{1,0:T(8,128)S(1)}, bf16[192,1536]{1,0:T(8,128)(2,1)S(1)}, bf16[192...) custom-call(f32[192,768]{1,0:T(8,128)S(1)} %get-tuple-element.96.refs_0_, ...), custom_call_target="tpu_custom_call" | custom-call | flops 35000000512 | bytes 1000 | tf_op jit(solution)/shard_map/ffn_both/pallas_call | solution.py:812
  20.6 0.7 collective-permute-start.3
  21.3 2.3 %collective-permute-start.9 = (f32[192,768]{1,0:T(8,128)S(1)}, f32[192,768]{1,0:T(8,128)S(1)}, u32[]{:S(2)}, u32[]{:S(2)}) collective-permute-start(f32[192,768]{1,0:T(8,128)S(1)} %get-tuple-element.124.refs_2_), channel_id=1, source_target_pairs={{0,8},{1,17},{2,10},{3,19},{4,12},{5,21},{6,14},{7,23},{8,0},{9,25... | collective-permute-start | bytes 1769480 | tf_op jit(solution)/shard_map/ppermute | solution.py:843
  24.0 4.7 %cross_backward.1 = (f32[192,768]{1,0:T(8,128)}, bf16[192,768]{1,0:T(8,128)(2,1)S(1)}, bf16[192,384]{1,0:T(8,128)(2,1)S(1)}, bf16[1024,384]{1,0:T(8,128)(2,1)S(1...) custom-call(s32[1,2]{1,0:T(1,128)S(1)} %copy-done.32, s32[1,2]{1,0:T(1,128)S(1)} %copy-done.31, ...), custom_call_target="tpu_custom_call" | custom-call | flops 35000000512 | bytes 1000 | tf_op jit(solution)/shard_map/cross_backward/pallas_call | solution.py:812
  28.8 0.6 collective-permute-start.4
  29.4 1.6 %collective-permute-done.4.refs_2_ = f32[192,768]{1,0:T(8,128)S(1)} collective-permute-done((f32[192,768]{1,0:T(8,128)S(1)}, f32[192,768]{1,0:T(8,128)S(1)}, u32[]{:S(2)}, u32[]{:S(2)}) %collective-permute-start.4) | collective-permute-done | bytes 589856 | tf_op jit(solution)/shard_map/ppermute | solution.py:833
  31.1 0.4 self_grad.1
  31.5 1.0 collective-permute-start.8
  33.2 5.3 %back_all.1 = (bf16[192,1152]{1,0:T(8,128)(2,1)S(1)}, f32[8,32]{1,0:T(8,128)S(1)}, f32[1408,768]{1,0:T(8,128)S(1)}) custom-call(s32[1,2]{1,0:T(1,128)S(1)} %copy-done.32, bf16[192,768]{1,0:T(8,128)(2,1)S(1)} %get-tuple-element.111.refs_1_.refs_15_.refs_2_, f32[6,32]{1,0:T(8,128)S(1)} %bitcast.6, bf16[384,768]{1,0:T(8,128)(2,1)S(1)} %copy-done.17, ...), custom_call_target="tpu_custom_call" | custom-call | flops 35000000512 | bytes 1000 | tf_op jit(solution)/shard_map/back_all/pallas_call | solution.py:812
  38.5 0.4 collective-permute-start.6
  39.0 1.2 collect.1
  40.2 0.7 collective-permute-start.10
  40.9 1.3 %collective-permute-start.11 = (f32[384,768]{1,0:T(8,128)}, f32[384,768]{1,0:T(8,128)}, u32[]{:S(2)}, u32[]{:S(2)}) collective-permute-start(f32[384,768]{1,0:T(8,128)} %get-tuple-element.129), channel_id=1, source_target_pairs={{0,16},{1,9},{2,18},{3,11},{4,20},{5,13},{6,22},{7,15},{8,24},{9,1... | collective-permute-start | bytes 3538952 | tf_op jit(solution)/shard_map/ppermute | solution.py:843
  42.2 3.1 %cross_weights.1.refs_4_ = f32[576,768]{1,0:T(8,128)} custom-call(bf16[2,512,768]{2,1,0:T(8,128)(2,1)S(1)} %copy-done.5, bf16[1024,384]{1,0:T(8,128)(2,1)S(1)} %get-tuple-element.114.refs_9_.refs_1_, bf16[1024,384]{1,0:T(8,128)(2,1)S(1)} %get-tuple-element.115.refs_10_.refs_2_, bf16[192,384]{1,0:T(8,128)(2,1)S(1)} %get-tuple-element.126.refs_3_.refs_5_, ...), custom_call_target="tpu_custom_call" | custom-call | flops 35000000512 | bytes 1000 | tf_op jit(solution)/shard_map/cross_weights/pallas_call | solution.py:812
  45.4 1.2 %collective-permute-start.13 = (f32[576,768]{1,0:T(8,128)}, f32[576,768]{1,0:T(8,128)}, u32[]{:S(2)}, u32[]{:S(2)}) collective-permute-start(f32[576,768]{1,0:T(8,128)} %cross_weights.1.refs_4_), channel_id=1, source_target_pairs={{0,2},{1,5},{2,0},{3,7},{4,6},{5,1},{6,4},{7,3},{8,10},{9,13},{10,... | collective-permute-start | bytes 5308424 | tf_op jit(solution)/shard_map/ppermute | solution.py:843
  46.6 2.7 %collective-permute-done.10.refs_3_ = f32[192,768]{1,0:T(8,128)S(1)} collective-permute-done((f32[192,768]{1,0:T(8,128)S(1)}, f32[192,768]{1,0:T(8,128)S(1)}, u32[]{:S(2)}, u32[]{:S(2)}) %collective-permute-start.10) | collective-permute-done | bytes 589856 | tf_op jit(solution)/shard_map/ppermute | solution.py:843
  49.4 2.4 %collective-permute-start.12 = (f32[600,768]{1,0:T(8,128)S(1)}, f32[600,768]{1,0:T(8,128)S(1)}, u32[]{:S(2)}, u32[]{:S(2)}) collective-permute-start(f32[600,768]{1,0:T(8,128)S(1)} %gather_self.1.refs_0_.refs_4_), channel_id=1, source_target_pairs={{0,1},{1,0},{2,3},{3,2},{4,5},{5,4},{6,7},{7,6},{8,9},{9,8},{10,11... | collective-permute-start | bytes 5529608 | tf_op jit(solution)/shard_map/ppermute | solution.py:833
  51.9 0.4 finish_self_norm.1
  52.3 0.6 collective-permute-start.14
  53.0 2.3 %collective-permute-done.12.refs_5_ = f32[600,768]{1,0:T(8,128)S(1)} collective-permute-done((f32[600,768]{1,0:T(8,128)S(1)}, f32[600,768]{1,0:T(8,128)S(1)}, u32[]{:S(2)}, u32[]{:S(2)}) %collective-permute-start.12) | collective-permute-done | bytes 1843232 | tf_op jit(solution)/shard_map/ppermute | solution.py:833
  55.3 8.8 %self_group.1 = (f32[96,1536]{1,0:T(8,128)S(1)}, f32[96,1536]{1,0:T(8,128)S(1)}) custom-call(bf16[192,768]{1,0:T(8,128)(2,1)S(1)} %copy-done.47, bf16[192,1152]{1,0:T(8,128)(2,1)S(1)} %get-tuple-element.130.refs_1_, bf16[192,768]{1,0:T(8,128)(2,1)S(1)} %copy-done.49, bf16[192,384]{1,0:T(8,128)(2,1)S(1)} %get-tuple-element.131.refs_3_, ...), custom_call_target="tpu_custom_call" | custom-call | flops 35000000512 | bytes 1000 | tf_op jit(solution)/shard_map/self_group/pallas_call | solution.py:812
  64.1 1.6 %cross_keep.1.refs_0_.refs_10_ = f32[384,768]{1,0:T(8,128)S(1)} custom-call(bf16[2,512,768]{2,1,0:T(8,128)(2,1)S(1)} %copy-done.5, bf16[1024,384]{1,0:T(8,128)(2,1)S(1)} %get-tuple-element.114.refs_9_.refs_1_, bf16[1024,384]{1,0:T(8,128)(2,1)S(1)} %get-tuple-element.115.refs_10_.refs_2_, f32[96,1536]{1,0:T(8,128)S(1)} %get-tuple-element.133.refs_3_), custom_call_target="tpu_custom_call" | custom-call | flops 35000000512 | bytes 1000 | tf_op jit(solution)/shard_map/cross_keep/pallas_call | solution.py:812
  65.7 3.9 %collective-permute-start.15 = (f32[96,1536]{1,0:T(8,128)S(1)}, f32[96,1536]{1,0:T(8,128)S(1)}, u32[]{:S(2)}, u32[]{:S(2)}) collective-permute-start(f32[96,1536]{1,0:T(8,128)S(1)} %get-tuple-element.133.refs_3_), channel_id=1, source_target_pairs={{0,8},{1,17},{2,10},{3,19},{4,12},{5,21},{6,14},{7,23},{8,0},{9,25... | collective-permute-start | bytes 1769480 | tf_op jit(solution)/shard_map/ppermute | solution.py:843
  69.7 2.4 %cross_fold.1 = (f32[200,1536]{1,0:T(8,128)S(1)}, f32[192,1536]{1,0:T(8,128)S(1)}, f32[16,384]{1,0:T(8,128)S(1)}) custom-call(f32[384,768]{1,0:T(8,128)S(1)} %cross_keep.1.refs_0_.refs_10_, f32[576,768]{1,0:T(8,128)} %collective-permute-done.13.refs_1_.refs_2_, f32[576,768]{1,0:T(8,128)} %collective-permute-done.13.refs_1_.refs_2_, ...), custom_call_target="tpu_custom_call" | custom-call | flops 35000000512 | bytes 1000 | tf_op jit(solution)/shard_map/cross_fold/pallas_call | solution.py:812
  72.1 0.4 collective-permute-start.18
  72.5 1.4 %gather_ffn.1.refs_5_.refs_4_ = f32[576,768]{1,0:T(8,128)S(1)} custom-call(f32[192,768]{1,0:T(8,128)S(1)} %copy-done.22, f32[384,768]{1,0:T(8,128)} %collective-permute-done.11.refs_1_, f32[200,1536]{1,0:T(8,128)S(1)} %get-tuple-element.135.refs_2_), custom_call_target="tpu_custom_call" | custom-call | flops 35000000512 | bytes 1000 | tf_op jit(solution)/shard_map/gather_ffn/pallas_call | solution.py:812
  73.9 1.1 collective-permute-start.16
  75.0 2.0 %finish_outputs.1 = (bf16[2,128,768]{2,1,0:T(8,128)(2,1)}, bf16[2,128,768]{2,1,0:T(8,128)(2,1)}, bf16[2,512,768]{2,1,0:T(8,128)(2,1)}, f32[8,128]{1,0:T(8,128)S(1)}) custom-call(s32[1,2]{1,0:T(1,128)S(1)} %copy-done.33, bf16[192,768]{1,0:T(8,128)(2,1)S(1)} %get-tuple-element.128.refs_1_, f32[1408,768]{1,0:T(8,128)S(1)} %get-tuple-element.117.refs_4_.refs_1_.refs_2_, ...), custom_call_target="tpu_custom_call" | custom-call | flops 35000000512 | bytes 1000 | tf_op jit(solution)/shard_map/finish_outputs/pallas_call | solution.py:812
  77.1 1.2 %collective-permute-done.16.refs_5_ = f32[576,768]{1,0:T(8,128)S(1)} collective-permute-done((f32[576,768]{1,0:T(8,128)S(1)}, f32[576,768]{1,0:T(8,128)S(1)}, u32[]{:S(2)}, u32[]{:S(2)}) %collective-permute-start.16) | collective-permute-done | bytes 1769504 | tf_op jit(solution)/shard_map/ppermute | solution.py:833
  78.5 6.3 %ffn_group.1 = (f32[96,3072]{1,0:T(8,128)S(1)}, f32[96,3072]{1,0:T(8,128)S(1)}) custom-call(bf16[192,768]{1,0:T(8,128)(2,1)S(1)} %copy-done.45, bf16[192,768]{1,0:T(8,128)(2,1)S(1)} %copy-done.44, bf16[192,1536]{1,0:T(8,128)(2,1)S(1)} %copy-done.40, bf16[192,1536]{1,0:T(8,128)(2,1)S(1)} %get-tuple-element.141.refs_3_, ...), custom_call_target="tpu_custom_call" | custom-call | flops 35000000512 | bytes 1000 | tf_op jit(solution)/shard_map/ffn_group/pallas_call | solution.py:812
  84.9 0.6 collective-permute-start.17
  85.5 2.6 %collective-permute-done.18.refs_2_.refs_1_ = f32[200,1536]{1,0:T(8,128)S(1)} collective-permute-done((f32[200,1536]{1,0:T(8,128)S(1)}, f32[200,1536]{1,0:T(8,128)S(1)}, u32[]{:S(2)}, u32[]{:S(2)}) %collective-permute-start.18) | collective-permute-done | bytes 1228832 | tf_op jit(solution)/shard_map/ppermute | solution.py:843
  88.2 1.7 %collective-permute-start.19 = (f32[104,1536]{1,0:T(8,128)S(1)}, f32[104,1536]{1,0:T(8,128)S(1)}, u32[]{:S(2)}, u32[]{:S(2)}) collective-permute-start(f32[104,1536]{1,0:T(8,128)S(1)} %get-tuple-element.146.refs_1_), channel_id=1, source_target_pairs={{0,8},{1,17},{2,10},{3,19},{4,12},{5,21},{6,14},{7,23},{8,0},{9,25... | collective-permute-start | bytes 1916936 | tf_op jit(solution)/shard_map/ppermute | solution.py:843
  90.2 3.0 %collective-permute-done.17.refs_2_ = f32[48,1536]{1,0:T(8,128)S(1)} collective-permute-done((f32[48,1536]{1,0:T(8,128)S(1)}, f32[48,1536]{1,0:T(8,128)S(1)}, u32[]{:S(2)}, u32[]{:S(2)}) %collective-permute-start.17) | collective-permute-done | bytes 294944 | tf_op jit(solution)/shard_map/ppermute | solution.py:843
  93.2 0.7 finish_self.1
  93.9 11.4 %collective-permute-done.20.refs_1_ = f32[96,3072]{1,0:T(8,128)S(1)} collective-permute-done((f32[96,3072]{1,0:T(8,128)S(1)}, f32[96,3072]{1,0:T(8,128)S(1)}, u32[]{:S(2)}, u32[]{:S(2)}) %collective-permute-start.20) | collective-permute-done | bytes 1179680 | tf_op jit(solution)/shard_map/ppermute | solution.py:843
  105.7 3.3 %collective-permute-done.19.refs_3_.refs_2_ = f32[104,1536]{1,0:T(8,128)S(1)} collective-permute-done((f32[104,1536]{1,0:T(8,128)S(1)}, f32[104,1536]{1,0:T(8,128)S(1)}, u32[]{:S(2)}, u32[]{:S(2)}) %collective-permute-start.19) | collective-permute-done | bytes 639008 | tf_op jit(solution)/shard_map/ppermute | solution.py:843
  109.1 5.4 %collective-permute-done.22.refs_2_ = f32[48,3072]{1,0:T(8,128)S(1)} collective-permute-done((f32[48,3072]{1,0:T(8,128)S(1)}, f32[48,3072]{1,0:T(8,128)S(1)}, u32[]{:S(2)}, u32[]{:S(2)}) %collective-permute-start.22) | collective-permute-done | bytes 589856 | tf_op jit(solution)/shard_map/ppermute | solution.py:843
  114.5 0.9 finish_ffn.1
  115.4 3.2 %collective-permute-done.21.refs_4_ = f32[56,1536]{1,0:T(8,128)S(1)} collective-permute-done((f32[56,1536]{1,0:T(8,128)S(1)}, f32[56,1536]{1,0:T(8,128)S(1)}, u32[]{:S(2)}, u32[]{:S(2)}) %collective-permute-start.21) | collective-permute-done | bytes 344096 | tf_op jit(solution)/shard_map/ppermute | solution.py:843
  118.5 0.8 finish_cross.1
  (142 shorter events, 3.2 us)
Async XLA Ops:
  0.7 7.7 %copy-start.4 = (bf16[2,512,768]{2,1,0:T(8,128)(2,1)S(1)}, bf16[2,512,768]{2,1,0:T(8,128)(2,1)}, u32[]{:S(2)}) copy-start(bf16[2,512,768]{2,1,0:T(8,128)(2,1)} %refs_0_.14) | copy-start | bytes 4718596
  0.7 7.7 %copy-start.8 = (bf16[768,384]{1,0:T(8,128)(2,1)S(1)}, bf16[768,384]{1,0:T(8,128)(2,1)}, u32[]{:S(2)}) copy-start(bf16[768,384]{1,0:T(8,128)(2,1)} %refs_11_.2) | copy-start | bytes 1769476
  0.7 7.7 %copy-start.10 = (bf16[768,384]{1,0:T(8,128)(2,1)S(1)}, bf16[768,384]{1,0:T(8,128)(2,1)}, u32[]{:S(2)}) copy-start(bf16[768,384]{1,0:T(8,128)(2,1)} %refs_12_.1) | copy-start | bytes 1769476
  5.2 12.4 %collective-permute-start.2 = (f32[104,768]{1,0:T(8,128)}, f32[104,768]{1,0:T(8,128)S(1)}, u32[]{:S(2)}, u32[]{:S(2)}) collective-permute-start(f32[104,768]{1,0:T(8,128)} %get-tuple-element.99.refs_7_), channel_id=1, source_target_pairs={{0,2},{1,5},{2,0},{3,7},{4,6},{5,1},{6,4},{7,3},{8,10},{9,13},{10,... | collective-permute-start | bytes 958472 | tf_op jit(solution)/shard_map/ppermute | solution.py:843
  7.4 4.2 %copy-start.6 = (bf16[768,384]{1,0:T(8,128)(2,1)S(1)}, bf16[768,384]{1,0:T(8,128)(2,1)}, u32[]{:S(2)}) copy-start(bf16[768,384]{1,0:T(8,128)(2,1)} %refs_8_.4) | copy-start | bytes 1769476
  7.4 4.2 %copy-start.7 = (bf16[384,768]{1,0:T(8,128)(2,1)S(1)}, bf16[384,768]{1,0:T(8,128)(2,1)}, u32[]{:S(2)}) copy-start(bf16[384,768]{1,0:T(8,128)(2,1)} %refs_7_.4) | copy-start | bytes 1769476
  7.4 4.2 %copy-start.27 = (f32[768]{0:T(1024)S(1)}, f32[768]{0:T(1024)}, u32[]{:S(2)}) copy-start(f32[768]{0:T(1024)} %refs_3_.7) | copy-start | bytes 9220
  7.4 4.2 %copy-start.31 = (s32[1,2]{1,0:T(1,128)S(1)}, s32[1,2]{1,0:T(1,128)}, u32[]{:S(2)}) copy-start(s32[1,2]{1,0:T(1,128)} %refs_1_.9) | copy-start | bytes 28
  7.4 4.2 %copy-start.32 = (s32[1,2]{1,0:T(1,128)S(1)}, s32[1,2]{1,0:T(1,128)}, u32[]{:S(2)}) copy-start(s32[1,2]{1,0:T(1,128)} %refs_0_.15) | copy-start | bytes 28
  7.4 4.2 %copy-start.46 = (bf16[192,768]{1,0:T(8,128)(2,1)S(1)}, bf16[192,768]{1,0:T(8,128)(2,1)}, u32[]{:S(2)}) copy-start(bf16[192,768]{1,0:T(8,128)(2,1)} %get-tuple-element.92.refs_2_.refs_0_) | copy-start | bytes 884740
  7.4 4.2 %collective-permute-start = (f32[192,768]{1,0:T(8,128)S(1)}, f32[192,768]{1,0:T(8,128)S(1)}, u32[]{:S(2)}, u32[]{:S(2)}) collective-permute-start(f32[192,768]{1,0:T(8,128)S(1)} %get-tuple-element.93.refs_3_), channel_id=1, source_target_pairs={{0,1},{1,0},{2,3},{3,2},{4,5},{5,4},{6,7},{7,6},{8,9},{9,8},{10,11... | collective-permute-start | bytes 1769480 | tf_op jit(solution)/shard_map/ppermute | solution.py:833
  15.5 2.1 %collective-permute-start.1 = (f32[192,768]{1,0:T(8,128)S(1)}, f32[192,768]{1,0:T(8,128)S(1)}, u32[]{:S(2)}, u32[]{:S(2)}) collective-permute-start(f32[192,768]{1,0:T(8,128)S(1)} %get-tuple-element.97.refs_3_.refs_1_), channel_id=1, source_target_pairs={{0,1},{1,0},{2,3},{3,2},{4,5},{5,4},{6,7},{7,6},{8,9},{9,8},{10,11... | collective-permute-start | bytes 1769480 | tf_op jit(solution)/shard_map/ppermute | solution.py:833
  16.3 13.0 %collective-permute-start.5 = (f32[192,768]{1,0:T(8,128)S(1)}, f32[192,768]{1,0:T(8,128)S(1)}, u32[]{:S(2)}, u32[]{:S(2)}) collective-permute-start(f32[192,768]{1,0:T(8,128)S(1)} %get-tuple-element.101.refs_9_), channel_id=1, source_target_pairs={{0,2},{1,5},{2,0},{3,7},{4,6},{5,1},{6,4},{7,3},{8,10},{9,13},{10,... | collective-permute-start | bytes 1769480 | tf_op jit(solution)/shard_map/ppermute | solution.py:843
  20.6 3.4 %copy-start.37 = (f32[192,768]{1,0:T(8,128)}, f32[192,768]{1,0:T(8,128)S(1)}, u32[]{:S(2)}) copy-start(f32[192,768]{1,0:T(8,128)S(1)} %get-tuple-element.102.refs_2_.refs_4_) | copy-start | bytes 1769476
  20.6 11.8 %copy-start.39 = (bf16[192,1536]{1,0:T(8,128)(2,1)}, bf16[192,1536]{1,0:T(8,128)(2,1)S(1)}, u32[]{:S(2)}) copy-start(bf16[192,1536]{1,0:T(8,128)(2,1)S(1)} %get-tuple-element.116.refs_13_.refs_2_) | copy-start | bytes 1769476
  20.6 3.4 %copy-start.34 = (bf16[1024,384]{1,0:T(8,128)(2,1)S(1)}, bf16[1024,384]{1,0:T(8,128)(2,1)}, u32[]{:S(2)}) copy-start(bf16[1024,384]{1,0:T(8,128)(2,1)} %get-tuple-element.105.refs_10_) | copy-start | bytes 2359300
  20.6 3.3 %collective-permute-start.3 = (f32[192,768]{1,0:T(8,128)S(1)}, f32[192,768]{1,0:T(8,128)S(1)}, u32[]{:S(2)}, u32[]{:S(2)}) collective-permute-start(f32[192,768]{1,0:T(8,128)S(1)} %get-tuple-element.103.refs_0_.refs_3_), channel_id=1, source_target_pairs={{0,1},{1,0},{2,3},{3,2},{4,5},{5,4},{6,7},{7,6},{8,9},{9,8},{10,11... | collective-permute-start | bytes 1769480 | tf_op jit(solution)/shard_map/ppermute | solution.py:833
  21.3 17.7 %collective-permute-start.9 = (f32[192,768]{1,0:T(8,128)S(1)}, f32[192,768]{1,0:T(8,128)S(1)}, u32[]{:S(2)}, u32[]{:S(2)}) collective-permute-start(f32[192,768]{1,0:T(8,128)S(1)} %get-tuple-element.124.refs_2_), channel_id=1, source_target_pairs={{0,8},{1,17},{2,10},{3,19},{4,12},{5,21},{6,14},{7,23},{8,0},{9,25... | collective-permute-start | bytes 1769480 | tf_op jit(solution)/shard_map/ppermute | solution.py:843
  23.6 15.4 %collective-permute-start.7 = (f32[208,768]{1,0:T(8,128)S(1)}, f32[208,768]{1,0:T(8,128)S(1)}, u32[]{:S(2)}, u32[]{:S(2)}) collective-permute-start(f32[208,768]{1,0:T(8,128)S(1)} %get-tuple-element.122), channel_id=1, source_target_pairs={{0,4},{1,3},{2,6},{3,1},{4,0},{5,7},{6,2},{7,5},{8,12},{9,11},{10,... | collective-permute-start | bytes 1916936 | tf_op jit(solution)/shard_map/ppermute | solution.py:843
  28.8 13.4 %copy-start.50 = (bf16[192,768]{1,0:T(8,128)(2,1)}, bf16[192,768]{1,0:T(8,128)(2,1)S(1)}, u32[]{:S(2)}) copy-start(bf16[192,768]{1,0:T(8,128)(2,1)S(1)} %get-tuple-element.127.refs_4_.refs_6_) | copy-start | bytes 884740
  28.8 13.4 %copy-start.54 = (bf16[192,384]{1,0:T(8,128)(2,1)}, bf16[192,384]{1,0:T(8,128)(2,1)S(1)}, u32[]{:S(2)}) copy-start(bf16[192,384]{1,0:T(8,128)(2,1)S(1)} %get-tuple-element.126.refs_3_.refs_5_) | copy-start | bytes 442372
  28.8 2.2 %collective-permute-start.4 = (f32[192,768]{1,0:T(8,128)S(1)}, f32[192,768]{1,0:T(8,128)S(1)}, u32[]{:S(2)}, u32[]{:S(2)}) collective-permute-start(f32[192,768]{1,0:T(8,128)S(1)} %get-tuple-element.109.refs_0_.refs_1_), channel_id=1, source_target_pairs={{0,1},{1,0},{2,3},{3,2},{4,5},{5,4},{6,7},{7,6},{8,9},{9,8},{10,11... | collective-permute-start | bytes 1769480 | tf_op jit(solution)/shard_map/ppermute | solution.py:833
  31.4 7.0 %copy-start.48 = (bf16[192,768]{1,0:T(8,128)(2,1)}, bf16[192,768]{1,0:T(8,128)(2,1)S(1)}, u32[]{:S(2)}) copy-start(bf16[192,768]{1,0:T(8,128)(2,1)S(1)} %get-tuple-element.111.refs_1_.refs_15_.refs_2_) | copy-start | bytes 884740
  31.5 7.5 %collective-permute-start.8 = (f32[96,768]{1,0:T(8,128)S(1)}, f32[96,768]{1,0:T(8,128)S(1)}, u32[]{:S(2)}, u32[]{:S(2)}) collective-permute-start(f32[96,768]{1,0:T(8,128)S(1)} %get-tuple-element.123.refs_0_), channel_id=1, source_target_pairs={{0,2},{1,5},{2,0},{3,7},{4,6},{5,1},{6,4},{7,3},{8,10},{9,13},{10,... | collective-permute-start | bytes 884744 | tf_op jit(solution)/shard_map/ppermute | solution.py:843
  38.5 3.7 %copy-start.5 = (bf16[2,512,768]{2,1,0:T(8,128)(2,1)S(1)}, bf16[2,512,768]{2,1,0:T(8,128)(2,1)}, u32[]{:S(2)}) copy-start(bf16[2,512,768]{2,1,0:T(8,128)(2,1)} %refs_0_.14) | copy-start | bytes 4718596
  38.5 13.3 %collective-permute-start.6 = (f32[1408,768]{1,0:T(8,128)S(1)}, f32[1408,768]{1,0:T(8,128)S(1)}, u32[]{:S(2)}, u32[]{:S(2)}) collective-permute-start(f32[1408,768]{1,0:T(8,128)S(1)} %get-tuple-element.117.refs_4_.refs_1_.refs_2_), channel_id=1, source_target_pairs={{0,1},{1,0},{2,3},{3,2},{4,5},{5,4},{6,7},{7,6},{8,9},{9,8},{10,11... | collective-permute-start | bytes 12976136 | tf_op jit(solution)/shard_map/ppermute | solution.py:833
  40.2 9.1 %collective-permute-start.10 = (f32[192,768]{1,0:T(8,128)S(1)}, f32[192,768]{1,0:T(8,128)S(1)}, u32[]{:S(2)}, u32[]{:S(2)}) collective-permute-start(f32[192,768]{1,0:T(8,128)S(1)} %get-tuple-element.125.refs_5_), channel_id=1, source_target_pairs={{0,4},{1,3},{2,6},{3,1},{4,0},{5,7},{6,2},{7,5},{8,12},{9,11},{10,... | collective-permute-start | bytes 1769480 | tf_op jit(solution)/shard_map/ppermute | solution.py:843
  40.9 31.6 %collective-permute-start.11 = (f32[384,768]{1,0:T(8,128)}, f32[384,768]{1,0:T(8,128)}, u32[]{:S(2)}, u32[]{:S(2)}) collective-permute-start(f32[384,768]{1,0:T(8,128)} %get-tuple-element.129), channel_id=1, source_target_pairs={{0,16},{1,9},{2,18},{3,11},{4,20},{5,13},{6,22},{7,15},{8,24},{9,1... | collective-permute-start | bytes 3538952 | tf_op jit(solution)/shard_map/ppermute | solution.py:843
  42.2 7.1 %copy-start.24 = (f32[104,768]{1,0:T(8,128)S(1)}, f32[104,768]{1,0:T(8,128)}, u32[]{:S(2)}) copy-start(f32[104,768]{1,0:T(8,128)} %copy-done.23) | copy-start | bytes 958468
  45.4 24.3 %collective-permute-start.13 = (f32[576,768]{1,0:T(8,128)}, f32[576,768]{1,0:T(8,128)}, u32[]{:S(2)}, u32[]{:S(2)}) collective-permute-start(f32[576,768]{1,0:T(8,128)} %cross_weights.1.refs_4_), channel_id=1, source_target_pairs={{0,2},{1,5},{2,0},{3,7},{4,6},{5,1},{6,4},{7,3},{8,10},{9,13},{10,... | collective-permute-start | bytes 5308424 | tf_op jit(solution)/shard_map/ppermute | solution.py:843
  49.4 5.8 %collective-permute-start.12 = (f32[600,768]{1,0:T(8,128)S(1)}, f32[600,768]{1,0:T(8,128)S(1)}, u32[]{:S(2)}, u32[]{:S(2)}) collective-permute-start(f32[600,768]{1,0:T(8,128)S(1)} %gather_self.1.refs_0_.refs_4_), channel_id=1, source_target_pairs={{0,1},{1,0},{2,3},{3,2},{4,5},{5,4},{6,7},{7,6},{8,9},{9,8},{10,11... | collective-permute-start | bytes 5529608 | tf_op jit(solution)/shard_map/ppermute | solution.py:833
  51.9 3.4 %copy-start.14 = (bf16[768,384]{1,0:T(8,128)(2,1)S(1)}, bf16[768,384]{1,0:T(8,128)(2,1)}, u32[]{:S(2)}) copy-start(bf16[768,384]{1,0:T(8,128)(2,1)} %refs_9_.1) | copy-start | bytes 1769476
  51.9 3.4 %copy-start.16 = (bf16[768,384]{1,0:T(8,128)(2,1)S(1)}, bf16[768,384]{1,0:T(8,128)(2,1)}, u32[]{:S(2)}) copy-start(bf16[768,384]{1,0:T(8,128)(2,1)} %refs_10_.1) | copy-start | bytes 1769476
  51.9 3.4 %copy-start.18 = (bf16[384,768]{1,0:T(8,128)(2,1)S(1)}, bf16[384,768]{1,0:T(8,128)(2,1)}, u32[]{:S(2)}) copy-start(bf16[384,768]{1,0:T(8,128)(2,1)} %refs_11_.3) | copy-start | bytes 1769476
  52.3 17.3 %collective-permute-start.14 = (f32[8,384]{1,0:T(8,128)S(1)}, f32[8,384]{1,0:T(8,128)S(1)}, u32[]{:S(2)}, u32[]{:S(2)}) collective-permute-start(f32[8,384]{1,0:T(8,128)S(1)} %get-tuple-element.132.refs_12_.refs_8_), channel_id=1, source_target_pairs={{0,2},{1,5},{2,0},{3,7},{4,6},{5,1},{6,4},{7,3},{8,10},{9,13},{10,... | collective-permute-start | bytes 36872 | tf_op jit(solution)/shard_map/ppermute | solution.py:843
  64.1 5.6 %copy-start.20 = (f32[192,768]{1,0:T(8,128)S(1)}, f32[192,768]{1,0:T(8,128)}, u32[]{:S(2)}) copy-start(f32[192,768]{1,0:T(8,128)} %copy-done.19) | copy-start | bytes 1769476
  64.1 5.6 %copy-start.51 = (bf16[192,768]{1,0:T(8,128)(2,1)S(1)}, bf16[192,768]{1,0:T(8,128)(2,1)}, u32[]{:S(2)}) copy-start(bf16[192,768]{1,0:T(8,128)(2,1)} %copy-done.50) | copy-start | bytes 884740
  64.1 5.6 %copy-start.53 = (bf16[192,384]{1,0:T(8,128)(2,1)S(1)}, bf16[192,384]{1,0:T(8,128)(2,1)}, u32[]{:S(2)}) copy-start(bf16[192,384]{1,0:T(8,128)(2,1)} %copy-done.52) | copy-start | bytes 442372
  64.1 5.6 %copy-start.55 = (bf16[192,384]{1,0:T(8,128)(2,1)S(1)}, bf16[192,384]{1,0:T(8,128)(2,1)}, u32[]{:S(2)}) copy-start(bf16[192,384]{1,0:T(8,128)(2,1)} %copy-done.54) | copy-start | bytes 442372
  65.7 19.1 %collective-permute-start.15 = (f32[96,1536]{1,0:T(8,128)S(1)}, f32[96,1536]{1,0:T(8,128)S(1)}, u32[]{:S(2)}, u32[]{:S(2)}) collective-permute-start(f32[96,1536]{1,0:T(8,128)S(1)} %get-tuple-element.133.refs_3_), channel_id=1, source_target_pairs={{0,8},{1,17},{2,10},{3,19},{4,12},{5,21},{6,14},{7,23},{8,0},{9,25... | collective-permute-start | bytes 1769480 | tf_op jit(solution)/shard_map/ppermute | solution.py:843
  72.1 15.9 %collective-permute-start.18 = (f32[200,1536]{1,0:T(8,128)S(1)}, f32[200,1536]{1,0:T(8,128)S(1)}, u32[]{:S(2)}, u32[]{:S(2)}) collective-permute-start(f32[200,1536]{1,0:T(8,128)S(1)} %get-tuple-element.135.refs_2_), channel_id=1, source_target_pairs={{0,4},{1,3},{2,6},{3,1},{4,0},{5,7},{6,2},{7,5},{8,12},{9,11},{10,... | collective-permute-start | bytes 3686408 | tf_op jit(solution)/shard_map/ppermute | solution.py:843
  73.9 4.4 %collective-permute-start.16 = (f32[576,768]{1,0:T(8,128)S(1)}, f32[576,768]{1,0:T(8,128)S(1)}, u32[]{:S(2)}, u32[]{:S(2)}) collective-permute-start(f32[576,768]{1,0:T(8,128)S(1)} %gather_ffn.1.refs_5_.refs_4_), channel_id=1, source_target_pairs={{0,1},{1,0},{2,3},{3,2},{4,5},{5,4},{6,7},{7,6},{8,9},{9,8},{10,11... | collective-permute-start | bytes 5308424 | tf_op jit(solution)/shard_map/ppermute | solution.py:833
  75.0 3.5 %copy-start.45 = (bf16[192,768]{1,0:T(8,128)(2,1)S(1)}, bf16[192,768]{1,0:T(8,128)(2,1)}, u32[]{:S(2)}) copy-start(bf16[192,768]{1,0:T(8,128)(2,1)} %get-tuple-element.140.refs_0_) | copy-start | bytes 884740
  84.9 8.3 %collective-permute-start.17 = (f32[48,1536]{1,0:T(8,128)S(1)}, f32[48,1536]{1,0:T(8,128)S(1)}, u32[]{:S(2)}, u32[]{:S(2)}) collective-permute-start(f32[48,1536]{1,0:T(8,128)S(1)} %self_fold.1.refs_3_), channel_id=1, source_target_pairs={{0,16},{1,9},{2,18},{3,11},{4,20},{5,13},{6,22},{7,15},{8,24},{9,1... | collective-permute-start | bytes 884744 | tf_op jit(solution)/shard_map/ppermute | solution.py:843
  88.2 20.7 %collective-permute-start.19 = (f32[104,1536]{1,0:T(8,128)S(1)}, f32[104,1536]{1,0:T(8,128)S(1)}, u32[]{:S(2)}, u32[]{:S(2)}) collective-permute-start(f32[104,1536]{1,0:T(8,128)S(1)} %get-tuple-element.146.refs_1_), channel_id=1, source_target_pairs={{0,8},{1,17},{2,10},{3,19},{4,12},{5,21},{6,14},{7,23},{8,0},{9,25... | collective-permute-start | bytes 1916936 | tf_op jit(solution)/shard_map/ppermute | solution.py:843
  90.0 15.3 %collective-permute-start.20 = (f32[96,3072]{1,0:T(8,128)S(1)}, f32[96,3072]{1,0:T(8,128)S(1)}, u32[]{:S(2)}, u32[]{:S(2)}) collective-permute-start(f32[96,3072]{1,0:T(8,128)S(1)} %relay.1.refs_3_), channel_id=1, source_target_pairs={{0,2},{1,5},{2,0},{3,7},{4,6},{5,1},{6,4},{7,3},{8,10},{9,13},{10,... | collective-permute-start | bytes 3538952 | tf_op jit(solution)/shard_map/ppermute | solution.py:843
  105.4 9.1 %collective-permute-start.22 = (f32[48,3072]{1,0:T(8,128)S(1)}, f32[48,3072]{1,0:T(8,128)S(1)}, u32[]{:S(2)}, u32[]{:S(2)}) collective-permute-start(f32[48,3072]{1,0:T(8,128)S(1)} %ffn_fold.1.refs_4_), channel_id=1, source_target_pairs={{0,4},{1,3},{2,6},{3,1},{4,0},{5,7},{6,2},{7,5},{8,12},{9,11},{10,... | collective-permute-start | bytes 1769480 | tf_op jit(solution)/shard_map/ppermute | solution.py:843
  109.0 9.5 %collective-permute-start.21 = (f32[56,1536]{1,0:T(8,128)S(1)}, f32[56,1536]{1,0:T(8,128)S(1)}, u32[]{:S(2)}, u32[]{:S(2)}) collective-permute-start(f32[56,1536]{1,0:T(8,128)S(1)} %get-tuple-element.155.refs_0_), channel_id=1, source_target_pairs={{0,16},{1,9},{2,18},{3,11},{4,20},{5,13},{6,22},{7,15},{8,24},{9,1... | collective-permute-start | bytes 1032200 | tf_op jit(solution)/shard_map/ppermute | solution.py:843
  (32 other events, 78.7 us)

commit v3 on v2

--- a/solution.py
+++ b/solution.py
@@ -508,12 +508,14 @@
     late_out[half:, inner:] = fold_lanes(nt(half_pick(1, width), low[...]))
 
 
-def cross_keep(enc, dk, dv, keep_out):
+def cross_keep(enc, dk, dv, own, dq, low, att, keep_out):
     steps, width = enc.shape[1:]
     inner = dk.shape[1]
     left = nt(half_pick(0, width), enc[...].reshape(2 * steps, width)).astype(bf16)
-    keep_out[:, :inner] = nn(left, dk[...])
-    keep_out[:, inner:] = nn(left, dv[...])
+    keep_out[:, :inner] = nn(own[...], dq[...])
+    keep_out[:, inner : 2 * inner] = nn(left, dk[...])
+    keep_out[:, 2 * inner : 3 * inner] = nn(left, dv[...])
+    keep_out[:, 3 * inner :] = nn(nt(half_pick(0, width), low[...]).astype(bf16), att[...])
 
 
 def side_by_side(out, at, small):
@@ -527,17 +529,16 @@
     return jnp.concatenate([rows[:, :n], rows[:, n : 2 * n]], 0)
 
 
-def cross_fold(keep, factors, moved, early, own, dq, low, att, small, small_moved, send_out, keep_out, small_out, total):
-    width = low.shape[1]
-    half, inner = own.shape[0], dq.shape[1]
-    rows = width // 16
-    total[:, :inner] = nn(own[...], dq[...]) + nn(
+def cross_fold(keep, factors, moved, early, small, small_moved, send_out, keep_out, small_out, total):
+    half, inner = keep.shape[0], factors.shape[1] // 2
+    rows = half // 8
+    total[:, :inner] = keep[:, :inner] + nn(
         unfold_lanes(early[:, :inner]).astype(bf16), factors[:, :inner].astype(bf16)
     )
-    total[:, 3 * inner :] = nn(nt(half_pick(0, width), low[...]).astype(bf16), att[...]) + nn(
+    total[:, 3 * inner :] = keep[:, 3 * inner :] + nn(
         unfold_lanes(factors[:, inner:]).astype(bf16), early[:, inner:].astype(bf16)
     )
-    total[:, inner : 3 * inner] = keep[...] + moved[...]
+    total[:, inner : 3 * inner] = keep[:, inner : 3 * inner] + moved[...]
     split_entries(1, lambda i: total[pl.ds(pl.multiple_of(i * rows, 8), rows), :], send_out, keep_out, rows)
     stack(small_out, small, small_moved)
     side_by_side(send_out, keep_out.shape[0], small_out)
@@ -1023,13 +1024,16 @@
             locals(), x, after_self, self_gain, cross_gain, rel_bias, enc_output, count
         )
     (keep_cross,) = call(
-        cross_keep, [((half, 2 * inner), f32, "v")], [(enc_output, "v"), (dk, "v"), (dv, "v")], after=(send_self,)
+        cross_keep,
+        [((half, wide), f32, "v")],
+        [(enc_output, "v"), (dk, "v"), (dv, "v"), (own_cross, "v"), (dq, "v"), (low_cross, "v"), (att_cross, "v")],
+        after=(send_self,)
     )
     send_cross, keep_cross, small_two = call(
         cross_fold,
         [((half // 2 + 8, wide), f32, "v"), ((half // 2, wide), f32, "v"), ((16, half), f32, "v")],
-        [(keep_cross, "v"), (late_cross_moved, "a", half, tokens), (late_cross_moved, "a", 0, half), (early_moved, "v"), (own_cross, "v"), (dq, "v"),
-         (low_cross, "v"), (att_cross, "v"), (small, "v"), (small_moved, "v")],
+        [(keep_cross, "v"), (late_cross_moved, "a", half, tokens), (late_cross_moved, "a", 0, half), (early_moved, "v"),
+         (small, "v"), (small_moved, "v")],
         scratch=[((half, wide), f32)],
         after=(keep_cross,),
     )

time: 120 us -> 121 us (level)
  Pallas kernels: 55.3 us -> 58.3 us
  waiting for transfers between devices: 36.7 us -> 34.6 us
    pallas_call x30, Pallas kernels: 55.3 us -> 58.3 us  [call(): pl.pallas_call(body, out_shape=[pltpu.HBM(shape, kind) if place == 'h' el...]
    ppermute x16, waiting for transfers between devices: 31.5 us -> 29.5 us  [stage_swap(): return lax.ppermute(values, ('dp', 'mp'), pairs)]
  transfers between devices with their start and end apart: 23 -> 23, of which waited for: 10 -> 10; matrix products, arithmetic and copies ran while one was open for 0% -> 0% of each run, Pallas kernels for 42% -> 44%
where the time goes in v3:
time: 121 us
  Pallas kernels  58.3 us (48%)
  waiting for transfers between devices  34.6 us (29%)
  starting transfers between devices  24.4 us (20%)
  local copies, waits for them, and re-layouts  1.64 us (1%)
  between operations  1.53 us (1%)
    pallas_call x30, Pallas kernels, call(): pl.pallas_call(body, out_shape=[pltpu.HBM(shape, kind) if place == 'h' el...  58.3 us
    ppermute x16, waiting for transfers between devices, stage_swap(): return lax.ppermute(values, ('dp', 'mp'), pairs)  29.5 us
    ppermute x16, starting transfers between devices, stage_swap(): return lax.ppermute(values, ('dp', 'mp'), pairs)  17.9 us
    ppermute x7, starting transfers between devices, pair_swap(): return lax.ppermute(values, 'mp', [(0, 1), (1, 0)])  6.46 us
    ppermute x7, waiting for transfers between devices, pair_swap(): return lax.ppermute(values, 'mp', [(0, 1), (1, 0)])  5.19 us
  transfers between devices with their start and end apart: 23, of which 10 were waited for; matrix products, arithmetic and copies ran while one was open for 0% of the time, Pallas kernels for 44%

profile of v3, /device:TPU:1, one launch (start us, length us, event | category | flops | bytes accessed | tf_op | source)
XLA Modules:
  0.0 120.5 jit_solution(14339560213675574855)
XLA Ops:
  0.7 4.5 %self_forward.1 = (bf16[192,768]{1,0:T(8,128)(2,1)}, bf16[192,768]{1,0:T(8,128)(2,1)}, bf16[192,1152]{1,0:T(8,128)(2,1)}, bf16[192,384]{1,0:T(8,128)(2,1)S(1)}, ...) custom-call(s32[1,2]{1,0:T(1,128)} %refs_0_.15, bf16[2,128,768]{2,1,0:T(8,128)(2,1)} %refs_1_.5, ...), custom_call_target="tpu_custom_call" | custom-call | flops 35000000512 | bytes 1000 | tf_op jit(solution)/shard_map/self_forward/pallas_call | solution.py:813
  5.2 2.1 %collective-permute-start.2 = (f32[104,768]{1,0:T(8,128)}, f32[104,768]{1,0:T(8,128)S(1)}, u32[]{:S(2)}, u32[]{:S(2)}) collective-permute-start(f32[104,768]{1,0:T(8,128)} %get-tuple-element.99.refs_7_), channel_id=1, source_target_pairs={{0,2},{1,5},{2,0},{3,7},{4,6},{5,1},{6,4},{7,3},{8,10},{9,13},{10,... | collective-permute-start | bytes 958472 | tf_op jit(solution)/shard_map/ppermute | solution.py:844
  7.4 1.0 collective-permute-start
  8.4 3.1 %encoder_forward.1 = (bf16[1024,384]{1,0:T(8,128)(2,1)S(1)}, bf16[384,1024]{1,0:T(8,128)(2,1)S(1)}, bf16[1024,384]{1,0:T(8,128)(2,1)}, bf16[1024,384]{1,0:T(8,128)(2,1)}, bf16[384,1024]{1,0:T(8,128)(2,1)}) custom-call(bf16[2,512,768]{2,1,0:T(8,128)(2,1)S(1)} %copy-done.4, bf16[768,384]{1,0:T(8,128)(2,1)S(1)} %copy-done.8, bf16[768,384]{1,0:T(8,128)(2,1)S(1)} %copy-done.10, ...), custom_call_target="tpu_custom_call" | custom-call | flops 35000000512 | bytes 1000 | tf_op jit(solution)/shard_map/encoder_forward/pallas_call | solution.py:813
  11.6 3.9 %cross_forward.1 = (f32[192,768]{1,0:T(8,128)S(1)}, bf16[192,384]{1,0:T(8,128)(2,1)}, bf16[192,384]{1,0:T(8,128)(2,1)S(1)}, f32[8,256]{1,0:T(8,128)S(1)}, f32[192,768]{1,0:T(8,128)S(1)}) custom-call(s32[1,2]{1,0:T(1,128)S(1)} %copy-done.32, s32[1,2]{1,0:T(1,128)S(1)} %copy-done.31, bf16[192,768]{1,0:T(8,128)(2,1)S(1)} %copy-done.46, ...), custom_call_target="tpu_custom_call" | custom-call | flops 35000000512 | bytes 1000 | tf_op jit(solution)/shard_map/cross_forward/pallas_call | solution.py:813
  15.7 0.7 pack_early.1
  16.3 1.3 %collective-permute-start.5 = (f32[192,768]{1,0:T(8,128)S(1)}, f32[192,768]{1,0:T(8,128)S(1)}, u32[]{:S(2)}, u32[]{:S(2)}) collective-permute-start(f32[192,768]{1,0:T(8,128)S(1)} %get-tuple-element.101.refs_9_), channel_id=1, source_target_pairs={{0,2},{1,5},{2,0},{3,7},{4,6},{5,1},{6,4},{7,3},{8,10},{9,13},{10,... | collective-permute-start | bytes 1769480 | tf_op jit(solution)/shard_map/ppermute | solution.py:844
  18.1 2.5 %ffn_both.1 = (f32[192,768]{1,0:T(8,128)S(1)}, bf16[192,768]{1,0:T(8,128)(2,1)}, f32[192,768]{1,0:T(8,128)S(1)}, bf16[192,1536]{1,0:T(8,128)(2,1)S(1)}, bf16[192...) custom-call(f32[192,768]{1,0:T(8,128)S(1)} %get-tuple-element.96.refs_0_, ...), custom_call_target="tpu_custom_call" | custom-call | flops 35000000512 | bytes 1000 | tf_op jit(solution)/shard_map/ffn_both/pallas_call | solution.py:813
  20.7 0.6 collective-permute-start.3
  21.3 2.3 %collective-permute-start.9 = (f32[192,768]{1,0:T(8,128)S(1)}, f32[192,768]{1,0:T(8,128)S(1)}, u32[]{:S(2)}, u32[]{:S(2)}) collective-permute-start(f32[192,768]{1,0:T(8,128)S(1)} %get-tuple-element.124.refs_2_), channel_id=1, source_target_pairs={{0,8},{1,17},{2,10},{3,19},{4,12},{5,21},{6,14},{7,23},{8,0},{9,25... | collective-permute-start | bytes 1769480 | tf_op jit(solution)/shard_map/ppermute | solution.py:844
  24.0 4.7 %cross_backward.1 = (f32[192,768]{1,0:T(8,128)}, bf16[192,768]{1,0:T(8,128)(2,1)S(1)}, bf16[192,384]{1,0:T(8,128)(2,1)S(1)}, bf16[1024,384]{1,0:T(8,128)(2,1)S(1...) custom-call(s32[1,2]{1,0:T(1,128)S(1)} %copy-done.32, s32[1,2]{1,0:T(1,128)S(1)} %copy-done.31, ...), custom_call_target="tpu_custom_call" | custom-call | flops 35000000512 | bytes 1000 | tf_op jit(solution)/shard_map/cross_backward/pallas_call | solution.py:813
  28.8 0.6 collective-permute-start.4
  29.3 1.6 %collective-permute-done.4.refs_2_ = f32[192,768]{1,0:T(8,128)S(1)} collective-permute-done((f32[192,768]{1,0:T(8,128)S(1)}, f32[192,768]{1,0:T(8,128)S(1)}, u32[]{:S(2)}, u32[]{:S(2)}) %collective-permute-start.4) | collective-permute-done | bytes 589856 | tf_op jit(solution)/shard_map/ppermute | solution.py:834
  31.0 0.4 self_grad.1
  31.5 1.0 collective-permute-start.8
  33.2 5.3 %back_all.1 = (bf16[192,1152]{1,0:T(8,128)(2,1)S(1)}, f32[8,32]{1,0:T(8,128)S(1)}, f32[1408,768]{1,0:T(8,128)S(1)}) custom-call(s32[1,2]{1,0:T(1,128)S(1)} %copy-done.32, bf16[192,768]{1,0:T(8,128)(2,1)S(1)} %get-tuple-element.111.refs_1_.refs_15_.refs_2_, f32[6,32]{1,0:T(8,128)S(1)} %bitcast.6, bf16[384,768]{1,0:T(8,128)(2,1)S(1)} %copy-done.17, ...), custom_call_target="tpu_custom_call" | custom-call | flops 35000000512 | bytes 1000 | tf_op jit(solution)/shard_map/back_all/pallas_call | solution.py:813
  38.5 0.4 collective-permute-start.6
  39.0 1.2 %collect.1 = (f32[192,768]{1,0:T(8,128)S(1)}, f32[384,768]{1,0:T(8,128)}) custom-call(f32[96,768]{1,0:T(8,128)S(1)} %get-tuple-element.123.refs_0_, f32[96,768]{1,0:T(8,128)S(1)} %collective-permute-done.8.refs_1_.refs_2_, f32[192,768]{1,0:T(8,128)S(1)} %get-tuple-element.124.refs_2_, f32[192,768]{1,0:T(8,128)S(1)} %collective-permute-done.9.refs_3_.refs_0_, ...), custom_call_target="tpu_custom_call" | custom-call | flops 35000000512 | bytes 1000 | tf_op jit(solution)/shard_map/collect/pallas_call | solution.py:813
  40.2 0.7 collective-permute-start.10
  40.9 1.3 %collective-permute-start.11 = (f32[384,768]{1,0:T(8,128)}, f32[384,768]{1,0:T(8,128)}, u32[]{:S(2)}, u32[]{:S(2)}) collective-permute-start(f32[384,768]{1,0:T(8,128)} %get-tuple-element.129), channel_id=1, source_target_pairs={{0,16},{1,9},{2,18},{3,11},{4,20},{5,13},{6,22},{7,15},{8,24},{9,1... | collective-permute-start | bytes 3538952 | tf_op jit(solution)/shard_map/ppermute | solution.py:844
  42.2 3.1 %cross_weights.1.refs_4_ = f32[576,768]{1,0:T(8,128)} custom-call(bf16[2,512,768]{2,1,0:T(8,128)(2,1)S(1)} %copy-done.5, bf16[1024,384]{1,0:T(8,128)(2,1)S(1)} %get-tuple-element.114.refs_9_.refs_1_, bf16[1024,384]{1,0:T(8,128)(2,1)S(1)} %get-tuple-element.115.refs_10_.refs_2_, bf16[192,384]{1,0:T(8,128)(2,1)S(1)} %get-tuple-element.126.refs_3_.refs_4_, ...), custom_call_target="tpu_custom_call" | custom-call | flops 35000000512 | bytes 1000 | tf_op jit(solution)/shard_map/cross_weights/pallas_call | solution.py:813
  45.3 1.2 %collective-permute-start.13 = (f32[576,768]{1,0:T(8,128)}, f32[576,768]{1,0:T(8,128)}, u32[]{:S(2)}, u32[]{:S(2)}) collective-permute-start(f32[576,768]{1,0:T(8,128)} %cross_weights.1.refs_4_), channel_id=1, source_target_pairs={{0,2},{1,5},{2,0},{3,7},{4,6},{5,1},{6,4},{7,3},{8,10},{9,13},{10,... | collective-permute-start | bytes 5308424 | tf_op jit(solution)/shard_map/ppermute | solution.py:844
  46.6 2.8 %collective-permute-done.10.refs_3_ = f32[192,768]{1,0:T(8,128)S(1)} collective-permute-done((f32[192,768]{1,0:T(8,128)S(1)}, f32[192,768]{1,0:T(8,128)S(1)}, u32[]{:S(2)}, u32[]{:S(2)}) %collective-permute-start.10) | collective-permute-done | bytes 589856 | tf_op jit(solution)/shard_map/ppermute | solution.py:844
  49.5 2.5 %collective-permute-start.12 = (f32[600,768]{1,0:T(8,128)S(1)}, f32[600,768]{1,0:T(8,128)S(1)}, u32[]{:S(2)}, u32[]{:S(2)}) collective-permute-start(f32[600,768]{1,0:T(8,128)S(1)} %gather_self.1.refs_0_.refs_4_), channel_id=1, source_target_pairs={{0,1},{1,0},{2,3},{3,2},{4,5},{5,4},{6,7},{7,6},{8,9},{9,8},{10,11... | collective-permute-start | bytes 5529608 | tf_op jit(solution)/shard_map/ppermute | solution.py:834
  52.0 0.4 finish_self_norm.1
  52.5 0.6 collective-permute-start.14
  53.1 2.3 %collective-permute-done.12.refs_5_ = f32[600,768]{1,0:T(8,128)S(1)} collective-permute-done((f32[600,768]{1,0:T(8,128)S(1)}, f32[600,768]{1,0:T(8,128)S(1)}, u32[]{:S(2)}, u32[]{:S(2)}) %collective-permute-start.12) | collective-permute-done | bytes 1843232 | tf_op jit(solution)/shard_map/ppermute | solution.py:834
  55.4 9.6 %self_group.1 = (f32[96,1536]{1,0:T(8,128)}, f32[96,1536]{1,0:T(8,128)S(1)}) custom-call(bf16[192,768]{1,0:T(8,128)(2,1)S(1)} %copy-done.47, bf16[192,1152]{1,0:T(8,128)(2,1)S(1)} %get-tuple-element.131.refs_1_, bf16[192,768]{1,0:T(8,128)(2,1)S(1)} %copy-done.49, bf16[192,384]{1,0:T(8,128)(2,1)S(1)} %get-tuple-element.132.refs_3_, ...), custom_call_target="tpu_custom_call" | custom-call | flops 35000000512 | bytes 1000 | tf_op jit(solution)/shard_map/self_group/pallas_call | solution.py:813
  65.0 3.8 %collective-permute-start.15 = (f32[96,1536]{1,0:T(8,128)}, f32[96,1536]{1,0:T(8,128)}, u32[]{:S(2)}, u32[]{:S(2)}) collective-permute-start(f32[96,1536]{1,0:T(8,128)} %get-tuple-element.134.refs_7_), channel_id=1, source_target_pairs={{0,8},{1,17},{2,10},{3,19},{4,12},{5,21},{6,14},{7,23},{8,0},{9,25... | collective-permute-start | bytes 1769480 | tf_op jit(solution)/shard_map/ppermute | solution.py:844
  68.8 2.2 %cross_keep.1.refs_0_.refs_6_ = f32[384,1536]{1,0:T(8,128)S(1)} custom-call(bf16[2,512,768]{2,1,0:T(8,128)(2,1)S(1)} %copy-done.5, bf16[1024,384]{1,0:T(8,128)(2,1)S(1)} %get-tuple-element.114.refs_9_.refs_1_, bf16[1024,384]{1,0:T(8,128)(2,1)S(1)} %get-tuple-element.115.refs_10_.refs_2_, bf16[384,192]{1,0:T(8,128)(2,1)S(1)} %get-tuple-element.130.refs_3_, ...), custom_call_target="tpu_custom_call" | custom-call | flops 35000000512 | bytes 1000 | tf_op jit(solution)/shard_map/cross_keep/pallas_call | solution.py:813
  71.1 1.9 %cross_fold.1 = (f32[200,1536]{1,0:T(8,128)S(1)}, f32[192,1536]{1,0:T(8,128)S(1)}, f32[16,384]{1,0:T(8,128)S(1)}) custom-call(f32[384,1536]{1,0:T(8,128)S(1)} %cross_keep.1.refs_0_.refs_6_, f32[576,768]{1,0:T(8,128)} %collective-permute-done.13.refs_1_.refs_2_, f32[576,768]{1,0:T(8,128)} %collective-permute-done.13.refs_1_.refs_2_, ...), custom_call_target="tpu_custom_call" | custom-call | flops 35000000512 | bytes 1000 | tf_op jit(solution)/shard_map/cross_fold/pallas_call | solution.py:813
  73.1 1.4 %gather_ffn.1.refs_5_.refs_4_ = f32[576,768]{1,0:T(8,128)S(1)} custom-call(f32[192,768]{1,0:T(8,128)S(1)} %copy-done.22, f32[384,768]{1,0:T(8,128)} %collective-permute-done.11.refs_1_, f32[200,1536]{1,0:T(8,128)S(1)} %get-tuple-element.135.refs_2_), custom_call_target="tpu_custom_call" | custom-call | flops 35000000512 | bytes 1000 | tf_op jit(solution)/shard_map/gather_ffn/pallas_call | solution.py:813
  74.5 1.2 %collective-permute-start.16 = (f32[576,768]{1,0:T(8,128)S(1)}, f32[576,768]{1,0:T(8,128)S(1)}, u32[]{:S(2)}, u32[]{:S(2)}) collective-permute-start(f32[576,768]{1,0:T(8,128)S(1)} %gather_ffn.1.refs_5_.refs_4_), channel_id=1, source_target_pairs={{0,1},{1,0},{2,3},{3,2},{4,5},{5,4},{6,7},{7,6},{8,9},{9,8},{10,11... | collective-permute-start | bytes 5308424 | tf_op jit(solution)/shard_map/ppermute | solution.py:834
  75.8 2.0 %finish_outputs.1 = (bf16[2,128,768]{2,1,0:T(8,128)(2,1)}, bf16[2,128,768]{2,1,0:T(8,128)(2,1)}, bf16[2,512,768]{2,1,0:T(8,128)(2,1)}, f32[8,128]{1,0:T(8,128)S(1)}) custom-call(s32[1,2]{1,0:T(1,128)S(1)} %copy-done.33, bf16[192,768]{1,0:T(8,128)(2,1)S(1)} %get-tuple-element.128.refs_1_, f32[1408,768]{1,0:T(8,128)S(1)} %get-tuple-element.117.refs_4_.refs_1_.refs_2_, ...), custom_call_target="tpu_custom_call" | custom-call | flops 35000000512 | bytes 1000 | tf_op jit(solution)/shard_map/finish_outputs/pallas_call | solution.py:813
  77.8 1.2 %collective-permute-done.16.refs_5_ = f32[576,768]{1,0:T(8,128)S(1)} collective-permute-done((f32[576,768]{1,0:T(8,128)S(1)}, f32[576,768]{1,0:T(8,128)S(1)}, u32[]{:S(2)}, u32[]{:S(2)}) %collective-permute-start.16) | collective-permute-done | bytes 1769504 | tf_op jit(solution)/shard_map/ppermute | solution.py:834
  79.2 6.3 %ffn_group.1 = (f32[96,3072]{1,0:T(8,128)S(1)}, f32[96,3072]{1,0:T(8,128)S(1)}) custom-call(bf16[192,768]{1,0:T(8,128)(2,1)S(1)} %copy-done.45, bf16[192,768]{1,0:T(8,128)(2,1)S(1)} %copy-done.44, bf16[192,1536]{1,0:T(8,128)(2,1)S(1)} %copy-done.40, bf16[192,1536]{1,0:T(8,128)(2,1)S(1)} %get-tuple-element.141.refs_3_, ...), custom_call_target="tpu_custom_call" | custom-call | flops 35000000512 | bytes 1000 | tf_op jit(solution)/shard_map/ffn_group/pallas_call | solution.py:813
  85.6 1.1 self_fold.1.refs_3_
  86.8 1.8 %collective-permute-done.18.refs_2_.refs_1_ = f32[200,1536]{1,0:T(8,128)S(1)} collective-permute-done((f32[200,1536]{1,0:T(8,128)S(1)}, f32[200,1536]{1,0:T(8,128)S(1)}, u32[]{:S(2)}, u32[]{:S(2)}) %collective-permute-start.18) | collective-permute-done | bytes 1228832 | tf_op jit(solution)/shard_map/ppermute | solution.py:844
  88.8 0.7 collective-permute-start.19
  89.7 6.4 %collective-permute-done.17.refs_2_ = f32[48,1536]{1,0:T(8,128)S(1)} collective-permute-done((f32[48,1536]{1,0:T(8,128)S(1)}, f32[48,1536]{1,0:T(8,128)S(1)}, u32[]{:S(2)}, u32[]{:S(2)}) %collective-permute-start.17) | collective-permute-done | bytes 294944 | tf_op jit(solution)/shard_map/ppermute | solution.py:844
  96.1 1.8 %finish_self.1 = (f32[48,384]{1,0:T(8,128)}, f32[48,384]{1,0:T(8,128)}, f32[48,384]{1,0:T(8,128)}, f32[48,384]{1,0:T(8,128)}, f32[8,128]{1,0:T(8,128)S(1)}) custom-call(f32[96,1536]{1,0:T(8,128)S(1)} %get-tuple-element.139.refs_0_, f32[96,1536]{1,0:T(8,128)} %collective-permute-done.15.refs_1_, f32[48,1536]{1,0:T(8,128)S(1)} %collective-permute-done.17.refs_2_, ...), custom_call_target="tpu_custom_call" | custom-call | flops 35000000512 | bytes 1000 | tf_op jit(solution)/shard_map/finish_self/pallas_call | solution.py:813
  97.9 6.9 %collective-permute-done.20.refs_1_ = f32[96,3072]{1,0:T(8,128)S(1)} collective-permute-done((f32[96,3072]{1,0:T(8,128)S(1)}, f32[96,3072]{1,0:T(8,128)S(1)}, u32[]{:S(2)}, u32[]{:S(2)}) %collective-permute-start.20) | collective-permute-done | bytes 1179680 | tf_op jit(solution)/shard_map/ppermute | solution.py:844
  104.9 2.0 %collective-permute-start.22 = (f32[48,3072]{1,0:T(8,128)S(1)}, f32[48,3072]{1,0:T(8,128)S(1)}, u32[]{:S(2)}, u32[]{:S(2)}) collective-permute-start(f32[48,3072]{1,0:T(8,128)S(1)} %ffn_fold.1.refs_4_), channel_id=1, source_target_pairs={{0,4},{1,3},{2,6},{3,1},{4,0},{5,7},{6,2},{7,5},{8,12},{9,11},{10,... | collective-permute-start | bytes 1769480 | tf_op jit(solution)/shard_map/ppermute | solution.py:844
  106.9 3.6 %collective-permute-done.19.refs_3_.refs_2_ = f32[104,1536]{1,0:T(8,128)S(1)} collective-permute-done((f32[104,1536]{1,0:T(8,128)S(1)}, f32[104,1536]{1,0:T(8,128)S(1)}, u32[]{:S(2)}, u32[]{:S(2)}) %collective-permute-start.19) | collective-permute-done | bytes 639008 | tf_op jit(solution)/shard_map/ppermute | solution.py:844
  110.7 3.8 %collective-permute-done.22.refs_2_ = f32[48,3072]{1,0:T(8,128)S(1)} collective-permute-done((f32[48,3072]{1,0:T(8,128)S(1)}, f32[48,3072]{1,0:T(8,128)S(1)}, u32[]{:S(2)}, u32[]{:S(2)}) %collective-permute-start.22) | collective-permute-done | bytes 589856 | tf_op jit(solution)/shard_map/ppermute | solution.py:844
  114.5 0.9 finish_ffn.1
  115.4 4.1 %collective-permute-done.21.refs_4_ = f32[56,1536]{1,0:T(8,128)S(1)} collective-permute-done((f32[56,1536]{1,0:T(8,128)S(1)}, f32[56,1536]{1,0:T(8,128)S(1)}, u32[]{:S(2)}, u32[]{:S(2)}) %collective-permute-start.21) | collective-permute-done | bytes 344096 | tf_op jit(solution)/shard_map/ppermute | solution.py:844
  119.5 0.8 finish_cross.1
  (134 shorter events, 3.0 us)
Async XLA Ops:
  0.7 7.7 %copy-start.4 = (bf16[2,512,768]{2,1,0:T(8,128)(2,1)S(1)}, bf16[2,512,768]{2,1,0:T(8,128)(2,1)}, u32[]{:S(2)}) copy-start(bf16[2,512,768]{2,1,0:T(8,128)(2,1)} %refs_0_.14) | copy-start | bytes 4718596
  0.7 7.7 %copy-start.8 = (bf16[768,384]{1,0:T(8,128)(2,1)S(1)}, bf16[768,384]{1,0:T(8,128)(2,1)}, u32[]{:S(2)}) copy-start(bf16[768,384]{1,0:T(8,128)(2,1)} %refs_11_.2) | copy-start | bytes 1769476
  0.7 7.7 %copy-start.10 = (bf16[768,384]{1,0:T(8,128)(2,1)S(1)}, bf16[768,384]{1,0:T(8,128)(2,1)}, u32[]{:S(2)}) copy-start(bf16[768,384]{1,0:T(8,128)(2,1)} %refs_12_.1) | copy-start | bytes 1769476
  5.2 12.4 %collective-permute-start.2 = (f32[104,768]{1,0:T(8,128)}, f32[104,768]{1,0:T(8,128)S(1)}, u32[]{:S(2)}, u32[]{:S(2)}) collective-permute-start(f32[104,768]{1,0:T(8,128)} %get-tuple-element.99.refs_7_), channel_id=1, source_target_pairs={{0,2},{1,5},{2,0},{3,7},{4,6},{5,1},{6,4},{7,3},{8,10},{9,13},{10,... | collective-permute-start | bytes 958472 | tf_op jit(solution)/shard_map/ppermute | solution.py:844
  7.4 4.2 %copy-start.6 = (bf16[768,384]{1,0:T(8,128)(2,1)S(1)}, bf16[768,384]{1,0:T(8,128)(2,1)}, u32[]{:S(2)}) copy-start(bf16[768,384]{1,0:T(8,128)(2,1)} %refs_8_.4) | copy-start | bytes 1769476
  7.4 4.2 %copy-start.7 = (bf16[384,768]{1,0:T(8,128)(2,1)S(1)}, bf16[384,768]{1,0:T(8,128)(2,1)}, u32[]{:S(2)}) copy-start(bf16[384,768]{1,0:T(8,128)(2,1)} %refs_7_.4) | copy-start | bytes 1769476
  7.4 4.2 %copy-start.27 = (f32[768]{0:T(1024)S(1)}, f32[768]{0:T(1024)}, u32[]{:S(2)}) copy-start(f32[768]{0:T(1024)} %refs_3_.7) | copy-start | bytes 9220
  7.4 4.2 %copy-start.31 = (s32[1,2]{1,0:T(1,128)S(1)}, s32[1,2]{1,0:T(1,128)}, u32[]{:S(2)}) copy-start(s32[1,2]{1,0:T(1,128)} %refs_1_.9) | copy-start | bytes 28
  7.4 4.2 %copy-start.32 = (s32[1,2]{1,0:T(1,128)S(1)}, s32[1,2]{1,0:T(1,128)}, u32[]{:S(2)}) copy-start(s32[1,2]{1,0:T(1,128)} %refs_0_.15) | copy-start | bytes 28
  7.4 4.2 %copy-start.46 = (bf16[192,768]{1,0:T(8,128)(2,1)S(1)}, bf16[192,768]{1,0:T(8,128)(2,1)}, u32[]{:S(2)}) copy-start(bf16[192,768]{1,0:T(8,128)(2,1)} %get-tuple-element.92.refs_2_.refs_0_) | copy-start | bytes 884740
  7.4 4.2 %collective-permute-start = (f32[192,768]{1,0:T(8,128)S(1)}, f32[192,768]{1,0:T(8,128)S(1)}, u32[]{:S(2)}, u32[]{:S(2)}) collective-permute-start(f32[192,768]{1,0:T(8,128)S(1)} %get-tuple-element.93.refs_3_), channel_id=1, source_target_pairs={{0,1},{1,0},{2,3},{3,2},{4,5},{5,4},{6,7},{7,6},{8,9},{9,8},{10,11... | collective-permute-start | bytes 1769480 | tf_op jit(solution)/shard_map/ppermute | solution.py:834
  15.5 2.1 %collective-permute-start.1 = (f32[192,768]{1,0:T(8,128)S(1)}, f32[192,768]{1,0:T(8,128)S(1)}, u32[]{:S(2)}, u32[]{:S(2)}) collective-permute-start(f32[192,768]{1,0:T(8,128)S(1)} %get-tuple-element.97.refs_3_.refs_1_), channel_id=1, source_target_pairs={{0,1},{1,0},{2,3},{3,2},{4,5},{5,4},{6,7},{7,6},{8,9},{9,8},{10,11... | collective-permute-start | bytes 1769480 | tf_op jit(solution)/shard_map/ppermute | solution.py:834
  16.3 13.0 %collective-permute-start.5 = (f32[192,768]{1,0:T(8,128)S(1)}, f32[192,768]{1,0:T(8,128)S(1)}, u32[]{:S(2)}, u32[]{:S(2)}) collective-permute-start(f32[192,768]{1,0:T(8,128)S(1)} %get-tuple-element.101.refs_9_), channel_id=1, source_target_pairs={{0,2},{1,5},{2,0},{3,7},{4,6},{5,1},{6,4},{7,3},{8,10},{9,13},{10,... | collective-permute-start | bytes 1769480 | tf_op jit(solution)/shard_map/ppermute | solution.py:844
  20.6 3.4 %copy-start.37 = (f32[192,768]{1,0:T(8,128)}, f32[192,768]{1,0:T(8,128)S(1)}, u32[]{:S(2)}) copy-start(f32[192,768]{1,0:T(8,128)S(1)} %get-tuple-element.102.refs_2_.refs_4_) | copy-start | bytes 1769476
  20.6 11.8 %copy-start.39 = (bf16[192,1536]{1,0:T(8,128)(2,1)}, bf16[192,1536]{1,0:T(8,128)(2,1)S(1)}, u32[]{:S(2)}) copy-start(bf16[192,1536]{1,0:T(8,128)(2,1)S(1)} %get-tuple-element.116.refs_13_.refs_2_) | copy-start | bytes 1769476
  20.6 3.4 %copy-start.34 = (bf16[1024,384]{1,0:T(8,128)(2,1)S(1)}, bf16[1024,384]{1,0:T(8,128)(2,1)}, u32[]{:S(2)}) copy-start(bf16[1024,384]{1,0:T(8,128)(2,1)} %get-tuple-element.105.refs_10_) | copy-start | bytes 2359300
  20.6 3.4 %copy-start.35 = (bf16[1024,384]{1,0:T(8,128)(2,1)S(1)}, bf16[1024,384]{1,0:T(8,128)(2,1)}, u32[]{:S(2)}) copy-start(bf16[1024,384]{1,0:T(8,128)(2,1)} %get-tuple-element.106.refs_11_) | copy-start | bytes 2359300
  20.6 3.4 %copy-start.36 = (bf16[384,1024]{1,0:T(8,128)(2,1)S(1)}, bf16[384,1024]{1,0:T(8,128)(2,1)}, u32[]{:S(2)}) copy-start(bf16[384,1024]{1,0:T(8,128)(2,1)} %get-tuple-element.107.refs_12_) | copy-start | bytes 2359300
  20.6 3.4 %copy-start.52 = (bf16[192,384]{1,0:T(8,128)(2,1)S(1)}, bf16[192,384]{1,0:T(8,128)(2,1)}, u32[]{:S(2)}) copy-start(bf16[192,384]{1,0:T(8,128)(2,1)} %get-tuple-element.104.refs_9_) | copy-start | bytes 442372
  20.7 3.3 %collective-permute-start.3 = (f32[192,768]{1,0:T(8,128)S(1)}, f32[192,768]{1,0:T(8,128)S(1)}, u32[]{:S(2)}, u32[]{:S(2)}) collective-permute-start(f32[192,768]{1,0:T(8,128)S(1)} %get-tuple-element.103.refs_0_.refs_3_), channel_id=1, source_target_pairs={{0,1},{1,0},{2,3},{3,2},{4,5},{5,4},{6,7},{7,6},{8,9},{9,8},{10,11... | collective-permute-start | bytes 1769480 | tf_op jit(solution)/shard_map/ppermute | solution.py:834
  21.3 17.6 %collective-permute-start.9 = (f32[192,768]{1,0:T(8,128)S(1)}, f32[192,768]{1,0:T(8,128)S(1)}, u32[]{:S(2)}, u32[]{:S(2)}) collective-permute-start(f32[192,768]{1,0:T(8,128)S(1)} %get-tuple-element.124.refs_2_), channel_id=1, source_target_pairs={{0,8},{1,17},{2,10},{3,19},{4,12},{5,21},{6,14},{7,23},{8,0},{9,25... | collective-permute-start | bytes 1769480 | tf_op jit(solution)/shard_map/ppermute | solution.py:844
  23.6 15.3 %collective-permute-start.7 = (f32[208,768]{1,0:T(8,128)S(1)}, f32[208,768]{1,0:T(8,128)S(1)}, u32[]{:S(2)}, u32[]{:S(2)}) collective-permute-start(f32[208,768]{1,0:T(8,128)S(1)} %get-tuple-element.122), channel_id=1, source_target_pairs={{0,4},{1,3},{2,6},{3,1},{4,0},{5,7},{6,2},{7,5},{8,12},{9,11},{10,... | collective-permute-start | bytes 1916936 | tf_op jit(solution)/shard_map/ppermute | solution.py:844
  28.8 2.2 %collective-permute-start.4 = (f32[192,768]{1,0:T(8,128)S(1)}, f32[192,768]{1,0:T(8,128)S(1)}, u32[]{:S(2)}, u32[]{:S(2)}) collective-permute-start(f32[192,768]{1,0:T(8,128)S(1)} %get-tuple-element.109.refs_0_.refs_1_), channel_id=1, source_target_pairs={{0,1},{1,0},{2,3},{3,2},{4,5},{5,4},{6,7},{7,6},{8,9},{9,8},{10,11... | collective-permute-start | bytes 1769480 | tf_op jit(solution)/shard_map/ppermute | solution.py:834
  31.4 7.1 %copy-start.48 = (bf16[192,768]{1,0:T(8,128)(2,1)}, bf16[192,768]{1,0:T(8,128)(2,1)S(1)}, u32[]{:S(2)}) copy-start(bf16[192,768]{1,0:T(8,128)(2,1)S(1)} %get-tuple-element.111.refs_1_.refs_15_.refs_2_) | copy-start | bytes 884740
  31.5 7.5 %collective-permute-start.8 = (f32[96,768]{1,0:T(8,128)S(1)}, f32[96,768]{1,0:T(8,128)S(1)}, u32[]{:S(2)}, u32[]{:S(2)}) collective-permute-start(f32[96,768]{1,0:T(8,128)S(1)} %get-tuple-element.123.refs_0_), channel_id=1, source_target_pairs={{0,2},{1,5},{2,0},{3,7},{4,6},{5,1},{6,4},{7,3},{8,10},{9,13},{10,... | collective-permute-start | bytes 884744 | tf_op jit(solution)/shard_map/ppermute | solution.py:844
  38.5 3.7 %copy-start.5 = (bf16[2,512,768]{2,1,0:T(8,128)(2,1)S(1)}, bf16[2,512,768]{2,1,0:T(8,128)(2,1)}, u32[]{:S(2)}) copy-start(bf16[2,512,768]{2,1,0:T(8,128)(2,1)} %refs_0_.14) | copy-start | bytes 4718596
  38.5 13.4 %collective-permute-start.6 = (f32[1408,768]{1,0:T(8,128)S(1)}, f32[1408,768]{1,0:T(8,128)S(1)}, u32[]{:S(2)}, u32[]{:S(2)}) collective-permute-start(f32[1408,768]{1,0:T(8,128)S(1)} %get-tuple-element.117.refs_4_.refs_1_.refs_2_), channel_id=1, source_target_pairs={{0,1},{1,0},{2,3},{3,2},{4,5},{5,4},{6,7},{7,6},{8,9},{9,8},{10,11... | collective-permute-start | bytes 12976136 | tf_op jit(solution)/shard_map/ppermute | solution.py:834
  40.2 9.1 %collective-permute-start.10 = (f32[192,768]{1,0:T(8,128)S(1)}, f32[192,768]{1,0:T(8,128)S(1)}, u32[]{:S(2)}, u32[]{:S(2)}) collective-permute-start(f32[192,768]{1,0:T(8,128)S(1)} %get-tuple-element.125.refs_5_), channel_id=1, source_target_pairs={{0,4},{1,3},{2,6},{3,1},{4,0},{5,7},{6,2},{7,5},{8,12},{9,11},{10,... | collective-permute-start | bytes 1769480 | tf_op jit(solution)/shard_map/ppermute | solution.py:844
  40.9 32.1 %collective-permute-start.11 = (f32[384,768]{1,0:T(8,128)}, f32[384,768]{1,0:T(8,128)}, u32[]{:S(2)}, u32[]{:S(2)}) collective-permute-start(f32[384,768]{1,0:T(8,128)} %get-tuple-element.129), channel_id=1, source_target_pairs={{0,16},{1,9},{2,18},{3,11},{4,20},{5,13},{6,22},{7,15},{8,24},{9,1... | collective-permute-start | bytes 3538952 | tf_op jit(solution)/shard_map/ppermute | solution.py:844
  42.2 7.1 %copy-start.24 = (f32[104,768]{1,0:T(8,128)S(1)}, f32[104,768]{1,0:T(8,128)}, u32[]{:S(2)}) copy-start(f32[104,768]{1,0:T(8,128)} %copy-done.23) | copy-start | bytes 958468
  45.3 25.7 %collective-permute-start.13 = (f32[576,768]{1,0:T(8,128)}, f32[576,768]{1,0:T(8,128)}, u32[]{:S(2)}, u32[]{:S(2)}) collective-permute-start(f32[576,768]{1,0:T(8,128)} %cross_weights.1.refs_4_), channel_id=1, source_target_pairs={{0,2},{1,5},{2,0},{3,7},{4,6},{5,1},{6,4},{7,3},{8,10},{9,13},{10,... | collective-permute-start | bytes 5308424 | tf_op jit(solution)/shard_map/ppermute | solution.py:844
  49.5 5.9 %collective-permute-start.12 = (f32[600,768]{1,0:T(8,128)S(1)}, f32[600,768]{1,0:T(8,128)S(1)}, u32[]{:S(2)}, u32[]{:S(2)}) collective-permute-start(f32[600,768]{1,0:T(8,128)S(1)} %gather_self.1.refs_0_.refs_4_), channel_id=1, source_target_pairs={{0,1},{1,0},{2,3},{3,2},{4,5},{5,4},{6,7},{7,6},{8,9},{9,8},{10,11... | collective-permute-start | bytes 5529608 | tf_op jit(solution)/shard_map/ppermute | solution.py:834
  52.0 3.4 %copy-start.14 = (bf16[768,384]{1,0:T(8,128)(2,1)S(1)}, bf16[768,384]{1,0:T(8,128)(2,1)}, u32[]{:S(2)}) copy-start(bf16[768,384]{1,0:T(8,128)(2,1)} %refs_9_.1) | copy-start | bytes 1769476
  52.0 3.4 %copy-start.16 = (bf16[768,384]{1,0:T(8,128)(2,1)S(1)}, bf16[768,384]{1,0:T(8,128)(2,1)}, u32[]{:S(2)}) copy-start(bf16[768,384]{1,0:T(8,128)(2,1)} %refs_10_.1) | copy-start | bytes 1769476
  52.0 3.4 %copy-start.18 = (bf16[384,768]{1,0:T(8,128)(2,1)S(1)}, bf16[384,768]{1,0:T(8,128)(2,1)}, u32[]{:S(2)}) copy-start(bf16[384,768]{1,0:T(8,128)(2,1)} %refs_11_.3) | copy-start | bytes 1769476
  52.0 3.4 %copy-start.30 = (f32[32,6]{0,1:T(8,128)S(1)}, f32[32,6]{0,1:T(8,128)}, u32[]{:S(2)}) copy-start(f32[32,6]{0,1:T(8,128)} %param.28) | copy-start | bytes 2308
  52.5 18.6 %collective-permute-start.14 = (f32[8,384]{1,0:T(8,128)S(1)}, f32[8,384]{1,0:T(8,128)S(1)}, u32[]{:S(2)}, u32[]{:S(2)}) collective-permute-start(f32[8,384]{1,0:T(8,128)S(1)} %get-tuple-element.133.refs_12_.refs_4_), channel_id=1, source_target_pairs={{0,2},{1,5},{2,0},{3,7},{4,6},{5,1},{6,4},{7,3},{8,10},{9,13},{10,... | collective-permute-start | bytes 36872 | tf_op jit(solution)/shard_map/ppermute | solution.py:844
  55.4 13.4 %copy-start.51 = (bf16[192,384]{1,0:T(8,128)(2,1)S(1)}, bf16[192,384]{1,0:T(8,128)(2,1)}, u32[]{:S(2)}) copy-start(bf16[192,384]{1,0:T(8,128)(2,1)} %copy-done.50) | copy-start | bytes 442372
  65.0 20.6 %collective-permute-start.15 = (f32[96,1536]{1,0:T(8,128)}, f32[96,1536]{1,0:T(8,128)}, u32[]{:S(2)}, u32[]{:S(2)}) collective-permute-start(f32[96,1536]{1,0:T(8,128)} %get-tuple-element.134.refs_7_), channel_id=1, source_target_pairs={{0,8},{1,17},{2,10},{3,19},{4,12},{5,21},{6,14},{7,23},{8,0},{9,25... | collective-permute-start | bytes 1769480 | tf_op jit(solution)/shard_map/ppermute | solution.py:844
  73.0 15.6 %collective-permute-start.18 = (f32[200,1536]{1,0:T(8,128)S(1)}, f32[200,1536]{1,0:T(8,128)S(1)}, u32[]{:S(2)}, u32[]{:S(2)}) collective-permute-start(f32[200,1536]{1,0:T(8,128)S(1)} %get-tuple-element.135.refs_2_), channel_id=1, source_target_pairs={{0,4},{1,3},{2,6},{3,1},{4,0},{5,7},{6,2},{7,5},{8,12},{9,11},{10,... | collective-permute-start | bytes 3686408 | tf_op jit(solution)/shard_map/ppermute | solution.py:844
  74.5 4.6 %collective-permute-start.16 = (f32[576,768]{1,0:T(8,128)S(1)}, f32[576,768]{1,0:T(8,128)S(1)}, u32[]{:S(2)}, u32[]{:S(2)}) collective-permute-start(f32[576,768]{1,0:T(8,128)S(1)} %gather_ffn.1.refs_5_.refs_4_), channel_id=1, source_target_pairs={{0,1},{1,0},{2,3},{3,2},{4,5},{5,4},{6,7},{7,6},{8,9},{9,8},{10,11... | collective-permute-start | bytes 5308424 | tf_op jit(solution)/shard_map/ppermute | solution.py:834
  75.8 3.4 %copy-start.44 = (bf16[192,768]{1,0:T(8,128)(2,1)S(1)}, bf16[192,768]{1,0:T(8,128)(2,1)}, u32[]{:S(2)}) copy-start(bf16[192,768]{1,0:T(8,128)(2,1)} %get-tuple-element.98.refs_4_.refs_6_.refs_1_) | copy-start | bytes 884740
  75.8 3.5 %copy-start.45 = (bf16[192,768]{1,0:T(8,128)(2,1)S(1)}, bf16[192,768]{1,0:T(8,128)(2,1)}, u32[]{:S(2)}) copy-start(bf16[192,768]{1,0:T(8,128)(2,1)} %get-tuple-element.140.refs_0_) | copy-start | bytes 884740
  86.7 9.4 %collective-permute-start.17 = (f32[48,1536]{1,0:T(8,128)S(1)}, f32[48,1536]{1,0:T(8,128)S(1)}, u32[]{:S(2)}, u32[]{:S(2)}) collective-permute-start(f32[48,1536]{1,0:T(8,128)S(1)} %self_fold.1.refs_3_), channel_id=1, source_target_pairs={{0,16},{1,9},{2,18},{3,11},{4,20},{5,13},{6,22},{7,15},{8,24},{9,1... | collective-permute-start | bytes 884744 | tf_op jit(solution)/shard_map/ppermute | solution.py:844
  88.8 21.7 %collective-permute-start.19 = (f32[104,1536]{1,0:T(8,128)S(1)}, f32[104,1536]{1,0:T(8,128)S(1)}, u32[]{:S(2)}, u32[]{:S(2)}) collective-permute-start(f32[104,1536]{1,0:T(8,128)S(1)} %get-tuple-element.146.refs_1_), channel_id=1, source_target_pairs={{0,8},{1,17},{2,10},{3,19},{4,12},{5,21},{6,14},{7,23},{8,0},{9,25... | collective-permute-start | bytes 1916936 | tf_op jit(solution)/shard_map/ppermute | solution.py:844
  89.4 15.3 %collective-permute-start.20 = (f32[96,3072]{1,0:T(8,128)S(1)}, f32[96,3072]{1,0:T(8,128)S(1)}, u32[]{:S(2)}, u32[]{:S(2)}) collective-permute-start(f32[96,3072]{1,0:T(8,128)S(1)} %relay.1.refs_3_), channel_id=1, source_target_pairs={{0,2},{1,5},{2,0},{3,7},{4,6},{5,1},{6,4},{7,3},{8,10},{9,13},{10,... | collective-permute-start | bytes 3538952 | tf_op jit(solution)/shard_map/ppermute | solution.py:844
  104.9 9.6 %collective-permute-start.22 = (f32[48,3072]{1,0:T(8,128)S(1)}, f32[48,3072]{1,0:T(8,128)S(1)}, u32[]{:S(2)}, u32[]{:S(2)}) collective-permute-start(f32[48,3072]{1,0:T(8,128)S(1)} %ffn_fold.1.refs_4_), channel_id=1, source_target_pairs={{0,4},{1,3},{2,6},{3,1},{4,0},{5,7},{6,2},{7,5},{8,12},{9,11},{10,... | collective-permute-start | bytes 1769480 | tf_op jit(solution)/shard_map/ppermute | solution.py:844
  110.6 8.9 %collective-permute-start.21 = (f32[56,1536]{1,0:T(8,128)S(1)}, f32[56,1536]{1,0:T(8,128)S(1)}, u32[]{:S(2)}, u32[]{:S(2)}) collective-permute-start(f32[56,1536]{1,0:T(8,128)S(1)} %get-tuple-element.155.refs_0_), channel_id=1, source_target_pairs={{0,16},{1,9},{2,18},{3,11},{4,20},{5,13},{6,22},{7,15},{8,24},{9,1... | collective-permute-start | bytes 1032200 | tf_op jit(solution)/shard_map/ppermute | solution.py:844
  (28 other events, 63.4 us)
